TPU v7x, 32 devices: a whole 2x2x4 slice. The times are simulated.
32 devices in a mesh: head: 8 (over y, x, core), dp: 4 (over z).
Axes of the slice: x: 2, y: 2, z: 4, core: 2. Of those that a mesh axis runs over, the one named last changes fastest.
Arguments:
- layer_input: bfloat16 [8, 1024, 2048], P('dp', 'head'), may hold values from -6 to 6
- doc_starts: int32 [8, 1024], P('dp'), may hold values from 0 to 1, as said below
- norm1_gain: float32 [2048], replicated, may hold values from 0.5 to 1.5
- w_query: bfloat16 [2048, 2048], P(None, 'head'), may hold values from -0.125 to 0.125
- w_forget: bfloat16 [2048, 2048], P(None, 'head'), may hold values from -0.125 to 0.125
- w_input: bfloat16 [2048, 2048], P(None, 'head'), may hold values from -0.125 to 0.125
- w_gate_out: bfloat16 [2048, 2048], P(None, 'head'), may hold values from -0.125 to 0.125
- forget_floor: float32 [2048], P('head'), may hold values from 0.92 to 1
- group_gain: float32 [2048], P('head'), may hold values from 0.5 to 1.5
- w_out: bfloat16 [2048, 2048], P('head'), may hold values from -0.125 to 0.125
- norm2_gain: float32 [2048], replicated, may hold values from 0.5 to 1.5
- ffn_gate: bfloat16 [2048, 5632], P(None, ('head', 'dp')), may hold values from -0.125 to 0.125
- ffn_up: bfloat16 [2048, 5632], P(None, ('head', 'dp')), may hold values from -0.125 to 0.125
- ffn_down: bfloat16 [2048, 5632], P(None, ('head', 'dp')), may hold values from -0.078125 to 0.078125
- out_cotangent: bfloat16 [8, 1024, 2048], P('dp', 'head'), may hold values from -6 to 6
Outputs:
- output: bfloat16 [8, 1024, 2048], P('dp', 'head')
- input_grad: float32 [8, 1024, 2048], P('dp', 'head')
- query_grad: float32 [2048, 2048], P('dp', 'head')
- forget_grad: float32 [2048, 2048], P('dp', 'head')
- input_proj_grad: float32 [2048, 2048], P('dp', 'head')
- gate_out_grad: float32 [2048, 2048], P('dp', 'head')
- out_proj_grad: float32 [2048, 2048], P('head', 'dp')
- group_gain_grad: float32 [2048], P(('head', 'dp'))
- floor_grad: float32 [2048], P(('head', 'dp'))
- norm1_gain_grad: float32 [2048], replicated
- norm2_gain_grad: float32 [2048], replicated
- ffn_gate_grad: float32 [2048, 5632], P(None, ('head', 'dp'))
- ffn_up_grad: float32 [2048, 5632], P(None, ('head', 'dp'))
- ffn_down_grad: float32 [2048, 5632], P(None, ('head', 'dp'))
Inputs may be any that keep to these rules, and one draw needn't show every extreme that they name: `doc_starts`: position 0 of every row is 1; every row has at most 4 other starts; in each aligned group of 2 rows one row, drawn from the seed, has exactly one other start, at a position below 64.
All inputs are finite; a program needn't handle non-finite values.
Results may differ from a plain program's by a relative error of at most 0.015.
The roundings to bfloat16 on the way count: a program that leaves them out, or rounds other values in their place, can miss the bound.
Values may be sent and summed in bfloat16 or wider, within the bound.
No kernel may reach another device: no remote copies, remote signals or barrier semaphores. Data moves between devices by JAX's collectives and lax.ppermute only.
A program may use at most 192 MiB of HBM per device.

v0:
```python
import jax
import jax.numpy as jnp
from jax import lax
from jax.sharding import PartitionSpec as P

HEAD_DIM = 128


highest = lax.Precision.HIGHEST
epsilon = 1e-06


def rms_scale(tensor):
    return lax.rsqrt(jnp.mean(tensor * tensor, axis=-1, keepdims=True) + epsilon)


def cross_rows(left, right):
    return lax.dot_general(
        left, right, (((0,), (0,)), ((), ())), preferred_element_type=jnp.float32
    )


def cross_cols(left, right):
    return lax.dot_general(
        left, right, (((1,), (1,)), ((), ())), preferred_element_type=jnp.float32
    )


def span_mix(carry_state, span_items):
    queries, forget_log, inject, values, starts = span_items
    span_len = queries.shape[1]
    lower_tri = (jnp.arange(span_len)[:, None] >= jnp.arange(span_len)[None, :]).astype(jnp.float32)
    decays = jnp.einsum("ts,rshc->rthc", lower_tri, forget_log, precision=highest)
    counts = jnp.einsum("ts,rs->rt", lower_tri, starts, precision=highest)
    final_decay = decays[:, -1]
    same_doc = (counts[:, :, None] == counts[:, None, :]) & (lower_tri[None] > 0)
    lifted = queries * jnp.exp(decays)
    scores = jnp.einsum("rthc,rshc->rhts", lifted, inject * jnp.exp(-decays), precision=highest)
    scores = jnp.where(same_doc[:, None], scores, 0.0)
    inside = jnp.einsum("rhts,rshd->rthd", scores, values, precision=highest)
    carried = (counts == 0).astype(jnp.float32)[:, :, None, None]
    earlier = jnp.einsum("rthc,rhcd->rthd", lifted * carried, carry_state, precision=highest)
    to_final = (counts == counts[:, -1:]).astype(jnp.float32)[:, :, None, None]
    added_state = jnp.einsum(
        "rshc,rshd->rhcd",
        inject * jnp.exp(final_decay[:, None] - decays) * to_final,
        values,
        precision=highest,
    )
    through = (counts[:, -1] == 0).astype(jnp.float32)[:, None, None, None]
    carry_state = carry_state * jnp.exp(final_decay)[:, :, :, None] * through + added_state
    return (carry_state, inside + earlier)


def mixer_core(queries, forget_pre, values, gate_pre, floor_bound, gain_vec, starts):
    row_count, seq_len, head_width = queries.shape
    head_count = head_width // HEAD_DIM
    span_len = 128
    span_count = seq_len // span_len
    inject = (1.0 - floor_bound) * jax.nn.sigmoid(-forget_pre)
    forget_log = jnp.log(1.0 - inject)

    def spans(tensor):
        return jnp.moveaxis(
            tensor.reshape(row_count, span_count, span_len, head_count, HEAD_DIM), 1, 0
        )

    start_spans = jnp.moveaxis(starts.reshape(row_count, span_count, span_len), 1, 0)
    start_state = jnp.zeros((row_count, head_count, HEAD_DIM, HEAD_DIM), jnp.float32)
    final_state, mixed = lax.scan(
        jax.checkpoint(span_mix),
        start_state,
        (spans(queries), spans(forget_log), spans(inject), spans(values), start_spans),
    )
    mixed = jnp.moveaxis(mixed, 0, 1).reshape(row_count, seq_len, head_count, HEAD_DIM)
    grouped = mixed * rms_scale(mixed) * gain_vec.reshape(head_count, HEAD_DIM)
    return grouped.reshape(row_count, seq_len, head_width) * jax.nn.silu(gate_pre)


def per_device(
    layer_input,
    doc_starts,
    norm1_gain,
    w_query,
    w_forget,
    w_input,
    w_gate_out,
    forget_floor,
    group_gain,
    w_out,
    norm2_gain,
    ffn_gate,
    ffn_up,
    ffn_down,
    out_cotangent,
):
    row_count, shard_len, model_width = layer_input.shape
    seq_len = doc_starts.shape[1]
    tokens = row_count * seq_len
    head_width = w_query.shape[1]
    own_rows = layer_input.astype(jnp.float32)
    full_input = lax.all_gather(layer_input, "head", axis=1, tiled=True)
    full_float = full_input.astype(jnp.float32)
    normed = (
        (full_float * rms_scale(full_float) * norm1_gain)
        .astype(jnp.bfloat16)
        .reshape(tokens, model_width)
    )
    proj_weights = jnp.concatenate((w_query, w_forget, w_input, w_gate_out), axis=1)
    projected = jnp.dot(normed, proj_weights, preferred_element_type=jnp.float32)
    projected = projected.reshape(row_count, seq_len, 4 * head_width)
    pieces = tuple(
        (projected[:, :, slot * head_width : (slot + 1) * head_width] for slot in range(4))
    )
    starts_float = doc_starts.astype(jnp.float32)

    def local_core(queries, forget_pre, values, gate_pre, floor_bound, gain_vec):
        return mixer_core(
            queries, forget_pre, values, gate_pre, floor_bound, gain_vec, starts_float
        )

    gated, core_back = jax.vjp(
        local_core, pieces[0], pieces[1], pieces[2], pieces[3], forget_floor, group_gain
    )
    gated_low = gated.astype(jnp.bfloat16).reshape(tokens, head_width)
    mixer_part = jnp.dot(gated_low, w_out, preferred_element_type=jnp.float32).reshape(
        row_count, seq_len, model_width
    )
    resid_rows = own_rows + lax.psum_scatter(mixer_part, "head", scatter_dimension=1, tiled=True)
    ffn_rows_in = (resid_rows * rms_scale(resid_rows) * norm2_gain).astype(jnp.bfloat16)
    ffn_input = lax.all_gather(ffn_rows_in, "head", axis=1, tiled=True)
    ffn_flat = ffn_input.reshape(tokens, model_width)
    gate_cols, up_cols, down_cols = (
        lax.all_gather(ffn_gate, "dp", axis=1, tiled=True),
        lax.all_gather(ffn_up, "dp", axis=1, tiled=True),
        lax.all_gather(ffn_down, "dp", axis=1, tiled=True),
    )
    gate_ff = jnp.dot(ffn_flat, gate_cols, preferred_element_type=jnp.float32)
    up_ff = jnp.dot(ffn_flat, up_cols, preferred_element_type=jnp.float32)
    inner_act = (jax.nn.silu(gate_ff) * up_ff).astype(jnp.bfloat16)
    ffn_part = cross_cols(inner_act, down_cols).reshape(row_count, seq_len, model_width)
    output = (
        resid_rows
        + lax.psum_scatter(
            ffn_part.astype(jnp.bfloat16), "head", scatter_dimension=1, tiled=True
        ).astype(jnp.float32)
    ).astype(jnp.bfloat16)
    grad_full = lax.all_gather(out_cotangent, "head", axis=1, tiled=True).reshape(
        tokens, model_width
    )
    inner_grad = jnp.dot(grad_full, down_cols, preferred_element_type=jnp.float32)
    gate_sig = jax.nn.sigmoid(gate_ff)
    gate_grad = (inner_grad * up_ff * gate_sig * (1.0 + gate_ff * (1.0 - gate_sig))).astype(
        jnp.bfloat16
    )
    up_grad = (inner_grad * gate_ff * gate_sig).astype(jnp.bfloat16)
    ffn_weight_grads = (
        lax.psum_scatter(
            cross_rows(ffn_flat, gate_grad).astype(jnp.bfloat16),
            "dp",
            scatter_dimension=1,
            tiled=True,
        ).astype(jnp.float32),
        lax.psum_scatter(
            cross_rows(ffn_flat, up_grad).astype(jnp.bfloat16),
            "dp",
            scatter_dimension=1,
            tiled=True,
        ).astype(jnp.float32),
        lax.psum_scatter(
            cross_rows(grad_full, inner_act).astype(jnp.bfloat16),
            "dp",
            scatter_dimension=1,
            tiled=True,
        ).astype(jnp.float32),
    )
    ffn_in_part = cross_cols(gate_grad, gate_cols) + cross_cols(up_grad, up_cols)
    ffn_in_grad = lax.psum_scatter(
        ffn_in_part.reshape(row_count, seq_len, model_width),
        "head",
        scatter_dimension=1,
        tiled=True,
    )
    row_scale = rms_scale(resid_rows)
    scaled = ffn_in_grad * norm2_gain
    resid_grad = out_cotangent.astype(jnp.float32) + row_scale * (
        scaled
        - resid_rows * row_scale * row_scale * jnp.mean(scaled * resid_rows, axis=-1, keepdims=True)
    )
    norm2_part = jnp.sum(ffn_in_grad * resid_rows * row_scale, axis=(0, 1))
    mixer_grad_full = lax.all_gather(resid_grad.astype(jnp.bfloat16), "head", axis=1, tiled=True)
    mixer_grad_full = mixer_grad_full.reshape(tokens, model_width)
    out_w_grad = cross_rows(gated_low, mixer_grad_full)
    gated_grad = cross_cols(mixer_grad_full, w_out).reshape(row_count, seq_len, head_width)
    query_g, forget_g, value_g, gate_g, floor_g, gain_g = core_back(gated_grad)
    proj_grad = jnp.concatenate((query_g, forget_g, value_g, gate_g), axis=-1).astype(jnp.bfloat16)
    proj_grad = proj_grad.reshape(tokens, 4 * head_width)
    proj_w_grad = cross_rows(normed, proj_grad)
    normed_part = cross_cols(proj_grad, proj_weights).reshape(row_count, seq_len, model_width)
    normed_grad = lax.psum_scatter(
        normed_part.astype(jnp.bfloat16), "head", scatter_dimension=1, tiled=True
    ).astype(jnp.float32)
    input_scale = rms_scale(own_rows)
    scaled_in = normed_grad * norm1_gain
    input_grad = resid_grad + input_scale * (
        scaled_in
        - own_rows
        * input_scale
        * input_scale
        * jnp.mean(scaled_in * own_rows, axis=-1, keepdims=True)
    )
    norm1_part = jnp.sum(normed_grad * own_rows * input_scale, axis=(0, 1))
    mixer_weight_grads = (
        lax.psum_scatter(proj_w_grad[:, 0:head_width], "dp", scatter_dimension=0, tiled=True),
        lax.psum_scatter(
            proj_w_grad[:, head_width : 2 * head_width], "dp", scatter_dimension=0, tiled=True
        ),
        lax.psum_scatter(
            proj_w_grad[:, 2 * head_width : 3 * head_width], "dp", scatter_dimension=0, tiled=True
        ),
        lax.psum_scatter(
            proj_w_grad[:, 3 * head_width : 4 * head_width], "dp", scatter_dimension=0, tiled=True
        ),
        lax.psum_scatter(out_w_grad, "dp", scatter_dimension=1, tiled=True),
        lax.psum_scatter(gain_g, "dp", scatter_dimension=0, tiled=True),
        lax.psum_scatter(floor_g, "dp", scatter_dimension=0, tiled=True),
    )
    norm1_total, norm2_total = lax.psum((norm1_part, norm2_part), ("head", "dp"))
    return (
        output,
        input_grad,
        mixer_weight_grads[0],
        mixer_weight_grads[1],
        mixer_weight_grads[2],
        mixer_weight_grads[3],
        mixer_weight_grads[4],
        mixer_weight_grads[5],
        mixer_weight_grads[6],
        norm1_total,
        norm2_total,
        ffn_weight_grads[0],
        ffn_weight_grads[1],
        ffn_weight_grads[2],
    )


def solution(mesh):
    placed = (
        P("dp", "head", None),
        P("dp", None),
        P(),
        P(None, "head"),
        P(None, "head"),
        P(None, "head"),
        P(None, "head"),
        P("head"),
        P("head"),
        P("head", None),
        P(),
        P(None, ("head", "dp")),
        P(None, ("head", "dp")),
        P(None, ("head", "dp")),
        P("dp", "head", None),
    )
    return jax.shard_map(
        per_device,
        mesh=mesh,
        in_specs=placed,
        out_specs=(
            P("dp", "head", None),
            P("dp", "head", None),
            P("dp", "head"),
            P("dp", "head"),
            P("dp", "head"),
            P("dp", "head"),
            P("head", "dp"),
            P(("head", "dp")),
            P(("head", "dp")),
            P(),
            P(),
            P(None, ("head", "dp")),
            P(None, ("head", "dp")),
            P(None, ("head", "dp")),
        ),
        check_vma=False,
    )
```

profile of v0, /device:TPU:0, one launch (start us, length us, event | category | flops | bytes accessed | tf_op | source)
XLA Modules:
  0.0 1343.5 jit_solution(16327901451608314590)
XLA Ops:
  10.2 57.7 %all-gather.8.cloned.1.call-done = bf16[2,1024,2048]{2,1,0:T(8,128)(2,1)} async-done(((bf16[2,128,2048]{2,1,0:T(8,128)(2,1)}), bf16[2,1024,2048]{2,1,0:T(8,128)(2,1)}) %all-gather.8.cloned.1.call-update) | async-done | bytes 8388624 | tf_op jit(solution)/shard_map/all_gather | solution.py:102
  67.9 5.2 fusion.78
  73.8 12.4 fusion.83
  86.2 3.5 fusion.122
  102.5 4.9 copy_bitcast_fusion.2
  110.4 75.4 %while.41 = (s32[]{:T(128)}, f32[2,2,128,128]{3,2,1,0:T(8,128)S(1)}, f32[8,2,128,2,128]{2,4,3,1,0:T(8,128)S(1)}, f32[8,2,2,128,128]{4,3,2,1,0:T(8,128)}, f32[8,2...) while((s32[]{:T(128)}, ...), condition=%wide.region_2.3_spmd.clone.clone, body=%wide.region_1.2_spmd.clone.clone.sunk | while | flops 504939520 | bytes 5890239 | solution.py:70
  188.6 4.0 reshape.298
  192.9 3.8 mul.601
  196.8 4.4 mul.602
  201.2 4.1 multiply_convert_fusion.4
  206.3 8.1 fusion.110
  215.1 115.5 %reduce-scatter.13.cloned.1.call-done = f32[2,128,2048]{2,1,0:T(8,128)} async-done(((f32[2,1024,2048]{2,1,0:T(8,128)}), f32[2,128,2048]{2,1,0:T(8,128)}) %reduce-scatter.13.cloned.1.call-update) | async-done | bytes 2097168 | tf_op jit(solution)/shard_map/reduce_scatter | solution.py:129
  337.1 52.2 %all-gather.10.cloned.1.call-done = bf16[2,1024,2048]{2,1,0:T(8,128)(2,1)} async-done(((bf16[2,128,2048]{2,1,0:T(8,128)(2,1)}), bf16[2,1024,2048]{2,1,0:T(8,128)(2,1)}) %all-gather.10.cloned.1.call-update) | async-done | bytes 8388624 | tf_op jit(solution)/shard_map/all_gather | solution.py:131
  389.3 11.1 fusion.123
  400.4 49.4 %all-gather.14.cloned.1.call-done = bf16[2048,704]{0,1:T(8,128)(2,1)} async-done(((bf16[2048,176]{0,1:T(8,128)(2,1)}), bf16[2048,704]{0,1:T(8,128)(2,1)}) %all-gather.14.cloned.1.call-update) | async-done | bytes 2883600 | tf_op jit(solution)/shard_map/all_gather | solution.py:135
  449.8 11.1 fusion.124
  460.9 48.2 %all-gather.16.cloned.1.call-done = bf16[2048,704]{0,1:T(8,128)(2,1)} async-done(((bf16[2048,176]{0,1:T(8,128)(2,1)}), bf16[2048,704]{0,1:T(8,128)(2,1)}) %all-gather.16.cloned.1.call-update) | async-done | bytes 2883600 | tf_op jit(solution)/shard_map/all_gather | solution.py:136
  509.1 54.9 %all-gather.18.cloned.1.call-done = bf16[2,1024,2048]{2,1,0:T(8,128)(2,1)} async-done(((bf16[2,128,2048]{2,1,0:T(8,128)(2,1)}), bf16[2,1024,2048]{2,1,0:T(8,128)(2,1)}) %all-gather.18.cloned.1.call-update) | async-done | bytes 8388624 | tf_op jit(solution)/shard_map/all_gather | solution.py:148
  564.0 15.2 %multiply_convert_fusion = (bf16[2048,704]{0,1:T(8,128)(2,1)S(1)}, bf16[2048,704]{0,1:T(8,128)(2,1)S(1)}, bf16[2048,704]{0,1:T(8,128)(2,1)}) fusion(f32[2048,704]{0,1:T(8,128)} %fusion.123, f32[2048,704]{0,1:T(8,128)} %fusion.124, bf16[2048,2048]{1,0:T(8,128)(2,1)} %bitcast.309, bf16[2048,704]{0,1:T(8,128)(2,1)} %all-gather.16.cloned.1.call-done), kind=kOutput, calls=%fused_computation.131 | convolution fusion | flops 5928648704 | bytes 31457280 | tf_op jit(solution)/shard_map/dot_general | solution.py:151
  579.3 10.6 fusion.125
  589.9 13.9 %convolution_add_fusion.4 = f32[2048,2048]{1,0:T(8,128)} fusion(f32[2048,2048]{1,0:T(8,128)} %fusion.125, bf16[2048,704]{0,1:T(8,128)(2,1)S(1)} %get-tuple-element.621, bf16[2048,704]{0,1:T(8,128)(2,1)S(1)} %copy-done.41), kind=kOutput, calls=%fused_computation.128 | convolution fusion | flops 5909774336 | bytes 39321600 | tf_op jit(solution)/shard_map/dot_general | solution.py:24
  603.8 116.1 %reduce-scatter.17.cloned.1.call-done = f32[2,128,2048]{2,1,0:T(8,128)} async-done(((f32[2,1024,2048]{2,1,0:T(8,128)}), f32[2,128,2048]{2,1,0:T(8,128)}) %reduce-scatter.17.cloned.1.call-update) | async-done | bytes 2097168 | tf_op jit(solution)/shard_map/reduce_scatter | solution.py:178
  724.6 10.6 convolution_convert_fusion.3
  735.3 10.8 convolution_convert_fusion.2
  748.6 10.6 fusion.88
  759.2 19.7 %all-gather.20.cloned.1.call-done = bf16[2,1024,2048]{2,1,0:T(8,128)(2,1)} async-done(((bf16[2,128,2048]{2,1,0:T(8,128)(2,1)}), bf16[2,1024,2048]{2,1,0:T(8,128)(2,1)}) %all-gather.20.cloned.1.call-update) | async-done | bytes 8388624 | tf_op jit(solution)/shard_map/all_gather | solution.py:191
  778.9 9.0 multiply_reduce_fusion.3
  787.9 3.6 reshape.302
  791.5 4.3 copy.119
  803.3 112.2 %while.40 = (s32[]{:T(128)}, f32[2,2,128,128]{3,2,1,0:T(8,128)S(1)}, bf16[8,2,128,2,128]{4,2,3,1,0:T(8,128)(2,1)}, f32[8,2,128,2,128]{2,4,3,1,0:T(8,128)}, f32[8...) while((s32[]{:T(128)}, ...), condition=%wide.region_14.15_spmd.clone, body=%wide.region_11.14_spmd.clone.sunk | while | flops 1110934528 | bytes 17740044 | solution.py:70
  915.5 3.8 copy.128
  924.8 4.1 reshape.303
  931.1 4.1 reshape.304
  941.2 3.8 multiply_reduce_fusion.2
  946.0 13.9 %convolution_convert_fusion.1 = bf16[2,1024,2048]{2,1,0:T(8,128)(2,1)} fusion(bf16[2048,256]{1,0:T(8,128)(2,1)S(1)} %copy-done.43, bf16[2048,256]{1,0:T(8,128)(2,1)S(1)} %copy-done.45, bf16[2048,256]{1,0:T(8,128)(2,1)S(1)} %copy-done.47, bf16[2048,256]{1,0:T(8,128)(2,1)} %param.22, bf16[2,1024,256]{2,1,0:T(8,128)(2,1)} %get-tuple-element.620, ...), kind=kOutput, calls=%fused_computation.135 | convolution fusion | flops 8627683328 | bytes 16777216 | tf_op jit(solution)/shard_map/dot_general | solution.py:24
  959.9 11.7 convolution_convert_fusion
  973.6 14.6 %fusion.85 = f32[2048,1024]{1,0:T(8,128)S(1)} fusion(bf16[2,1024,2048]{2,1,0:T(8,128)(2,1)} %all-gather.8.cloned.1.call-done, f32[2048]{0:T(1024)S(1)} %copy-done.28, f32[2,1024]{1,0:T(2,128)S(1)} %copy-done.38, bf16[2,1024,256]{2,1,0:T(8,128)(2,1)} %get-tuple-element.620, bf16[2,1024,256]{2,1,0:T(8,128)(2,1)S(1)} %copy-done.18, ...), kind=kOutput, calls=%fused_computation.136 | convolution fusion | flops 8623489024 | bytes 20987904 | tf_op jit(solution)/shard_map/dot_general | solution.py:18
  994.0 7.3 convolution_bitcast_fusion.6
  1010.6 11.8 all-reduce.4
  1023.6 7.7 reduce-scatter.19.cloned.1.call-done
  1033.5 39.8 %all-reduce.3 = (f32[2048]{0:T(1024)}, f32[2048]{0:T(1024)}) all-reduce(f32[2048]{0:T(1024)S(1)} %get-tuple-element.549, f32[2048]{0:T(1024)S(1)} %copy-done.26), channel_id=1, replica_groups=mesh['head'=8,'dp'=4] {'head','dp'}, use_global_device_ids=true, to_apply=%region_27.28 | all-reduce | flops 4096 | bytes 32768 | tf_op jit(solution)/shard_map/psum | solution.py:228
  1073.2 33.5 %reduce-scatter.15.cloned.1.call-done = bf16[2,128,2048]{2,1,0:T(8,128)(2,1)} async-done(((bf16[2,1024,2048]{2,1,0:T(8,128)(2,1)}), bf16[2,128,2048]{2,1,0:T(8,128)(2,1)}) %reduce-scatter.15.cloned.1.call-update) | async-done | bytes 1048592 | tf_op jit(solution)/shard_map/reduce_scatter | solution.py:144
  1106.8 5.8 fusion.91
  1112.6 40.6 %reduce-scatter.21.cloned.1.call-done = f32[512,256]{1,0:T(8,128)} async-done(((f32[2048,256]{1,0:T(8,128)}), f32[512,256]{1,0:T(8,128)}) %reduce-scatter.21.cloned.1.call-update) | async-done | bytes 524304 | tf_op jit(solution)/shard_map/reduce_scatter | solution.py:214
  1153.1 45.6 %reduce-scatter.23.cloned.1.call-done = f32[512,256]{1,0:T(8,128)} async-done(((f32[2048,256]{1,0:T(8,128)}), f32[512,256]{1,0:T(8,128)}) %reduce-scatter.23.cloned.1.call-update) | async-done | bytes 524304 | tf_op jit(solution)/shard_map/reduce_scatter | solution.py:215
  1198.7 45.6 %reduce-scatter.25.cloned.1.call-done = f32[512,256]{1,0:T(8,128)} async-done(((f32[2048,256]{1,0:T(8,128)}), f32[512,256]{1,0:T(8,128)}) %reduce-scatter.25.cloned.1.call-update) | async-done | bytes 524304 | tf_op jit(solution)/shard_map/reduce_scatter | solution.py:218
  1244.3 45.8 %reduce-scatter.27.cloned.1.call-done = f32[512,256]{1,0:T(8,128)} async-done(((f32[2048,256]{1,0:T(8,128)}), f32[512,256]{1,0:T(8,128)}) %reduce-scatter.27.cloned.1.call-update) | async-done | bytes 524304 | tf_op jit(solution)/shard_map/reduce_scatter | solution.py:221
  1290.1 45.6 %reduce-scatter.29.cloned.1.call-done = f32[256,512]{1,0:T(8,128)} async-done(((f32[256,2048]{1,0:T(8,128)}), f32[256,512]{1,0:T(8,128)}) %reduce-scatter.29.cloned.1.call-update) | async-done | bytes 524304 | tf_op jit(solution)/shard_map/reduce_scatter | solution.py:224
  (521 shorter events, 265.0 us)
Async XLA Ops:
  8.0 198.3 %copy-start = (bf16[256,2048]{1,0:T(8,128)(2,1)S(1)}, bf16[256,2048]{1,0:T(8,128)(2,1)}, u32[]{:S(2)}) copy-start(bf16[256,2048]{1,0:T(8,128)(2,1)} %param.28) | copy-start | bytes 3145732
  8.0 59.9 %all-gather.8.cloned.1.call-start = ((), (), s32[]{:S(2)}) async-start(), calls=%async_computation.12 | async-start | bytes 9437184 | tf_op jit(solution)/shard_map/all_gather | solution.py:102
  8.8 321.8 %reduce-scatter.13.cloned.1.call-start = ((), (), s32[]{:S(2)}) async-start(), calls=%async_computation.13 | async-start | bytes 18874368 | tf_op jit(solution)/shard_map/reduce_scatter | solution.py:129
  9.5 76.7 %copy-start.35 = (f32[256]{0:T(256)}, f32[256]{0:T(256)S(1)}, u32[]{:S(2)}) copy-start(f32[256]{0:T(256)S(1)} %broadcast_subtract_fusion) | copy-start | bytes 3076
  10.2 63.5 %copy-start.27 = (f32[2048]{0:T(1024)S(1)}, f32[2048]{0:T(1024)}, u32[]{:S(2)}) copy-start(f32[2048]{0:T(1024)} %param.21) | copy-start | bytes 24580
  10.2 63.5 %copy-start.42 = (bf16[2048,256]{1,0:T(8,128)(2,1)S(1)}, bf16[2048,256]{1,0:T(8,128)(2,1)}, u32[]{:S(2)}) copy-start(bf16[2048,256]{1,0:T(8,128)(2,1)} %param.25) | copy-start | bytes 3145732
  67.9 5.9 copy-start.44
  67.9 5.9 copy-start.46
  67.9 5.9 copy-start.48
  86.2 5.1 copy-start.7
  102.5 4.9 copy-start.15
  186.0 6.5 copy-start.22
  214.4 122.7 %all-gather.12.cloned.1.call-start = ((), (), s32[]{:S(2)}) async-start(), calls=%async_computation.15 | async-start | bytes 3604480 | tf_op jit(solution)/shard_map/all_gather | solution.py:134
  215.0 118.4 %copy-start.24 = (f32[2048]{0:T(1024)S(1)}, f32[2048]{0:T(1024)}, u32[]{:S(2)}) copy-start(f32[2048]{0:T(1024)} %param.29) | copy-start | bytes 24580
  215.0 174.3 %all-gather.10.cloned.1.call-start = ((), (), s32[]{:S(2)}) async-start(), calls=%async_computation.14 | async-start | bytes 9437184 | tf_op jit(solution)/shard_map/all_gather | solution.py:131
  333.4 389.4 %copy-start.1 = (f32[2,128,2048]{2,1,0:T(8,128)}, f32[2,128,2048]{2,1,0:T(8,128)S(1)}, u32[]{:S(2)}) copy-start(f32[2,128,2048]{2,1,0:T(8,128)S(1)} %get-tuple-element.602) | copy-start | bytes 6291460
  333.4 389.4 %copy-start.29 = (f32[2,128]{1,0:T(2,128)}, f32[2,128]{1,0:T(2,128)S(1)}, u32[]{:S(2)}) copy-start(f32[2,128]{1,0:T(2,128)S(1)} %add_rsqrt_fusion.2) | copy-start | bytes 3076
  335.0 114.8 %all-gather.14.cloned.1.call-start = ((), (), s32[]{:S(2)}) async-start(), calls=%async_computation.16 | async-start | bytes 3604480 | tf_op jit(solution)/shard_map/all_gather | solution.py:135
  335.6 173.6 %all-gather.16.cloned.1.call-start = ((), (), s32[]{:S(2)}) async-start(), calls=%async_computation.17 | async-start | bytes 3604480 | tf_op jit(solution)/shard_map/all_gather | solution.py:136
  336.3 227.7 %all-gather.18.cloned.1.call-start = ((), (), s32[]{:S(2)}) async-start(), calls=%async_computation.19 | async-start | bytes 9437184 | tf_op jit(solution)/shard_map/all_gather | solution.py:148
  337.1 382.8 %reduce-scatter.17.cloned.1.call-start = ((), (), s32[]{:S(2)}) async-start(), calls=%async_computation.20 | async-start | bytes 18874368 | tf_op jit(solution)/shard_map/reduce_scatter | solution.py:178
  564.0 15.2 %copy-start.40 = (bf16[2048,704]{0,1:T(8,128)(2,1)S(1)}, bf16[2048,704]{0,1:T(8,128)(2,1)}, u32[]{:S(2)}) copy-start(bf16[2048,704]{0,1:T(8,128)(2,1)} %all-gather.12.cloned.1.call-done) | copy-start | bytes 8650756
  579.2 10.6 copy-start.51
  579.2 10.6 copy-start.50
  579.2 10.6 copy-start.41
  603.8 175.1 %all-gather.20.cloned.1.call-start = ((), (), s32[]{:S(2)}) async-start(), calls=%async_computation.21 | async-start | bytes 9437184 | tf_op jit(solution)/shard_map/all_gather | solution.py:191
  724.5 278.7 %reduce-scatter.31.cloned.1.call-start = ((), (), s32[]{:S(2)}) async-start(), calls=%async_computation.28 | async-start | bytes 3604480 | tf_op jit(solution)/shard_map/reduce_scatter | solution.py:158
  735.2 270.4 %reduce-scatter.33.cloned.1.call-start = ((), (), s32[]{:S(2)}) async-start(), calls=%async_computation.29 | async-start | bytes 3604480 | tf_op jit(solution)/shard_map/reduce_scatter | solution.py:164
  746.1 262.0 %reduce-scatter.35.cloned.1.call-start = ((), (), s32[]{:S(2)}) async-start(), calls=%async_computation.30 | async-start | bytes 3604480 | tf_op jit(solution)/shard_map/reduce_scatter | solution.py:170
  759.1 19.8 %copy-start.16 = (f32[2,1024,256]{2,1,0:T(8,128)S(1)}, f32[2,1024,256]{2,1,0:T(8,128)}, u32[]{:S(2)}) copy-start(f32[2,1024,256]{2,1,0:T(8,128)} %get-tuple-element.604) | copy-start | bytes 6291460
  759.1 272.1 %reduce-scatter.19.cloned.1.call-start = ((), (), s32[]{:S(2)}) async-start(), calls=%async_computation.22 | async-start | bytes 9437184 | tf_op jit(solution)/shard_map/reduce_scatter | solution.py:200
  915.5 6.3 copy-start.13
  935.2 5.9 copy-start.14
  935.2 5.9 copy-start.36
  941.2 4.8 copy-start.17
  941.2 4.8 copy-start.19
  941.2 4.8 copy-start.43
  959.9 146.9 %reduce-scatter.15.cloned.1.call-start = ((), (), s32[]{:S(2)}) async-start(), calls=%async_computation.18 | async-start | bytes 9437184 | tf_op jit(solution)/shard_map/reduce_scatter | solution.py:144
  971.7 181.5 %reduce-scatter.21.cloned.1.call-start = ((), (), s32[]{:S(2)}) async-start(), calls=%async_computation.23 | async-start | bytes 2621440 | tf_op jit(solution)/shard_map/reduce_scatter | solution.py:214
  991.7 207.1 %reduce-scatter.23.cloned.1.call-start = ((), (), s32[]{:S(2)}) async-start(), calls=%async_computation.24 | async-start | bytes 2621440 | tf_op jit(solution)/shard_map/reduce_scatter | solution.py:215
  992.2 252.1 %reduce-scatter.25.cloned.1.call-start = ((), (), s32[]{:S(2)}) async-start(), calls=%async_computation.25 | async-start | bytes 2621440 | tf_op jit(solution)/shard_map/reduce_scatter | solution.py:218
  993.0 297.1 %reduce-scatter.27.cloned.1.call-start = ((), (), s32[]{:S(2)}) async-start(), calls=%async_computation.26 | async-start | bytes 2621440 | tf_op jit(solution)/shard_map/reduce_scatter | solution.py:221
  993.7 342.0 %reduce-scatter.29.cloned.1.call-start = ((), (), s32[]{:S(2)}) async-start(), calls=%async_computation.27 | async-start | bytes 2621440 | tf_op jit(solution)/shard_map/reduce_scatter | solution.py:224
  1008.0 25.4 %copy-start.26 = (f32[2048]{0:T(1024)S(1)}, f32[2048]{0:T(1024)}, u32[]{:S(2)}) copy-start(f32[2048]{0:T(1024)} %get-tuple-element.547) | copy-start | bytes 24580
  1008.0 98.7 %copy-start.2 = (f32[2,128,2048]{2,1,0:T(8,128)S(1)}, f32[2,128,2048]{2,1,0:T(8,128)}, u32[]{:S(2)}) copy-start(f32[2,128,2048]{2,1,0:T(8,128)} %copy-done.1) | copy-start | bytes 6291460
  1008.0 98.7 %copy-start.25 = (f32[2048]{0:T(1024)S(1)}, f32[2048]{0:T(1024)}, u32[]{:S(2)}) copy-start(f32[2048]{0:T(1024)} %param.29) | copy-start | bytes 24580
  1008.1 98.7 %copy-start.30 = (f32[2,128]{1,0:T(2,128)S(1)}, f32[2,128]{1,0:T(2,128)}, u32[]{:S(2)}) copy-start(f32[2,128]{1,0:T(2,128)} %copy-done.29) | copy-start | bytes 3076
  1008.1 98.7 %copy-start.34 = (f32[2,128]{1,0:T(2,128)S(1)}, f32[2,128]{1,0:T(2,128)}, u32[]{:S(2)}) copy-start(f32[2,128]{1,0:T(2,128)} %copy-done.33) | copy-start | bytes 3076
  (23 other events, 58.4 us)
Sparse Core Ops, SparseCore 0:
  10.8 57.0 all-gather.7
  214.6 115.9 reduce-scatter.12
  603.9 115.9 reduce-scatter.16
Sparse Core Ops, SparseCore 1:
  216.5 59.0 all-gather.11
  335.1 54.2 all-gather.9
  390.8 59.0 all-gather.13
  451.4 57.7 all-gather.15
  511.1 52.9 all-gather.17
  724.6 54.2 all-gather.19
  781.1 56.2 reduce-scatter.30
  839.5 55.9 reduce-scatter.32
  897.6 55.9 reduce-scatter.34
  959.9 71.3 reduce-scatter.18
  1035.0 71.7 reduce-scatter.14
  1109.6 43.4 reduce-scatter.20
  1156.0 42.7 reduce-scatter.22
  1201.6 42.7 reduce-scatter.24
  1247.3 42.7 reduce-scatter.26
  1293.0 42.7 reduce-scatter.28
where the time goes:
time: 1350 us; the launch traced here: 1340 us
  waiting for transfers between devices  783 us (58%)
  matrix products  304 us (23%)
  local copies, waits for them, and re-layouts  125 us (9%)
  other arithmetic  60.6 us (4%)
  blocking collectives  51.5 us (4%)
  between operations  17.2 us (1%)
    reduce_scatter x1, waiting for transfers between devices, per_device(): lax.psum_scatter(ffn_in_part.reshape(row_count, seq_len, model_width), 'h...  116 us
    reduce_scatter x1, waiting for transfers between devices, per_device(): lax.psum_scatter(mixer_part, 'head', scatter_dimension=1, tiled=True)  115 us
    dot_general x5, matrix products, cross_cols(): lax.dot_general(left, right, (((1,), (1,)), ((), ())), preferred_element_...  59 us
    all_gather x1, waiting for transfers between devices, per_device(): full_input = lax.all_gather(layer_input, 'head', axis=1, tiled=True)  57.7 us
    all_gather x1, waiting for transfers between devices, per_device(): lax.all_gather(out_cotangent, 'head', axis=1, tiled=True)  54.9 us
    dot_general x5, matrix products, cross_rows(): lax.dot_general(left, right, (((0,), (0,)), ((), ())), preferred_element_...  53.8 us
    all_gather x1, waiting for transfers between devices, per_device(): ffn_input = lax.all_gather(ffn_rows_in, 'head', axis=1, tiled=True)  52.2 us
    all_gather x1, waiting for transfers between devices, per_device(): lax.all_gather(ffn_up, 'dp', axis=1, tiled=True)  49.4 us
  transfers between devices with their start and end apart: 19, of which 15 were waited for; matrix products, arithmetic and copies ran while one was open for 22% of the time, Pallas kernels for 0%

commit v1 on v0

v1 whole, which is shorter than its diff:
```python
import functools

import jax
import jax.numpy as jnp
from jax import lax
from jax.experimental import pallas as pl
from jax.experimental.pallas import tpu as pltpu
from jax.sharding import PartitionSpec as P

HEAD_DIM = 128
epsilon = 1e-06
f32 = jnp.float32
bf16 = jnp.bfloat16


def swap(tensor, bit, size):
    return lax.ppermute(tensor, "head", [(at, at ^ bit) for at in range(size)])


def mm(left, right, dims, out=f32):
    return lax.dot_general(left, right, (dims, ((), ())), preferred_element_type=out)


NN = ((1,), (0,))
NT = ((1,), (1,))
TN = ((0,), (0,))


def rms_scale(tensor):
    return lax.rsqrt(jnp.mean(tensor * tensor, axis=-1, keepdims=True) + epsilon)


def gather_near(own, bits, size):
    return swap(own, bits[0], size), swap(own, bits[1], size)


def gather_far(near, bits, size):
    half = near[0].shape[0] // 2
    return swap(near[0][:half], bits[1], size), swap(near[1][half:], bits[0], size)


def gather_chips(own, bits, size):
    if len(bits) == 2:
        near = gather_near(own, bits, size)
        return [own, *near, *gather_far(near, bits, size)]
    parts = [own]
    for bit in bits:
        moved = swap(jnp.stack(parts), bit, size)
        parts = parts + [moved[at] for at in range(len(parts))]
    return parts


def scatter_chips(part_of, bits, size):
    if len(bits) == 2:
        first, second = bits
        both = part_of(3).astype(bf16)
        half = both.shape[0] // 2
        top_both, bottom_both = swap(both[:half], first, size), swap(both[half:], second, size)
        at_first, at_second = part_of(1), part_of(2)
        top_first = swap(at_first[:half].astype(bf16), first, size)
        bottom_second = swap(at_second[half:].astype(bf16), second, size)
        bottom_first = swap(
            (at_first[half:].astype(f32) + bottom_both.astype(f32)).astype(bf16), first, size
        )
        top_second = swap(
            (at_second[:half].astype(f32) + top_both.astype(f32)).astype(bf16), second, size
        )
        own = part_of(0).astype(f32)
        top = own[:half] + top_first.astype(f32) + top_second.astype(f32)
        bottom = own[half:] + bottom_first.astype(f32) + bottom_second.astype(f32)
        return jnp.concatenate((top, bottom))
    parts = [part_of(at).astype(f32) for at in range(1 << len(bits))]
    for bit in reversed(bits):
        count = len(parts) // 2
        moved = swap(jnp.stack(parts[count:]).astype(bf16), bit, size)
        parts = [parts[at] + moved[at].astype(f32) for at in range(count)]
    return parts[0]


def after(tensor, *others):
    return lax.optimization_barrier((tensor,) + others)[0]


def halves(tensor):
    high = tensor.astype(bf16)
    return high, (tensor - high.astype(f32)).astype(bf16)


def cumulate(triangle, tensor):
    high, low = halves(tensor)
    return mm(triangle, high, NN) + mm(triangle, low, NN)


def span_masks(info, block, blocks, seg_ref):
    span = seg_ref.shape[-1]
    across = jnp.broadcast_to(seg_ref[0], (span, span))
    down = across.T
    rows = lax.broadcasted_iota(jnp.int32, (span, span), 0)
    cols = lax.broadcasted_iota(jnp.int32, (span, span), 1)
    before = info[1 + block]
    last = info[1 + blocks + block]
    same = (across == down) & (rows >= cols)
    column = down[:, :1]
    carried = (column == before).astype(f32)
    to_final = (column == last).astype(f32)
    through = (before == last).astype(f32)
    return rows, cols, same, carried, to_final, through


def head_columns(head, half_heads, half_width):
    base = (head // half_heads) * 4 * half_width + (head % half_heads) * HEAD_DIM
    return [slice(base + at * half_width, base + at * half_width + HEAD_DIM) for at in range(4)]


def forward_kernel(
    blocks, half_heads, info, proj_ref, floor_ref, gain_ref, seg_ref, gated_ref, mixed_ref, states_ref, scores_ref, state
):
    block = pl.program_id(0)
    half_width = half_heads * HEAD_DIM

    @pl.when(block == 0)
    def _():
        state[...] = jnp.zeros_like(state)

    rows, cols, same, carried, to_final, through = span_masks(info, block, blocks, seg_ref)
    span = rows.shape[0]
    lower = (rows >= cols).astype(bf16)
    for head in range(2 * half_heads):
        lanes = slice(head * HEAD_DIM, (head + 1) * HEAD_DIM)
        at_q, at_f, at_v, at_g = head_columns(head, half_heads, half_width)
        queries, forget_pre = proj_ref[:, at_q], proj_ref[:, at_f]
        values, gate = proj_ref[:, at_v].astype(bf16), proj_ref[:, at_g]
        inject = (1.0 - floor_ref[:, lanes]) / (1.0 + jnp.exp(forget_pre))
        decays = cumulate(lower, jnp.log(1.0 - inject))
        last = decays[span - 1 :, :]
        lifted, lifted_rest = halves(queries * jnp.exp(decays))
        lowered, lowered_rest = halves(inject * jnp.exp(-decays))
        scores = mm(lifted, lowered, NT) + mm(lifted, lowered_rest, NT) + mm(lifted_rest, lowered, NT)
        scores = jnp.where(same, scores, 0.0).astype(bf16)
        scores_ref[0, head] = scores
        now = state[head]
        states_ref[0, head] = now
        mixed = mm(scores, values, NN) + carried * mm(lifted, now.astype(bf16), NT)
        kept = (inject * jnp.exp(last - decays) * to_final).astype(bf16)
        state[head] = now * (jnp.exp(last) * through) + mm(values, kept, TN)
        mixed_ref[:, lanes] = mixed
        grouped = mixed * rms_scale(mixed) * gain_ref[:, lanes]
        gated_ref[:, lanes] = (grouped * gate / (1.0 + jnp.exp(-gate))).astype(bf16)


def backward_kernel(
    blocks, half_heads, info, proj_ref, floor_ref, gain_ref, seg_ref, mixed_ref, grad_ref, states_ref, scores_ref,
    proj_grad_ref, floor_grad_ref, gain_grad_ref, state_grad,
):
    step = pl.program_id(0)
    block = blocks - 1 - step
    half_width = half_heads * HEAD_DIM

    @pl.when(step == 0)
    def _():
        state_grad[...] = jnp.zeros_like(state_grad)
        floor_grad_ref[...] = jnp.zeros_like(floor_grad_ref)
        gain_grad_ref[...] = jnp.zeros_like(gain_grad_ref)

    rows, cols, same, carried, to_final, through = span_masks(info, block, blocks, seg_ref)
    span = rows.shape[0]
    lower = (rows >= cols).astype(bf16)
    upper = (rows <= cols).astype(bf16)
    is_last = lax.broadcasted_iota(jnp.int32, (span, 1), 0) == span - 1
    for head in range(2 * half_heads):
        lanes = slice(head * HEAD_DIM, (head + 1) * HEAD_DIM)
        at_q, at_f, at_v, at_g = head_columns(head, half_heads, half_width)
        queries, forget_pre = proj_ref[:, at_q], proj_ref[:, at_f]
        values, gate = proj_ref[:, at_v].astype(bf16), proj_ref[:, at_g]
        mixed, gain, grad = mixed_ref[:, lanes], gain_ref[:, lanes], grad_ref[:, lanes]
        gate_sig = 1.0 / (1.0 + jnp.exp(-gate))
        scale = rms_scale(mixed)
        unit = mixed * scale
        grouped_grad = grad * gate * gate_sig
        proj_grad_ref[:, at_g] = (
            grad * unit * gain * gate_sig * (1.0 + gate * (1.0 - gate_sig))
        ).astype(bf16)
        gain_grad_ref[:, lanes] += jnp.sum(grouped_grad * unit, axis=0, keepdims=True)
        unit_grad = grouped_grad * gain
        mixed_grad, mixed_rest = halves(
            scale * (unit_grad - unit * jnp.mean(unit_grad * unit, axis=-1, keepdims=True))
        )
        room = 1.0 - floor_ref[:, lanes]
        sig = 1.0 / (1.0 + jnp.exp(forget_pre))
        inject = room * sig
        decays = cumulate(lower, jnp.log(1.0 - inject))
        last = decays[span - 1 :, :]
        rise, fall, rest = jnp.exp(decays), jnp.exp(-decays), jnp.exp(last - decays) * to_final
        lifted = (queries * rise).astype(bf16)
        lowered = (inject * fall).astype(bf16)
        kept = (inject * rest).astype(bf16)
        scores = scores_ref[0, head]
        scores_grad = mm(mixed_grad, values, NT) + mm(mixed_rest, values, NT)
        scores_grad = jnp.where(same, scores_grad, 0.0).astype(bf16)
        now, after = states_ref[0, head], state_grad[head]
        after_low, now_low = after.astype(bf16), now.astype(bf16)
        state_part = mm(mixed_grad, now_low, NN) + mm(mixed_rest, now_low, NN)
        lifted_grad = mm(scores_grad, lowered, NN) + carried * state_part
        lowered_grad = mm(scores_grad, lifted, TN)
        kept_grad = mm(values, after_low, NN)
        value_grad = mm(scores, mixed_grad, TN) + mm(kept, after_low, NT)
        kept_term = kept_grad * kept.astype(f32)
        decay_grad = lifted_grad * lifted.astype(f32) - lowered_grad * lowered.astype(f32) - kept_term
        pass_on = jnp.exp(last) * through
        last_grad = jnp.sum(kept_term, axis=0, keepdims=True) + pass_on * jnp.sum(
            now * after, axis=0, keepdims=True
        )
        decay_grad = decay_grad + jnp.where(is_last, last_grad, 0.0)
        log_grad = cumulate(upper, decay_grad)
        inject_grad = lowered_grad * fall + kept_grad * rest - log_grad / (1.0 - inject)
        state_grad[head] = after * pass_on + mm(
            mixed_grad, (lifted.astype(f32) * carried).astype(bf16), TN
        )
        proj_grad_ref[:, at_q] = (lifted_grad * rise).astype(bf16)
        proj_grad_ref[:, at_f] = (-inject_grad * room * sig * (1.0 - sig)).astype(bf16)
        proj_grad_ref[:, at_v] = value_grad.astype(bf16)
        floor_grad_ref[:, lanes] -= jnp.sum(inject_grad * sig, axis=0, keepdims=True)


def recurrence(info, proj, floor_row, gain_row, seg, half_heads, size):
    blocks, _, span = seg.shape
    width = floor_row.shape[1]
    spot = lambda block, info: (block ^ info[0], 0)
    fixed = lambda block, info: (0, 0)
    return pl.pallas_call(
        functools.partial(forward_kernel, blocks, half_heads),
        out_shape=(
            jax.ShapeDtypeStruct((blocks * span, width), bf16),
            jax.ShapeDtypeStruct((blocks * span, width), f32),
            jax.ShapeDtypeStruct((blocks, 2 * half_heads, HEAD_DIM, HEAD_DIM), f32),
            jax.ShapeDtypeStruct((blocks, 2 * half_heads, span, span), bf16),
        ),
        grid_spec=pltpu.PrefetchScalarGridSpec(
            num_scalar_prefetch=1,
            grid=(blocks,),
            in_specs=[
                pl.BlockSpec((span, 4 * width), spot),
                pl.BlockSpec((1, width), fixed),
                pl.BlockSpec((1, width), fixed),
                pl.BlockSpec((1, 1, span), lambda block, info: (block, 0, 0)),
            ],
            out_specs=[
                pl.BlockSpec((span, width), spot),
                pl.BlockSpec((span, width), spot),
                pl.BlockSpec(
                    (1, 2 * half_heads, HEAD_DIM, HEAD_DIM), lambda block, info: (block, 0, 0, 0)
                ),
                pl.BlockSpec((1, 2 * half_heads, span, span), lambda block, info: (block, 0, 0, 0)),
            ],
            scratch_shapes=[pltpu.VMEM((2 * half_heads, HEAD_DIM, HEAD_DIM), f32)],
        ),
        compiler_params=pltpu.CompilerParams(vmem_limit_bytes=24 * 1024 * 1024),
        cost_estimate=pl.CostEstimate(
            flops=blocks * 2 * half_heads * 16 * HEAD_DIM**3, bytes_accessed=16 * 2**20, transcendentals=0
        ),
    )(info, proj, floor_row, gain_row, seg)


def recurrence_back(info, proj, floor_row, gain_row, seg, mixed, grad, states, scores, half_heads, size):
    blocks, _, span = seg.shape
    width = floor_row.shape[1]
    spot = lambda step, info: ((blocks - 1 - step) ^ info[0], 0)
    fixed = lambda step, info: (0, 0)
    return pl.pallas_call(
        functools.partial(backward_kernel, blocks, half_heads),
        out_shape=(
            jax.ShapeDtypeStruct((blocks * span, 4 * width), bf16),
            jax.ShapeDtypeStruct((1, width), f32),
            jax.ShapeDtypeStruct((1, width), f32),
        ),
        grid_spec=pltpu.PrefetchScalarGridSpec(
            num_scalar_prefetch=1,
            grid=(blocks,),
            in_specs=[
                pl.BlockSpec((span, 4 * width), spot),
                pl.BlockSpec((1, width), fixed),
                pl.BlockSpec((1, width), fixed),
                pl.BlockSpec((1, 1, span), lambda step, info: (blocks - 1 - step, 0, 0)),
                pl.BlockSpec((span, width), spot),
                pl.BlockSpec((span, width), spot),
                pl.BlockSpec(
                    (1, 2 * half_heads, HEAD_DIM, HEAD_DIM),
                    lambda step, info: (blocks - 1 - step, 0, 0, 0),
                ),
                pl.BlockSpec(
                    (1, 2 * half_heads, span, span), lambda step, info: (blocks - 1 - step, 0, 0, 0)
                ),
            ],
            out_specs=[
                pl.BlockSpec((span, 4 * width), spot),
                pl.BlockSpec((1, width), fixed),
                pl.BlockSpec((1, width), fixed),
            ],
            scratch_shapes=[pltpu.VMEM((2 * half_heads, HEAD_DIM, HEAD_DIM), f32)],
        ),
        compiler_params=pltpu.CompilerParams(vmem_limit_bytes=24 * 1024 * 1024),
        cost_estimate=pl.CostEstimate(
            flops=blocks * 2 * half_heads * 32 * HEAD_DIM**3, bytes_accessed=24 * 2**20, transcendentals=0
        ),
    )(info, proj, floor_row, gain_row, seg, mixed, grad, states, scores)


def per_device(
    size,
    depth,
    layer_input,
    doc_starts,
    norm1_gain,
    w_query,
    w_forget,
    w_input,
    w_gate_out,
    forget_floor,
    group_gain,
    w_out,
    norm2_gain,
    ffn_gate,
    ffn_up,
    ffn_down,
    out_cotangent,
):
    row_count, shard_len, model_width = layer_input.shape
    assert row_count == 2 and size & (size - 1) == 0
    seq_len = doc_starts.shape[1]
    half_width = w_query.shape[1]
    half_heads = half_width // HEAD_DIM
    width = 2 * half_width
    me = lax.axis_index("head")
    place = lax.axis_index("dp")
    row = me % 2
    bits = [1 << at for at in range(1, size.bit_length() - 1)]
    own_tokens = 2 * shard_len
    hidden_dev = ffn_gate.shape[1]
    hidden_half = depth * hidden_dev

    def pick(tensor, at):
        return lax.dynamic_index_in_dim(tensor, at, 0, keepdims=False)

    def to_row(tensor):
        return jnp.concatenate((pick(tensor, row), swap(pick(tensor, 1 - row), 1, size)))

    def from_row(tensor):
        mine, other = tensor[:shard_len], swap(tensor[shard_len:], 1, size)
        return jnp.where(row == 0, jnp.stack((mine, other)), jnp.stack((other, mine)))

    def chunk(tensor, at):
        return tensor[at * own_tokens : (at + 1) * own_tokens]

    gate_up = lax.all_gather(jnp.stack((ffn_gate.T, ffn_up.T)), "dp", axis=1, tiled=True)
    down = lax.all_gather(after(ffn_down.T, gate_up), "dp", axis=0, tiled=True)

    own_rows = to_row(layer_input).astype(f32)
    input_scale = rms_scale(own_rows)
    normed_own = (own_rows * input_scale * norm1_gain).astype(bf16)
    normed_parts = gather_chips(normed_own, bits, size)
    normed = jnp.concatenate(normed_parts)

    proj_own = jnp.concatenate((w_query, w_forget, w_input, w_gate_out), axis=1)
    proj_weights = jnp.concatenate((proj_own, swap(proj_own, 1, size)), axis=1)
    out_weights = jnp.concatenate((w_out, swap(w_out, 1, size)))
    vectors = jnp.stack((forget_floor, group_gain))
    vectors = jnp.concatenate((vectors, swap(vectors, 1, size)), axis=1)
    floor_row, gain_row = vectors[:1], vectors[1:]

    seg = jnp.cumsum(pick(doc_starts, row)).reshape(size, shard_len)
    seg_last = seg[:, -1]
    info = jnp.concatenate((me[None], jnp.zeros((1,), jnp.int32), seg_last[:-1], seg_last))
    seg = seg[:, None, :]

    proj = mm(normed, proj_weights, NN)
    gated, mixed, states, scores = recurrence(info, proj, floor_row, gain_row, seg, half_heads, size)
    cot_own = to_row(out_cotangent)
    if len(bits) == 2:
        cot_near = gather_near(after(cot_own, *normed_parts), bits, size)

    resid = own_rows + scatter_chips(
        lambda at: mm(chunk(gated, at), out_weights, NN).astype(bf16), bits, size
    )
    row_scale = rms_scale(resid)
    ffn_own = (resid * row_scale * norm2_gain).astype(bf16)
    ffn_parts = gather_chips(ffn_own, bits, size)
    ffn_in = jnp.concatenate(ffn_parts)
    if len(bits) == 2:
        cot_held = [after(near, *ffn_parts) for near in cot_near]
        cot_parts = [cot_own, *cot_near, *gather_far(cot_held, bits, size)]
    else:
        cot_parts = gather_chips(after(cot_own, *ffn_parts), bits, size)
    cot = jnp.concatenate(cot_parts)

    gate_up = jnp.concatenate((gate_up, swap(gate_up, 1, size)), axis=1)
    gate_rows, up_rows = gate_up[0], gate_up[1]
    down_rows = jnp.concatenate((down, swap(down, 1, size)))
    gate_ff = mm(ffn_in, gate_rows, NT)
    up_ff = mm(ffn_in, up_rows, NT)
    gate_sig = jax.nn.sigmoid(gate_ff)
    inner = (gate_ff * gate_sig * up_ff).astype(bf16)

    def pair_grad(left, right, cut):
        other = swap(mm(left[:, cut:], right, TN).astype(bf16), 1, size)
        return (mm(left[:, :cut], right, TN) + other.astype(f32)).astype(bf16)

    down_grad = pair_grad(inner, cot, hidden_half)
    ffn_down_grad = lax.psum_scatter(down_grad, "dp", scatter_dimension=0, tiled=True)

    inner_grad = mm(cot, down_rows, NT)
    gate_grad = (inner_grad * up_ff * gate_sig * (1.0 + gate_ff * (1.0 - gate_sig))).astype(bf16)
    up_grad = (inner_grad * gate_ff * gate_sig).astype(bf16)
    ffn_in_grad = scatter_chips(
        lambda at: (
            mm(chunk(gate_grad, at), gate_rows, NN) + mm(chunk(up_grad, at), up_rows, NN)
        ).astype(bf16),
        bits,
        size,
    )
    gate_up_grad = jnp.stack(
        (pair_grad(gate_grad, ffn_in, hidden_half), pair_grad(up_grad, ffn_in, hidden_half))
    )
    gate_up_grad = lax.psum_scatter(
        after(gate_up_grad, down_grad), "dp", scatter_dimension=1, tiled=True
    )

    scaled = ffn_in_grad * norm2_gain
    resid_grad = cot_own.astype(f32) + row_scale * (
        scaled - resid * row_scale * row_scale * jnp.mean(scaled * resid, axis=-1, keepdims=True)
    )
    norm2_part = jnp.sum(ffn_in_grad * resid * row_scale, axis=0)
    mixer_parts = gather_chips(resid_grad.astype(bf16), bits, size)
    mixer_grad = jnp.concatenate(mixer_parts)

    inner_late = after(inner, *mixer_parts)
    output = resid + scatter_chips(
        lambda at: mm(chunk(inner_late, at), down_rows, NN).astype(bf16), bits, size
    )
    output = from_row(output.astype(bf16))

    gated_grad = mm(mixer_grad, out_weights, NT)
    proj_grad, floor_grad, gain_grad = recurrence_back(
        info, proj, floor_row, gain_row, seg, mixed, gated_grad, states, scores, half_heads, size
    )
    normed_grad = scatter_chips(
        lambda at: mm(chunk(proj_grad, at), proj_weights, NT).astype(bf16), bits, size
    )
    scaled_in = normed_grad * norm1_gain
    input_grad = resid_grad + input_scale * (
        scaled_in
        - own_rows
        * input_scale
        * input_scale
        * jnp.mean(scaled_in * own_rows, axis=-1, keepdims=True)
    )
    norm1_part = jnp.sum(normed_grad * own_rows * input_scale, axis=0)
    input_grad = from_row(input_grad)

    out_grad = pair_grad(gated, mixer_grad, half_width)
    proj_w_grad = mm(normed, proj_grad[:, 2 * width :], TN).astype(bf16)
    proj_w_grad = mm(normed, proj_grad[:, : 2 * width], TN) + swap(proj_w_grad, 1, size).astype(f32)
    proj_w_grad = lax.psum_scatter(
        proj_w_grad.astype(bf16), "dp", scatter_dimension=0, tiled=True
    ).astype(f32)
    out_grad = lax.psum_scatter(out_grad, "dp", scatter_dimension=1, tiled=True)

    vector_grads = jnp.concatenate((gain_grad, floor_grad))
    vector_grads = vector_grads[:, :half_width] + swap(vector_grads[:, half_width:], 1, size)
    moved = [
        lax.ppermute(vector_grads, "dp", [(at, (at + slot) % depth) for at in range(depth)])
        for slot in range(1, depth)
    ]
    vector_grads = sum(moved, vector_grads)
    vector_len = half_width // depth
    vector_grads = lax.dynamic_slice_in_dim(vector_grads, place * vector_len, vector_len, 1)
    norm_grads = jnp.stack((norm1_part, norm2_part))
    for bit in [1] + bits:
        norm_grads = norm_grads + swap(norm_grads, bit, size)
    moved = [
        lax.ppermute(norm_grads, "dp", [(at, (at + slot) % depth) for at in range(depth)])
        for slot in range(1, depth)
    ]
    stacked = jnp.stack([norm_grads] + moved)
    order = (place - jnp.arange(depth)) % depth
    norm_grads = jnp.sum(jnp.zeros_like(stacked).at[order].set(stacked), axis=0)

    return (
        output,
        input_grad,
        proj_w_grad[:, 0:half_width],
        proj_w_grad[:, half_width : 2 * half_width],
        proj_w_grad[:, 2 * half_width : 3 * half_width],
        proj_w_grad[:, 3 * half_width : 4 * half_width],
        out_grad.astype(f32),
        vector_grads[0],
        vector_grads[1],
        norm_grads[0],
        norm_grads[1],
        gate_up_grad[0].astype(f32).T,
        gate_up_grad[1].astype(f32).T,
        ffn_down_grad.astype(f32).T,
    )


def solution(mesh):
    placed = (
        P("dp", "head", None),
        P("dp", None),
        P(),
        P(None, "head"),
        P(None, "head"),
        P(None, "head"),
        P(None, "head"),
        P("head"),
        P("head"),
        P("head", None),
        P(),
        P(None, ("head", "dp")),
        P(None, ("head", "dp")),
        P(None, ("head", "dp")),
        P("dp", "head", None),
    )
    return jax.shard_map(
        functools.partial(per_device, mesh.shape["head"], mesh.shape["dp"]),
        mesh=mesh,
        in_specs=placed,
        out_specs=(
            P("dp", "head", None),
            P("dp", "head", None),
            P("dp", "head"),
            P("dp", "head"),
            P("dp", "head"),
            P("dp", "head"),
            P("head", "dp"),
            P(("head", "dp")),
            P(("head", "dp")),
            P(),
            P(),
            P(None, ("head", "dp")),
            P(None, ("head", "dp")),
            P(None, ("head", "dp")),
        ),
        check_vma=False,
    )
```

time: 1350 us -> 657 us (0.49)
  waiting for transfers between devices: 783 us -> 289 us
  matrix products: 304 us -> 162 us
  local copies, waits for them, and re-layouts: 125 us -> 49.5 us
  starting transfers between devices: 1.05 us -> 61.2 us
  blocking collectives: 51.5 us -> 0 us
  Pallas kernels: 0 us -> 33 us
  other arithmetic: 60.6 us -> 38.7 us
    reduce_scatter x12 -> x4, waiting for transfers between devices: 496 us -> 69 us  [the longest x1 69 us: per_device(): lax.psum_scatter(proj_w_grad.astype(bf16), 'dp', scatter_dimension=0, til...]
    all_gather x7 -> x2, waiting for transfers between devices: 282 us -> 6.68 us  [the longest x1 6.68 us: per_device(): lax.all_gather(jnp.stack((ffn_gate.T, ffn_up.T)), 'dp', axis=1, tiled=True)]
    ppermute x0 -> x64, waiting for transfers between devices: none -> 214 us  [the longest x58 210 us: swap(): return lax.ppermute(tensor, 'head', [(at, at ^ bit) for at in range(size)])]
    dot_general x159 -> x35, matrix products: 304 us -> 162 us  [mm(): lax.dot_general(left, right, (dims, ((), ())), preferred_element_type=out)]
    ppermute x0 -> x64, starting transfers between devices: none -> 60.8 us  [the longest x58 51.3 us: swap(): return lax.ppermute(tensor, 'head', [(at, at ^ bit) for at in range(size)])]
    psum x1 -> x0, blocking collectives: 39.8 us -> none  [per_device(): lax.psum((norm1_part, norm2_part), ('head', 'dp'))]
    squeeze x40 -> x3, local copies, waits for them, and re-layouts: 38.3 us -> 3.46 us  [the longest x2 2.94 us: pick(): return lax.dynamic_index_in_dim(tensor, at, 0, keepdims=False)]
    pallas_call x0 -> x2, Pallas kernels: none -> 33 us  [the longest x1 16.8 us: recurrence_back(): pl.pallas_call(functools.partial(backward_kernel, blocks, half_heads), ou...]
  transfers between devices with their start and end apart: 19 -> 70, of which waited for: 15 -> 30; matrix products, arithmetic and copies ran while one was open for 22% -> 30% of each run, Pallas kernels for 0% -> 5%
where the time goes in v1:
time: 657 us; the launch traced here: 649 us
  waiting for transfers between devices  289 us (44%)
  matrix products  162 us (25%)
  starting transfers between devices  61.2 us (9%)
  local copies, waits for them, and re-layouts  49.5 us (8%)
  other arithmetic  38.7 us (6%)
  Pallas kernels  33 us (5%)
  between operations  15.8 us (2%)
    ppermute x58, waiting for transfers between devices, swap(): return lax.ppermute(tensor, 'head', [(at, at ^ bit) for at in range(size)])  210 us
    dot_general x35, matrix products, mm(): lax.dot_general(left, right, (dims, ((), ())), preferred_element_type=out)  162 us
    reduce_scatter x1, waiting for transfers between devices, per_device(): lax.psum_scatter(proj_w_grad.astype(bf16), 'dp', scatter_dimension=0, til...  69 us
    ppermute x58, starting transfers between devices, swap(): return lax.ppermute(tensor, 'head', [(at, at ^ bit) for at in range(size)])  51.3 us
    unnamed x151, local copies, waits for them, and re-layouts  23.3 us
    pallas_call x1, Pallas kernels, recurrence_back(): pl.pallas_call(functools.partial(backward_kernel, blocks, half_heads), ou...  16.8 us
    pallas_call x1, Pallas kernels, recurrence(): pl.pallas_call(functools.partial(forward_kernel, blocks, half_heads), out...  16.2 us
  transfers between devices with their start and end apart: 70, of which 30 were waited for; matrix products, arithmetic and copies ran while one was open for 30% of the time, Pallas kernels for 5%

profile of v1, /device:TPU:0, one launch (start us, length us, event | category | flops | bytes accessed | tf_op | source)
XLA Modules:
  0.0 649.3 jit_solution(18169936507836388188)
XLA Ops:
  9.9 3.9 pad_maximum_fusion.1
  31.5 20.4 %collective-permute-done.1 = bf16[256,2048]{1,0:T(8,128)(2,1)S(1)} collective-permute-done((bf16[256,2048]{1,0:T(8,128)(2,1)S(1)}, bf16[256,2048]{1,0:T(8,128)(2,1)S(1)}, u32[]{:S(2)}, u32[]{:S(2)}) %collective-permute-start.1) | collective-permute-done | bytes 1048608 | tf_op jit(solution)/shard_map/ppermute | solution.py:17
  56.9 8.9 %collective-permute-done.3 = bf16[128,2048]{1,0:T(8,128)(2,1)S(1)} collective-permute-done((bf16[128,2048]{1,0:T(8,128)(2,1)S(1)}, bf16[128,2048]{1,0:T(8,128)(2,1)S(1)}, u32[]{:S(2)}, u32[]{:S(2)}) %collective-permute-start.3) | collective-permute-done | bytes 524320 | tf_op jit(solution)/shard_map/ppermute | solution.py:17
  68.6 4.1 constant_dynamic-update-slice_fusion.5
  72.7 8.9 %fusion.91.proj_ref = f32[1024,2048]{1,0:T(8,128)S(1)} fusion(bf16[1024,2048]{1,0:T(8,128)(2,1)S(1)} %constant_dynamic-update-slice_fusion, bf16[2048,2048]{1,0:T(8,128)(2,1)S(1)} %constant_dynamic-update-slice_fusion.5), kind=kOutput, calls=%fused_computation.226 | convolution fusion | flops 8589934592 | bytes 20971520 | tf_op jit(solution)/shard_map/dot_general | solution.py:21
  81.6 16.2 %shard_map.254 = (bf16[1024,512]{1,0:T(8,128)(2,1)S(1)}, f32[1024,512]{1,0:T(8,128)S(1)}, f32[8,4,128,128]{3,2,1,0:T(8,128)S(1)}, bf16[8,4,128,128]{3,2,1,0:T(8,128)(2,1)S(1)}) custom-call(s32[17]{0:T(128)S(1)} %pad_add_fusion.info, f32[1024,2048]{1,0:T(8,128)S(1)} %fusion.91.proj_ref, f32[1,512]{1,0:T(1,128)S(1)} %get-tuple-element.89.floor_ref, ...), custom_call_target="tpu_custom_call" | custom-call | flops 1073741824 | bytes 16777216 | tf_op jit(solution)/shard_map/pallas_call | solution.py:230
  106.0 7.7 %collective-permute-done.11 = bf16[128,2048]{1,0:T(8,128)(2,1)S(1)} collective-permute-done((bf16[128,2048]{1,0:T(8,128)(2,1)S(1)}, bf16[128,2048]{1,0:T(8,128)(2,1)S(1)}, u32[]{:S(2)}, u32[]{:S(2)}) %collective-permute-start.11) | collective-permute-done | bytes 524320 | tf_op jit(solution)/shard_map/ppermute | solution.py:17
  118.5 6.7 %all-gather.3.cloned.1.call-done = bf16[2,704,2048]{2,1,0:T(8,128)(2,1)} async-done(((bf16[2,176,2048]{2,1,0:T(8,128)(2,1)}), bf16[2,704,2048]{2,1,0:T(8,128)(2,1)}) %all-gather.3.cloned.1.call-update) | async-done | bytes 5767184 | tf_op jit(solution)/shard_map/all_gather | solution.py:354
  125.2 3.7 fusion.22
  129.5 5.0 collective-permute-done.12
  143.5 21.0 %collective-permute-done.14 = bf16[256,2048]{1,0:T(8,128)(2,1)S(1)} collective-permute-done((bf16[256,2048]{1,0:T(8,128)(2,1)S(1)}, bf16[256,2048]{1,0:T(8,128)(2,1)S(1)}, u32[]{:S(2)}, u32[]{:S(2)}) %collective-permute-start.14) | collective-permute-done | bytes 1048608 | tf_op jit(solution)/shard_map/ppermute | solution.py:17
  167.2 19.8 %collective-permute-done.20 = bf16[256,2048]{1,0:T(8,128)(2,1)S(1)} collective-permute-done((bf16[256,2048]{1,0:T(8,128)(2,1)S(1)}, bf16[256,2048]{1,0:T(8,128)(2,1)S(1)}, u32[]{:S(2)}, u32[]{:S(2)}) %collective-permute-start.20) | collective-permute-done | bytes 1048608 | tf_op jit(solution)/shard_map/ppermute | solution.py:17
  189.2 6.8 %collective-permute-done.16 = bf16[128,2048]{1,0:T(8,128)(2,1)S(1)} collective-permute-done((bf16[128,2048]{1,0:T(8,128)(2,1)S(1)}, bf16[128,2048]{1,0:T(8,128)(2,1)S(1)}, u32[]{:S(2)}, u32[]{:S(2)}) %collective-permute-start.16) | collective-permute-done | bytes 524320 | tf_op jit(solution)/shard_map/ppermute | solution.py:17
  199.0 7.2 %collective-permute-done.22 = bf16[128,2048]{1,0:T(8,128)(2,1)S(1)} collective-permute-done((bf16[128,2048]{1,0:T(8,128)(2,1)S(1)}, bf16[128,2048]{1,0:T(8,128)(2,1)S(1)}, u32[]{:S(2)}, u32[]{:S(2)}) %collective-permute-start.22) | collective-permute-done | bytes 524320 | tf_op jit(solution)/shard_map/ppermute | solution.py:17
  208.3 3.3 constant_dynamic-update-slice_fusion.18
  213.6 3.1 constant_dynamic-update-slice_fusion.17
  216.7 12.8 %fusion.9 = f32[1024,1408]{1,0:T(8,128)} fusion(bf16[1024,2048]{1,0:T(8,128)(2,1)} %copy-done.38, bf16[2,1408,2048]{2,1,0:T(8,128)(2,1)S(1)} %constant_dynamic-update-slice_fusion.17), kind=kOutput, calls=%fused_computation.31 | convolution fusion | flops 5905580032 | bytes 15728640 | tf_op jit(solution)/shard_map/dot_general | solution.py:21
  232.2 10.3 %fusion.92 = f32[1024,1408]{1,0:T(8,128)} fusion(bf16[1024,2048]{1,0:T(8,128)(2,1)} %constant_dynamic-update-slice_fusion.19, bf16[1408,2048]{1,0:T(8,128)(2,1)S(1)} %constant_dynamic-update-slice_fusion.25), kind=kOutput, calls=%fused_computation.227 | convolution fusion | flops 5905580032 | bytes 15728640 | tf_op jit(solution)/shard_map/dot_general | solution.py:21
  242.5 15.3 %multiply_convert_fusion.1 = (bf16[1024,1408]{1,0:T(8,128)(2,1)}, bf16[1024,1408]{1,0:T(8,128)(2,1)S(1)}, bf16[1024,1408]{1,0:T(8,128)(2,1)}) fusion(f32[1024,1408]{1,0:T(8,128)} %fusion.92, f32[1024,1408]{1,0:T(8,128)} %fusion.9, bf16[1024,2048]{1,0:T(8,128)(2,1)S(1)} %copy-done.39, bf16[2,1408,2048]{2,1,0:T(8,128)(2,1)} %copy-done.25), kind=kOutput, calls=%fused_computation.9 | convolution fusion | flops 5928648704 | bytes 30146560 | tf_op jit(solution)/shard_map/dot_general | solution.py:21
  257.8 5.7 fusion.7
  263.6 4.9 fusion.5
  282.2 8.7 %collective-permute-done.28 = bf16[128,2048]{1,0:T(8,128)(2,1)S(1)} collective-permute-done((bf16[128,2048]{1,0:T(8,128)(2,1)S(1)}, bf16[128,2048]{1,0:T(8,128)(2,1)S(1)}, u32[]{:S(2)}, u32[]{:S(2)}) %collective-permute-start.28) | collective-permute-done | bytes 524320 | tf_op jit(solution)/shard_map/ppermute | solution.py:17
  292.2 11.1 %collective-permute-done.26 = bf16[128,2048]{1,0:T(8,128)(2,1)S(1)} collective-permute-done((bf16[128,2048]{1,0:T(8,128)(2,1)S(1)}, bf16[128,2048]{1,0:T(8,128)(2,1)S(1)}, u32[]{:S(2)}, u32[]{:S(2)}) %collective-permute-start.26) | collective-permute-done | bytes 524320 | tf_op jit(solution)/shard_map/ppermute | solution.py:17
  306.4 7.1 %collective-permute-done.29 = bf16[128,2048]{1,0:T(8,128)(2,1)S(1)} collective-permute-done((bf16[128,2048]{1,0:T(8,128)(2,1)S(1)}, bf16[128,2048]{1,0:T(8,128)(2,1)S(1)}, u32[]{:S(2)}, u32[]{:S(2)}) %collective-permute-start.29) | collective-permute-done | bytes 524320 | tf_op jit(solution)/shard_map/ppermute | solution.py:17
  321.0 20.2 %collective-permute-done.31 = bf16[256,2048]{1,0:T(8,128)(2,1)S(1)} collective-permute-done((bf16[256,2048]{1,0:T(8,128)(2,1)S(1)}, bf16[256,2048]{1,0:T(8,128)(2,1)S(1)}, u32[]{:S(2)}, u32[]{:S(2)}) %collective-permute-start.31) | collective-permute-done | bytes 1048608 | tf_op jit(solution)/shard_map/ppermute | solution.py:17
  342.2 7.2 %convolution_convert_fusion.1 = bf16[704,2048]{1,0:T(8,128)(2,1)} fusion(bf16[1024,2048]{1,0:T(8,128)(2,1)} %constant_dynamic-update-slice_fusion.19, bf16[1024,1408]{1,0:T(8,128)(2,1)S(1)} %get-tuple-element.32), kind=kOutput, calls=%fused_computation.19 | convolution fusion | flops 2954231808 | bytes 8650752 | tf_op jit(solution)/shard_map/dot_general | solution.py:21
  353.2 10.7 %collective-permute-done.34 = bf16[128,2048]{1,0:T(8,128)(2,1)S(1)} collective-permute-done((bf16[128,2048]{1,0:T(8,128)(2,1)S(1)}, bf16[128,2048]{1,0:T(8,128)(2,1)S(1)}, u32[]{:S(2)}, u32[]{:S(2)}) %collective-permute-start.34) | collective-permute-done | bytes 524320 | tf_op jit(solution)/shard_map/ppermute | solution.py:17
  370.3 8.4 %add_convert_fusion.1 = bf16[704,2048]{1,0:T(8,128)(2,1)} fusion(bf16[704,2048]{1,0:T(8,128)(2,1)} %collective-permute-done.63, bf16[1024,2048]{1,0:T(8,128)(2,1)} %constant_dynamic-update-slice_fusion.19, bf16[1024,1408]{1,0:T(8,128)(2,1)} %copy-done.33), kind=kOutput, calls=%fused_computation.5 | convolution fusion | flops 2957115392 | bytes 11534336 | tf_op jit(solution)/shard_map/dot_general | solution.py:21
  378.9 6.2 convolution_convert_fusion.3
  385.4 3.8 convolution_convert_fusion.2
  390.5 3.5 fusion.10
  394.7 3.5 fusion.11
  401.2 5.4 fusion.93.grad_ref
  407.7 16.8 %shard_map.255 = (bf16[1024,2048]{1,0:T(8,128)(2,1)S(1)}, f32[1,512]{1,0:T(1,128)S(1)}, f32[1,512]{1,0:T(1,128)S(1)}) custom-call(s32[17]{0:T(128)S(1)} %pad_add_fusion.info, f32[1024,2048]{1,0:T(8,128)S(1)} %bitcast.126, f32[1,512]{1,0:T(1,128)S(1)} %get-tuple-element.89.floor_ref, f32[1,512]{1,0:T(1,128)S(1)} %get-tuple-element.88.gain_ref, ...), custom_call_target="tpu_custom_call" | custom-call | flops 2147483648 | bytes 25165824 | tf_op jit(solution)/shard_map/pallas_call | solution.py:269
  424.9 6.7 %convolution_convert_fusion = bf16[2048,1024]{1,0:T(8,128)(2,1)} fusion(bf16[1024,2048]{1,0:T(8,128)(2,1)S(1)} %copy-done.43, bf16[1024,2048]{1,0:T(8,128)(2,1)S(1)} %get-tuple-element.36), kind=kOutput, calls=%fused_computation.18 | convolution fusion | flops 4297064448 | bytes 10485760 | tf_op jit(solution)/shard_map/dot_general | solution.py:21
  439.3 5.7 convolution_convert_fusion.11
  445.1 5.8 convolution_convert_fusion.9
  450.9 5.7 convolution_convert_fusion.10
  456.7 7.6 %fusion.23 = f32[256,2048]{1,0:T(8,128)} fusion(bf16[2048,2048]{1,0:T(8,128)(2,1)} %copy-done.44, bf16[1024,2048]{1,0:T(8,128)(2,1)S(1)} %get-tuple-element.36), kind=kOutput, calls=%fused_computation.55 | convolution fusion | flops 2148532224 | bytes 11534336 | tf_op jit(solution)/shard_map/dot_general | solution.py:21
  482.7 6.4 add_convert_fusion
  489.2 13.5 %collective-permute-done.43 = bf16[128,2048]{1,0:T(8,128)(2,1)} collective-permute-done((bf16[128,2048]{1,0:T(8,128)(2,1)}, bf16[128,2048]{1,0:T(8,128)(2,1)}, u32[]{:S(2)}, u32[]{:S(2)}) %collective-permute-start.43) | collective-permute-done | bytes 524320 | tf_op jit(solution)/shard_map/ppermute | solution.py:17
  507.1 6.8 %collective-permute-done.36 = bf16[128,2048]{1,0:T(8,128)(2,1)} collective-permute-done((bf16[128,2048]{1,0:T(8,128)(2,1)}, bf16[128,2048]{1,0:T(8,128)(2,1)}, u32[]{:S(2)}, u32[]{:S(2)}) %collective-permute-start.36) | collective-permute-done | bytes 524320 | tf_op jit(solution)/shard_map/ppermute | solution.py:17
  518.2 6.9 %collective-permute-done.46 = bf16[128,2048]{1,0:T(8,128)(2,1)S(1)} collective-permute-done((bf16[128,2048]{1,0:T(8,128)(2,1)}, bf16[128,2048]{1,0:T(8,128)(2,1)S(1)}, u32[]{:S(2)}, u32[]{:S(2)}) %collective-permute-start.46) | collective-permute-done | bytes 524320 | tf_op jit(solution)/shard_map/ppermute | solution.py:17
  530.8 5.5 collective-permute-done.35
  536.9 9.0 %collective-permute-done.39 = bf16[128,2048]{1,0:T(8,128)(2,1)S(1)} collective-permute-done((bf16[128,2048]{1,0:T(8,128)(2,1)S(1)}, bf16[128,2048]{1,0:T(8,128)(2,1)S(1)}, u32[]{:S(2)}, u32[]{:S(2)}) %collective-permute-start.39) | collective-permute-done | bytes 524320 | tf_op jit(solution)/shard_map/ppermute | solution.py:17
  560.2 3.1 maximum_select_fusion
  567.5 3.3 convert_bitcast_fusion
  570.8 69.0 %reduce-scatter.5.cloned.1.call-done = bf16[512,1024]{1,0:T(8,128)(2,1)} async-done(((bf16[2048,1024]{1,0:T(8,128)(2,1)}), bf16[512,1024]{1,0:T(8,128)(2,1)}) %reduce-scatter.5.cloned.1.call-update) | async-done | bytes 1048592 | tf_op jit(solution)/shard_map/reduce_scatter | solution.py:462
  (384 shorter events, 170.1 us)
Async XLA Ops:
  7.2 117.9 %all-gather.3.cloned.1.call-start = ((), (), s32[]{:S(2)}) async-start(), calls=%async_computation.4 | async-start | bytes 7208960 | tf_op jit(solution)/shard_map/all_gather | solution.py:354
  9.4 15.6 %collective-permute-start = (bf16[128,2048]{1,0:T(8,128)(2,1)}, bf16[128,2048]{1,0:T(8,128)(2,1)S(1)}, u32[]{:S(2)}, u32[]{:S(2)}) collective-permute-start(bf16[128,2048]{1,0:T(8,128)(2,1)} %get-tuple-element.85), channel_id=1, source_target_pairs={{0,4},{4,0},{8,12},{12,8},{16,20},{20,16},{24,28},{28,24},{1,5},{5... | collective-permute-start | bytes 1572872 | tf_op jit(solution)/shard_map/ppermute | solution.py:17
  13.8 54.8 %collective-permute-start.5 = (bf16[2048,1024]{1,0:T(8,128)(2,1)}, bf16[2048,1024]{1,0:T(8,128)(2,1)}, u32[]{:S(2)}, u32[]{:S(2)}) collective-permute-start(bf16[2048,1024]{1,0:T(8,128)(2,1)} %pad_maximum_fusion.1), channel_id=1, source_target_pairs={{0,4},{4,0},{8,12},{12,8},{16,20},{20,16},{24,28},{28,24},{1,5},{5... | collective-permute-start | bytes 12582920 | tf_op jit(solution)/shard_map/ppermute | solution.py:17
  14.0 17.5 %collective-permute-start.6 = (f32[2,256]{1,0:T(2,128)S(1)}, f32[2,256]{1,0:T(2,128)S(1)}, u32[]{:S(2)}, u32[]{:S(2)}) collective-permute-start(f32[2,256]{1,0:T(2,128)S(1)} %pad_maximum_fusion.11), channel_id=1, source_target_pairs={{0,4},{4,0},{8,12},{12,8},{16,20},{20,16},{24,28},{28,24},{1,5},{5... | collective-permute-start | bytes 6152 | tf_op jit(solution)/shard_map/ppermute | solution.py:17
  14.4 39.5 %collective-permute-start.7 = (bf16[256,2048]{1,0:T(8,128)(2,1)}, bf16[256,2048]{1,0:T(8,128)(2,1)}, u32[]{:S(2)}, u32[]{:S(2)}) collective-permute-start(bf16[256,2048]{1,0:T(8,128)(2,1)} %param.24), channel_id=1, source_target_pairs={{0,4},{4,0},{8,12},{12,8},{16,20},{20,16},{24,28},{28,24},{1,5},{5... | collective-permute-start | bytes 3145736 | tf_op jit(solution)/shard_map/ppermute | solution.py:17
  15.9 192.4 %all-gather.5.cloned.1.call-start = ((), (), s32[]{:S(2)}) async-start(), calls=%async_computation.5 | async-start | bytes 3604480 | tf_op jit(solution)/shard_map/all_gather | solution.py:355
  25.6 26.3 %collective-permute-start.1 = (bf16[256,2048]{1,0:T(8,128)(2,1)S(1)}, bf16[256,2048]{1,0:T(8,128)(2,1)S(1)}, u32[]{:S(2)}, u32[]{:S(2)}) collective-permute-start(bf16[256,2048]{1,0:T(8,128)(2,1)S(1)} %get-tuple-element.54), channel_id=1, source_target_pairs={{0,8},{4,12},{8,0},{12,4},{16,24},{20,28},{24,16},{28,20},{1,9},{5... | collective-permute-start | bytes 3145736 | tf_op jit(solution)/shard_map/ppermute | solution.py:17
  28.6 26.6 %collective-permute-start.2 = (bf16[256,2048]{1,0:T(8,128)(2,1)S(1)}, bf16[256,2048]{1,0:T(8,128)(2,1)S(1)}, u32[]{:S(2)}, u32[]{:S(2)}) collective-permute-start(bf16[256,2048]{1,0:T(8,128)(2,1)S(1)} %get-tuple-element.54), channel_id=1, source_target_pairs={{0,16},{4,20},{8,24},{12,28},{16,0},{20,4},{24,8},{28,12},{1,17},{... | collective-permute-start | bytes 3145736 | tf_op jit(solution)/shard_map/ppermute | solution.py:17
  98.7 14.9 %collective-permute-start.11 = (bf16[128,2048]{1,0:T(8,128)(2,1)S(1)}, bf16[128,2048]{1,0:T(8,128)(2,1)S(1)}, u32[]{:S(2)}, u32[]{:S(2)}) collective-permute-start(bf16[128,2048]{1,0:T(8,128)(2,1)S(1)} %get-tuple-element.83), channel_id=1, source_target_pairs={{0,16},{4,20},{8,24},{12,28},{16,0},{20,4},{24,8},{28,12},{1,17},{... | collective-permute-start | bytes 1572872 | tf_op jit(solution)/shard_map/ppermute | solution.py:17
  99.5 16.5 %collective-permute-start.9 = (bf16[128,2048]{1,0:T(8,128)(2,1)S(1)}, bf16[128,2048]{1,0:T(8,128)(2,1)S(1)}, u32[]{:S(2)}, u32[]{:S(2)}) collective-permute-start(bf16[128,2048]{1,0:T(8,128)(2,1)S(1)} %get-tuple-element.82), channel_id=1, source_target_pairs={{0,8},{4,12},{8,0},{12,4},{16,24},{20,28},{24,16},{28,20},{1,9},{5... | collective-permute-start | bytes 1572872 | tf_op jit(solution)/shard_map/ppermute | solution.py:17
  103.2 25.8 %collective-permute-start.8 = (bf16[128,2048]{1,0:T(8,128)(2,1)}, bf16[128,2048]{1,0:T(8,128)(2,1)}, u32[]{:S(2)}, u32[]{:S(2)}) collective-permute-start(bf16[128,2048]{1,0:T(8,128)(2,1)} %slice.388), channel_id=1, source_target_pairs={{0,8},{4,12},{8,0},{12,4},{16,24},{20,28},{24,16},{28,20},{1,9},{5... | collective-permute-start | bytes 1572872 | tf_op jit(solution)/shard_map/ppermute | solution.py:17
  104.7 24.9 %collective-permute-start.13 = (bf16[128,2048]{1,0:T(8,128)(2,1)}, bf16[128,2048]{1,0:T(8,128)(2,1)}, u32[]{:S(2)}, u32[]{:S(2)}) collective-permute-start(bf16[128,2048]{1,0:T(8,128)(2,1)} %slice.394), channel_id=1, source_target_pairs={{0,16},{4,20},{8,24},{12,28},{16,0},{20,4},{24,8},{28,12},{1,17},{... | collective-permute-start | bytes 1572872 | tf_op jit(solution)/shard_map/ppermute | solution.py:17
  114.6 19.9 %collective-permute-start.12 = (bf16[128,2048]{1,0:T(8,128)(2,1)}, bf16[128,2048]{1,0:T(8,128)(2,1)}, u32[]{:S(2)}, u32[]{:S(2)}) collective-permute-start(bf16[128,2048]{1,0:T(8,128)(2,1)} %add_convert_fusion.10), channel_id=1, source_target_pairs={{0,8},{4,12},{8,0},{12,4},{16,24},{20,28},{24,16},{28,20},{1,9},{5... | collective-permute-start | bytes 1572872 | tf_op jit(solution)/shard_map/ppermute | solution.py:17
  117.0 17.5 %collective-permute-start.10 = (bf16[128,2048]{1,0:T(8,128)(2,1)}, bf16[128,2048]{1,0:T(8,128)(2,1)}, u32[]{:S(2)}, u32[]{:S(2)}) collective-permute-start(bf16[128,2048]{1,0:T(8,128)(2,1)} %add_convert_fusion.11), channel_id=1, source_target_pairs={{0,16},{4,20},{8,24},{12,28},{16,0},{20,4},{24,8},{28,12},{1,17},{... | collective-permute-start | bytes 1572872 | tf_op jit(solution)/shard_map/ppermute | solution.py:17
  125.1 88.4 %collective-permute-start.18 = (bf16[2,704,2048]{2,1,0:T(8,128)(2,1)}, bf16[2,704,2048]{2,1,0:T(8,128)(2,1)}, u32[]{:S(2)}, u32[]{:S(2)}) collective-permute-start(bf16[2,704,2048]{2,1,0:T(8,128)(2,1)} %all-gather.3.cloned.1.call-done), channel_id=1, source_target_pairs={{0,4},{4,0},{8,12},{12,8},{16,20},{20,16},{24,28},{28,24},{1,5},{5... | collective-permute-start | bytes 17301512 | tf_op jit(solution)/shard_map/ppermute | solution.py:17
  128.9 434.4 %reduce-scatter.7.cloned.1.call-start = ((), (), s32[]{:S(2)}) async-start(), calls=%async_computation.7 | async-start | bytes 1310720 | tf_op jit(solution)/shard_map/reduce_scatter | solution.py:465
  138.3 26.2 %collective-permute-start.14 = (bf16[256,2048]{1,0:T(8,128)(2,1)S(1)}, bf16[256,2048]{1,0:T(8,128)(2,1)S(1)}, u32[]{:S(2)}, u32[]{:S(2)}) collective-permute-start(bf16[256,2048]{1,0:T(8,128)(2,1)S(1)} %get-tuple-element.50), channel_id=1, source_target_pairs={{0,8},{4,12},{8,0},{12,4},{16,24},{20,28},{24,16},{28,20},{1,9},{5... | collective-permute-start | bytes 3145736 | tf_op jit(solution)/shard_map/ppermute | solution.py:17
  139.4 26.2 %collective-permute-start.15 = (bf16[256,2048]{1,0:T(8,128)(2,1)S(1)}, bf16[256,2048]{1,0:T(8,128)(2,1)S(1)}, u32[]{:S(2)}, u32[]{:S(2)}) collective-permute-start(bf16[256,2048]{1,0:T(8,128)(2,1)S(1)} %get-tuple-element.50), channel_id=1, source_target_pairs={{0,16},{4,20},{8,24},{12,28},{16,0},{20,4},{24,8},{28,12},{1,17},{... | collective-permute-start | bytes 3145736 | tf_op jit(solution)/shard_map/ppermute | solution.py:17
  141.0 45.9 %collective-permute-start.20 = (bf16[256,2048]{1,0:T(8,128)(2,1)S(1)}, bf16[256,2048]{1,0:T(8,128)(2,1)S(1)}, u32[]{:S(2)}, u32[]{:S(2)}) collective-permute-start(bf16[256,2048]{1,0:T(8,128)(2,1)S(1)} %pad_maximum_fusion.6), channel_id=1, source_target_pairs={{0,8},{4,12},{8,0},{12,4},{16,24},{20,28},{24,16},{28,20},{1,9},{5... | collective-permute-start | bytes 3145736 | tf_op jit(solution)/shard_map/ppermute | solution.py:17
  141.6 46.5 %collective-permute-start.21 = (bf16[256,2048]{1,0:T(8,128)(2,1)S(1)}, bf16[256,2048]{1,0:T(8,128)(2,1)S(1)}, u32[]{:S(2)}, u32[]{:S(2)}) collective-permute-start(bf16[256,2048]{1,0:T(8,128)(2,1)S(1)} %pad_maximum_fusion.6), channel_id=1, source_target_pairs={{0,16},{4,20},{8,24},{12,28},{16,0},{20,4},{24,8},{28,12},{1,17},{... | collective-permute-start | bytes 3145736 | tf_op jit(solution)/shard_map/ppermute | solution.py:17
  164.5 31.5 %collective-permute-start.16 = (bf16[128,2048]{1,0:T(8,128)(2,1)S(1)}, bf16[128,2048]{1,0:T(8,128)(2,1)S(1)}, u32[]{:S(2)}, u32[]{:S(2)}) collective-permute-start(bf16[128,2048]{1,0:T(8,128)(2,1)S(1)} %slice.395), channel_id=1, source_target_pairs={{0,16},{4,20},{8,24},{12,28},{16,0},{20,4},{24,8},{28,12},{1,17},{... | collective-permute-start | bytes 1572872 | tf_op jit(solution)/shard_map/ppermute | solution.py:17
  165.7 30.4 %collective-permute-start.17 = (bf16[128,2048]{1,0:T(8,128)(2,1)S(1)}, bf16[128,2048]{1,0:T(8,128)(2,1)S(1)}, u32[]{:S(2)}, u32[]{:S(2)}) collective-permute-start(bf16[128,2048]{1,0:T(8,128)(2,1)S(1)} %slice.396), channel_id=1, source_target_pairs={{0,8},{4,12},{8,0},{12,4},{16,24},{20,28},{24,16},{28,20},{1,9},{5... | collective-permute-start | bytes 1572872 | tf_op jit(solution)/shard_map/ppermute | solution.py:17
  208.3 21.2 %collective-permute-start.24 = (bf16[704,2048]{1,0:T(8,128)(2,1)}, bf16[704,2048]{1,0:T(8,128)(2,1)S(1)}, u32[]{:S(2)}, u32[]{:S(2)}) collective-permute-start(bf16[704,2048]{1,0:T(8,128)(2,1)} %all-gather.5.cloned.1.call-done), channel_id=1, source_target_pairs={{0,4},{4,0},{8,12},{12,8},{16,20},{20,16},{24,28},{28,24},{1,5},{5... | collective-permute-start | bytes 8650760 | tf_op jit(solution)/shard_map/ppermute | solution.py:17
  276.1 14.8 %collective-permute-start.28 = (bf16[128,2048]{1,0:T(8,128)(2,1)S(1)}, bf16[128,2048]{1,0:T(8,128)(2,1)S(1)}, u32[]{:S(2)}, u32[]{:S(2)}) collective-permute-start(bf16[128,2048]{1,0:T(8,128)(2,1)S(1)} %get-tuple-element.81), channel_id=1, source_target_pairs={{0,16},{4,20},{8,24},{12,28},{16,0},{20,4},{24,8},{28,12},{1,17},{... | collective-permute-start | bytes 1572872 | tf_op jit(solution)/shard_map/ppermute | solution.py:17
  277.3 29.1 %collective-permute-start.25 = (bf16[128,2048]{1,0:T(8,128)(2,1)S(1)}, bf16[128,2048]{1,0:T(8,128)(2,1)S(1)}, u32[]{:S(2)}, u32[]{:S(2)}) collective-permute-start(bf16[128,2048]{1,0:T(8,128)(2,1)S(1)} %slice.404), channel_id=1, source_target_pairs={{0,8},{4,12},{8,0},{12,4},{16,24},{20,28},{24,16},{28,20},{1,9},{5... | collective-permute-start | bytes 1572872 | tf_op jit(solution)/shard_map/ppermute | solution.py:17
  278.4 25.0 %collective-permute-start.26 = (bf16[128,2048]{1,0:T(8,128)(2,1)S(1)}, bf16[128,2048]{1,0:T(8,128)(2,1)S(1)}, u32[]{:S(2)}, u32[]{:S(2)}) collective-permute-start(bf16[128,2048]{1,0:T(8,128)(2,1)S(1)} %get-tuple-element.80), channel_id=1, source_target_pairs={{0,8},{4,12},{8,0},{12,4},{16,24},{20,28},{24,16},{28,20},{1,9},{5... | collective-permute-start | bytes 1572872 | tf_op jit(solution)/shard_map/ppermute | solution.py:17
  281.2 25.2 %collective-permute-start.30 = (bf16[128,2048]{1,0:T(8,128)(2,1)S(1)}, bf16[128,2048]{1,0:T(8,128)(2,1)S(1)}, u32[]{:S(2)}, u32[]{:S(2)}) collective-permute-start(bf16[128,2048]{1,0:T(8,128)(2,1)S(1)} %slice.414), channel_id=1, source_target_pairs={{0,16},{4,20},{8,24},{12,28},{16,0},{20,4},{24,8},{28,12},{1,17},{... | collective-permute-start | bytes 1572872 | tf_op jit(solution)/shard_map/ppermute | solution.py:17
  291.1 22.5 %collective-permute-start.29 = (bf16[128,2048]{1,0:T(8,128)(2,1)S(1)}, bf16[128,2048]{1,0:T(8,128)(2,1)S(1)}, u32[]{:S(2)}, u32[]{:S(2)}) collective-permute-start(bf16[128,2048]{1,0:T(8,128)(2,1)S(1)} %add_convert_fusion.8), channel_id=1, source_target_pairs={{0,8},{4,12},{8,0},{12,4},{16,24},{20,28},{24,16},{28,20},{1,9},{5... | collective-permute-start | bytes 1572872 | tf_op jit(solution)/shard_map/ppermute | solution.py:17
  318.9 22.3 %collective-permute-start.31 = (bf16[256,2048]{1,0:T(8,128)(2,1)S(1)}, bf16[256,2048]{1,0:T(8,128)(2,1)S(1)}, u32[]{:S(2)}, u32[]{:S(2)}) collective-permute-start(bf16[256,2048]{1,0:T(8,128)(2,1)S(1)} %get-tuple-element.45), channel_id=1, source_target_pairs={{0,8},{4,12},{8,0},{12,4},{16,24},{20,28},{24,16},{28,20},{1,9},{5... | collective-permute-start | bytes 3145736 | tf_op jit(solution)/shard_map/ppermute | solution.py:17
  320.0 29.5 %collective-permute-start.32 = (bf16[256,2048]{1,0:T(8,128)(2,1)S(1)}, bf16[256,2048]{1,0:T(8,128)(2,1)S(1)}, u32[]{:S(2)}, u32[]{:S(2)}) collective-permute-start(bf16[256,2048]{1,0:T(8,128)(2,1)S(1)} %get-tuple-element.45), channel_id=1, source_target_pairs={{0,16},{4,20},{8,24},{12,28},{16,0},{20,4},{24,8},{28,12},{1,17},{... | collective-permute-start | bytes 3145736 | tf_op jit(solution)/shard_map/ppermute | solution.py:17
  349.5 20.8 %collective-permute-start.63 = (bf16[704,2048]{1,0:T(8,128)(2,1)}, bf16[704,2048]{1,0:T(8,128)(2,1)}, u32[]{:S(2)}, u32[]{:S(2)}) collective-permute-start(bf16[704,2048]{1,0:T(8,128)(2,1)} %convolution_convert_fusion.1), channel_id=1, source_target_pairs={{0,4},{4,0},{8,12},{12,8},{16,20},{20,16},{24,28},{28,24},{1,5},{5... | collective-permute-start | bytes 8650760 | tf_op jit(solution)/shard_map/ppermute | solution.py:17
  370.3 194.9 %reduce-scatter.11.cloned.1.call-start = ((), (), s32[]{:S(2)}) async-start(), calls=%async_computation.9 | async-start | bytes 3604480 | tf_op jit(solution)/shard_map/reduce_scatter | solution.py:408
  378.7 188.8 %reduce-scatter.9.cloned.1.call-start = ((), (), s32[]{:S(2)}) async-start(), calls=%async_computation.8 | async-start | bytes 7208960 | tf_op jit(solution)/shard_map/reduce_scatter | solution.py:423
  401.1 238.7 %reduce-scatter.5.cloned.1.call-start = ((), (), s32[]{:S(2)}) async-start(), calls=%async_computation.6 | async-start | bytes 5242880 | tf_op jit(solution)/shard_map/reduce_scatter | solution.py:462
  424.5 41.9 %collective-permute-start.51 = (f32[2,256]{1,0:T(2,128)S(1)}, f32[2,256]{1,0:T(2,128)S(1)}, u32[]{:S(2)}, u32[]{:S(2)}) collective-permute-start(f32[2,256]{1,0:T(2,128)S(1)} %pad_maximum_fusion.10), channel_id=1, source_target_pairs={{0,4},{4,0},{8,12},{12,8},{16,20},{20,16},{24,28},{28,24},{1,5},{5... | collective-permute-start | bytes 6152 | tf_op jit(solution)/shard_map/ppermute | solution.py:17
  431.6 50.3 %collective-permute-start.49 = (bf16[2048,1024]{1,0:T(8,128)(2,1)}, bf16[2048,1024]{1,0:T(8,128)(2,1)S(1)}, u32[]{:S(2)}, u32[]{:S(2)}) collective-permute-start(bf16[2048,1024]{1,0:T(8,128)(2,1)} %convolution_convert_fusion), channel_id=1, source_target_pairs={{0,4},{4,0},{8,12},{12,8},{16,20},{20,16},{24,28},{28,24},{1,5},{5... | collective-permute-start | bytes 12582920 | tf_op jit(solution)/shard_map/ppermute | solution.py:17
  476.3 39.4 %collective-permute-start.42 = (bf16[128,2048]{1,0:T(8,128)(2,1)}, bf16[128,2048]{1,0:T(8,128)(2,1)}, u32[]{:S(2)}, u32[]{:S(2)}) collective-permute-start(bf16[128,2048]{1,0:T(8,128)(2,1)} %slice.428), channel_id=1, source_target_pairs={{0,8},{4,12},{8,0},{12,4},{16,24},{20,28},{24,16},{28,20},{1,9},{5... | collective-permute-start | bytes 1572872 | tf_op jit(solution)/shard_map/ppermute | solution.py:17
  476.9 25.8 %collective-permute-start.43 = (bf16[128,2048]{1,0:T(8,128)(2,1)}, bf16[128,2048]{1,0:T(8,128)(2,1)}, u32[]{:S(2)}, u32[]{:S(2)}) collective-permute-start(bf16[128,2048]{1,0:T(8,128)(2,1)} %get-tuple-element.74), channel_id=1, source_target_pairs={{0,8},{4,12},{8,0},{12,4},{16,24},{20,28},{24,16},{28,20},{1,9},{5... | collective-permute-start | bytes 1572872 | tf_op jit(solution)/shard_map/ppermute | solution.py:17
  478.3 38.5 %collective-permute-start.47 = (bf16[128,2048]{1,0:T(8,128)(2,1)}, bf16[128,2048]{1,0:T(8,128)(2,1)}, u32[]{:S(2)}, u32[]{:S(2)}) collective-permute-start(bf16[128,2048]{1,0:T(8,128)(2,1)} %slice.434), channel_id=1, source_target_pairs={{0,16},{4,20},{8,24},{12,28},{16,0},{20,4},{24,8},{28,12},{1,17},{... | collective-permute-start | bytes 1572872 | tf_op jit(solution)/shard_map/ppermute | solution.py:17
  479.9 24.7 %collective-permute-start.38 = (bf16[128,2048]{1,0:T(8,128)(2,1)}, bf16[128,2048]{1,0:T(8,128)(2,1)}, u32[]{:S(2)}, u32[]{:S(2)}) collective-permute-start(bf16[128,2048]{1,0:T(8,128)(2,1)} %get-tuple-element.79), channel_id=1, source_target_pairs={{0,16},{4,20},{8,24},{12,28},{16,0},{20,4},{24,8},{28,12},{1,17},{... | collective-permute-start | bytes 1572872 | tf_op jit(solution)/shard_map/ppermute | solution.py:17
  481.9 32.1 %collective-permute-start.36 = (bf16[128,2048]{1,0:T(8,128)(2,1)}, bf16[128,2048]{1,0:T(8,128)(2,1)}, u32[]{:S(2)}, u32[]{:S(2)}) collective-permute-start(bf16[128,2048]{1,0:T(8,128)(2,1)} %get-tuple-element.78), channel_id=1, source_target_pairs={{0,8},{4,12},{8,0},{12,4},{16,24},{20,28},{24,16},{28,20},{1,9},{5... | collective-permute-start | bytes 1572872 | tf_op jit(solution)/shard_map/ppermute | solution.py:17
  502.7 22.4 %collective-permute-start.46 = (bf16[128,2048]{1,0:T(8,128)(2,1)}, bf16[128,2048]{1,0:T(8,128)(2,1)S(1)}, u32[]{:S(2)}, u32[]{:S(2)}) collective-permute-start(bf16[128,2048]{1,0:T(8,128)(2,1)} %add_convert_fusion.4), channel_id=1, source_target_pairs={{0,8},{4,12},{8,0},{12,4},{16,24},{20,28},{24,16},{28,20},{1,9},{5... | collective-permute-start | bytes 1572872 | tf_op jit(solution)/shard_map/ppermute | solution.py:17
  504.6 21.4 %collective-permute-start.44 = (bf16[128,2048]{1,0:T(8,128)(2,1)S(1)}, bf16[128,2048]{1,0:T(8,128)(2,1)S(1)}, u32[]{:S(2)}, u32[]{:S(2)}) collective-permute-start(bf16[128,2048]{1,0:T(8,128)(2,1)S(1)} %add_convert_fusion.5), channel_id=1, source_target_pairs={{0,16},{4,20},{8,24},{12,28},{16,0},{20,4},{24,8},{28,12},{1,17},{... | collective-permute-start | bytes 1572872 | tf_op jit(solution)/shard_map/ppermute | solution.py:17
  513.9 22.4 %collective-permute-start.35 = (bf16[128,2048]{1,0:T(8,128)(2,1)}, bf16[128,2048]{1,0:T(8,128)(2,1)S(1)}, u32[]{:S(2)}, u32[]{:S(2)}) collective-permute-start(bf16[128,2048]{1,0:T(8,128)(2,1)} %slice.418), channel_id=1, source_target_pairs={{0,8},{4,12},{8,0},{12,4},{16,24},{20,28},{24,16},{28,20},{1,9},{5... | collective-permute-start | bytes 1572872 | tf_op jit(solution)/shard_map/ppermute | solution.py:17
  515.7 21.2 %collective-permute-start.40 = (bf16[128,2048]{1,0:T(8,128)(2,1)S(1)}, bf16[128,2048]{1,0:T(8,128)(2,1)S(1)}, u32[]{:S(2)}, u32[]{:S(2)}) collective-permute-start(bf16[128,2048]{1,0:T(8,128)(2,1)S(1)} %copy-done.37), channel_id=1, source_target_pairs={{0,16},{4,20},{8,24},{12,28},{16,0},{20,4},{24,8},{28,12},{1,17},{... | collective-permute-start | bytes 1572872 | tf_op jit(solution)/shard_map/ppermute | solution.py:17
  516.8 29.1 %collective-permute-start.39 = (bf16[128,2048]{1,0:T(8,128)(2,1)S(1)}, bf16[128,2048]{1,0:T(8,128)(2,1)S(1)}, u32[]{:S(2)}, u32[]{:S(2)}) collective-permute-start(bf16[128,2048]{1,0:T(8,128)(2,1)S(1)} %add_convert_fusion.6), channel_id=1, source_target_pairs={{0,8},{4,12},{8,0},{12,4},{16,24},{20,28},{24,16},{28,20},{1,9},{5... | collective-permute-start | bytes 1572872 | tf_op jit(solution)/shard_map/ppermute | solution.py:17
  525.1 20.8 %collective-permute-start.37 = (bf16[128,2048]{1,0:T(8,128)(2,1)S(1)}, bf16[128,2048]{1,0:T(8,128)(2,1)S(1)}, u32[]{:S(2)}, u32[]{:S(2)}) collective-permute-start(bf16[128,2048]{1,0:T(8,128)(2,1)S(1)} %add_convert_fusion.7), channel_id=1, source_target_pairs={{0,16},{4,20},{8,24},{12,28},{16,0},{20,4},{24,8},{28,12},{1,17},{... | collective-permute-start | bytes 1572872 | tf_op jit(solution)/shard_map/ppermute | solution.py:17
  530.3 29.8 %collective-permute-start.48 = (f32[128,2048]{1,0:T(8,128)}, f32[128,2048]{1,0:T(8,128)}, u32[]{:S(2)}, u32[]{:S(2)}) collective-permute-start(f32[128,2048]{1,0:T(8,128)} %get-tuple-element.59), channel_id=1, source_target_pairs={{0,4},{4,0},{8,12},{12,8},{16,20},{20,16},{24,28},{28,24},{1,5},{5... | collective-permute-start | bytes 3145736 | tf_op jit(solution)/shard_map/ppermute | solution.py:17
  (87 other events, 1148.3 us)
Sparse Core Ops, SparseCore 0:
  16.0 109.1 all-gather.2
  129.0 57.5 all-gather.4
  370.4 27.0 reduce-scatter.6
  399.8 54.8 reduce-scatter.10
  456.9 103.2 reduce-scatter.8
  562.5 77.2 reduce-scatter.4

commit v2 on v1

--- a/solution.py
+++ b/solution.py
@@ -39,46 +39,71 @@
     return swap(near[0][:half], bits[1], size), swap(near[1][half:], bits[0], size)
 
 
-def gather_chips(own, bits, size):
+def gather_start(own, bits, size):
     if len(bits) == 2:
         near = gather_near(own, bits, size)
-        return [own, *near, *gather_far(near, bits, size)]
+        return near, [own, *near, *gather_far(near, bits, size)]
     parts = [own]
     for bit in bits:
         moved = swap(jnp.stack(parts), bit, size)
         parts = parts + [moved[at] for at in range(len(parts))]
-    return parts
-
-
-def scatter_chips(part_of, bits, size):
-    if len(bits) == 2:
-        first, second = bits
-        both = part_of(3).astype(bf16)
-        half = both.shape[0] // 2
-        top_both, bottom_both = swap(both[:half], first, size), swap(both[half:], second, size)
-        at_first, at_second = part_of(1), part_of(2)
-        top_first = swap(at_first[:half].astype(bf16), first, size)
-        bottom_second = swap(at_second[half:].astype(bf16), second, size)
-        bottom_first = swap(
-            (at_first[half:].astype(f32) + bottom_both.astype(f32)).astype(bf16), first, size
+    return parts[1:], parts
+
+
+class Scatter:
+    def __init__(self, part_of, bits, size):
+        self.bits, self.size = bits, size
+        self.moved, self.sends = [], None
+        if len(bits) == 2:
+            first, second = bits
+            both = part_of(3)
+            self.half = half = both.shape[0] // 2
+            top_both, bottom_both = swap(both[:half], first, size), swap(both[half:], second, size)
+            self.at_first, self.at_second = part_of(1), part_of(2)
+            top_first = swap(self.at_first[:half], first, size)
+            bottom_second = swap(self.at_second[half:], second, size)
+            self.moved = [top_both, bottom_both, top_first, bottom_second]
+            self.own = part_of(0)
+        else:
+            self.parts = [part_of(at) for at in range(1 << len(bits))]
+
+    def finish(self):
+        self.moved = list(tie(*self.moved))
+        top_both, bottom_both = self.moved[:2]
+        self.sends = (
+            add(self.at_first[self.half :], bottom_both).astype(bf16),
+            add(self.at_second[: self.half], top_both).astype(bf16),
         )
-        top_second = swap(
-            (at_second[:half].astype(f32) + top_both.astype(f32)).astype(bf16), second, size
-        )
-        own = part_of(0).astype(f32)
-        top = own[:half] + top_first.astype(f32) + top_second.astype(f32)
-        bottom = own[half:] + bottom_first.astype(f32) + bottom_second.astype(f32)
-        return jnp.concatenate((top, bottom))
-    parts = [part_of(at).astype(f32) for at in range(1 << len(bits))]
-    for bit in reversed(bits):
-        count = len(parts) // 2
-        moved = swap(jnp.stack(parts[count:]).astype(bf16), bit, size)
-        parts = [parts[at] + moved[at].astype(f32) for at in range(count)]
-    return parts[0]
-
-
-def after(tensor, *others):
-    return lax.optimization_barrier((tensor,) + others)[0]
+
+    def total(self, held=None):
+        bits, size = self.bits, self.size
+        if len(bits) == 2:
+            first, second = bits
+            if self.sends is None:
+                self.finish()
+            bottom_first, top_second = swap(self.sends[0], first, size), swap(self.sends[1], second, size)
+            bottom_first, top_second, held = tie(bottom_first, top_second, held)
+            top_first, bottom_second = self.moved[2:]
+            top = add(self.own[: self.half], top_first, top_second)
+            bottom = add(self.own[self.half :], bottom_first, bottom_second)
+            return jnp.concatenate((top, bottom)), held
+        parts = [part.astype(f32) for part in self.parts]
+        for bit in reversed(bits):
+            count = len(parts) // 2
+            moved = swap(jnp.stack(parts[count:]).astype(bf16), bit, size)
+            parts = [add(parts[at], moved[at]) for at in range(count)]
+        return parts[0], held
+
+
+def add(first, *rest):
+    total = first.astype(f32)
+    for term in rest:
+        total = total + term.astype(f32)
+    return total
+
+
+def tie(*tensors):
+    return lax.optimization_barrier(tensors)
 
 
 def halves(tensor):
@@ -254,9 +279,9 @@
             ],
             scratch_shapes=[pltpu.VMEM((2 * half_heads, HEAD_DIM, HEAD_DIM), f32)],
         ),
-        compiler_params=pltpu.CompilerParams(vmem_limit_bytes=24 * 1024 * 1024),
+        compiler_params=pltpu.CompilerParams(vmem_limit_bytes=16 * 2**20),
         cost_estimate=pl.CostEstimate(
-            flops=blocks * 2 * half_heads * 16 * HEAD_DIM**3, bytes_accessed=16 * 2**20, transcendentals=0
+            flops=0, bytes_accessed=0, transcendentals=0
         ),
     )(info, proj, floor_row, gain_row, seg)
 
@@ -298,11 +323,145 @@
             ],
             scratch_shapes=[pltpu.VMEM((2 * half_heads, HEAD_DIM, HEAD_DIM), f32)],
         ),
-        compiler_params=pltpu.CompilerParams(vmem_limit_bytes=24 * 1024 * 1024),
+        compiler_params=pltpu.CompilerParams(vmem_limit_bytes=20 * 2**20),
         cost_estimate=pl.CostEstimate(
-            flops=blocks * 2 * half_heads * 32 * HEAD_DIM**3, bytes_accessed=24 * 2**20, transcendentals=0
+            flops=0, bytes_accessed=0, transcendentals=0
         ),
     )(info, proj, floor_row, gain_row, seg, mixed, grad, states, scores)
+
+
+def stack_kernel(count, own, other, *refs):
+    outs, sems = refs[:count], refs[count]
+    half = own.shape[1]
+    copies = []
+    for at in range(count):
+        for side, source in enumerate((own, other)):
+            target = outs[at].at[pl.ds(side * half, half)]
+            copies.append(pltpu.make_async_copy(source.at[at], target, sems.at[at, side]))
+    for copy in copies:
+        copy.start()
+    for copy in copies:
+        copy.wait()
+
+
+def stack_rows(own, other):
+    count, rows, depth = own.shape
+    return pl.pallas_call(
+        functools.partial(stack_kernel, count),
+        out_shape=[jax.ShapeDtypeStruct((2 * rows, depth), own.dtype)] * count,
+        in_specs=[pl.BlockSpec(memory_space=pl.ANY)] * 2,
+        out_specs=[pl.BlockSpec(memory_space=pltpu.VMEM)] * count,
+        scratch_shapes=[pltpu.SemaphoreType.DMA((count, 2))],
+        compiler_params=pltpu.CompilerParams(vmem_limit_bytes=4 * 2**20),
+        cost_estimate=pl.CostEstimate(flops=0, bytes_accessed=0, transcendentals=0),
+    )(own, other)
+
+
+def add_kernel(left, right, out):
+    out[...] = (left[...].astype(f32) + right[...].astype(f32)).astype(bf16)
+
+
+def add_pair(left, right):
+    rows, depth = left.shape
+    step = rows
+    while step > 256 and step % 32 == 0:
+        step //= 2
+    block = pl.BlockSpec((step, depth), lambda at: (at, 0))
+    return pl.pallas_call(
+        add_kernel,
+        out_shape=jax.ShapeDtypeStruct((rows, depth), bf16),
+        grid=(rows // step,),
+        in_specs=[block] * 2,
+        out_specs=block,
+        compiler_params=pltpu.CompilerParams(vmem_limit_bytes=10 * 2**20),
+        cost_estimate=pl.CostEstimate(flops=0, bytes_accessed=0, transcendentals=0),
+    )(left, right)
+
+
+def cross_kernel(groups, count, left_cols, right_cols, *refs):
+    lefts, rights = refs[: sum(groups)], refs[sum(groups) : sum(groups) + count]
+    out, left_held, right_held, out_held, left_sem, right_sem, out_sem = refs[sum(groups) + count :]
+    rows, width = out.shape[1:]
+    spare = left_cols % 128
+    step = out_held.shape[3]
+    tiles = width // step
+    left_copies, right_copies = [], [[] for _ in range(tiles)]
+    at = 0
+    for group, many in enumerate(groups):
+        first = 0
+        for ref in lefts[at : at + many]:
+            here = pl.ds(first, ref.shape[0])
+            left_copies.append(
+                pltpu.make_async_copy(ref, left_held.at[group, here], left_sem.at[len(left_copies)])
+            )
+            first += ref.shape[0]
+        at += many
+    for tile in range(tiles):
+        first = 0
+        for index, ref in enumerate(rights):
+            source = ref.at[:, pl.ds(right_cols + tile * step, step)]
+            target = right_held.at[tile, pl.ds(first, ref.shape[0])]
+            right_copies[tile].append(
+                pltpu.make_async_copy(source, target, right_sem.at[tile, index])
+            )
+            first += ref.shape[0]
+    for copy in right_copies[0] + left_copies:
+        copy.start()
+    for copies in right_copies[1:]:
+        for copy in copies:
+            copy.start()
+    for copy in left_copies:
+        copy.wait()
+    out_copies = []
+    for tile in range(tiles):
+        for copy in right_copies[tile]:
+            copy.wait()
+        for group in range(len(groups)):
+            left = left_held[group, :, left_cols - spare : left_cols + rows]
+            product = mm(left, right_held[tile], TN)
+            out_held[tile, group] = product[spare:].astype(bf16)
+            out_copies.append(
+                pltpu.make_async_copy(
+                    out_held.at[tile, group],
+                    out.at[group, :, pl.ds(tile * step, step)],
+                    out_sem.at[tile, group],
+                )
+            )
+            out_copies[-1].start()
+    for copy in out_copies:
+        copy.wait()
+
+
+def cross(groups, rights, left_cols=None, right_cols=None):
+    tokens = sum(part.shape[0] for part in rights)
+    left_width, right_width = groups[0][0].shape[1], rights[0].shape[1]
+    left_cols, right_cols = left_cols or (0, left_width), right_cols or (0, right_width)
+    rows, width = left_cols[1], right_cols[1]
+    step = 512 if width % 512 == 0 else width
+    tiles, many = width // step, len(groups)
+    anywhere = pl.BlockSpec(memory_space=pl.ANY)
+    args = [part for group in groups for part in group] + list(rights)
+    return pl.pallas_call(
+        functools.partial(
+            cross_kernel, [len(group) for group in groups], len(rights), left_cols[0], right_cols[0]
+        ),
+        out_shape=jax.ShapeDtypeStruct((many, rows, width), bf16),
+        in_specs=[anywhere] * len(args),
+        out_specs=anywhere,
+        scratch_shapes=[
+            pltpu.VMEM((many, tokens, left_width), bf16),
+            pltpu.VMEM((tiles, tokens, step), bf16),
+            pltpu.VMEM((tiles, many, rows, step), bf16),
+            pltpu.SemaphoreType.DMA((len(args) - len(rights),)),
+            pltpu.SemaphoreType.DMA((tiles, len(rights))),
+            pltpu.SemaphoreType.DMA((tiles, many)),
+        ],
+        compiler_params=pltpu.CompilerParams(
+            vmem_limit_bytes=2 * (many * tokens * left_width + tokens * width + many * rows * width)
+            + 10 * 2**20
+        ),
+        cost_estimate=pl.CostEstimate(flops=0, bytes_accessed=0, transcendentals=0),
+    )(*args)
 
 
 def per_device(
@@ -348,21 +507,34 @@
         mine, other = tensor[:shard_len], swap(tensor[shard_len:], 1, size)
         return jnp.where(row == 0, jnp.stack((mine, other)), jnp.stack((other, mine)))
 
+    two = len(bits) == 2
+
     def chunk(tensor, at):
         return tensor[at * own_tokens : (at + 1) * own_tokens]
 
-    gate_up = lax.all_gather(jnp.stack((ffn_gate.T, ffn_up.T)), "dp", axis=1, tiled=True)
-    down = lax.all_gather(after(ffn_down.T, gate_up), "dp", axis=0, tiled=True)
-
-    own_rows = to_row(layer_input).astype(f32)
-    input_scale = rms_scale(own_rows)
-    normed_own = (own_rows * input_scale * norm1_gain).astype(bf16)
-    normed_parts = gather_chips(normed_own, bits, size)
-    normed = jnp.concatenate(normed_parts)
+    pair_rows = layer_input.astype(f32)
+    pair_scale = rms_scale(pair_rows)
+    pair_normed = (pair_rows * pair_scale * norm1_gain).astype(bf16)
+    normed_mine, normed_theirs = pick(pair_normed, row), pick(pair_normed, 1 - row)
+    gate_up, normed_mine, normed_theirs = tie((ffn_gate.T, ffn_up.T), normed_mine, normed_theirs)
+    normed_sib = swap(normed_theirs, 1, size)
+    if two:
+        first, second = bits
+        near_first = [swap(normed_mine, first, size), swap(normed_theirs, first | 1, size)]
+        near_second = [swap(normed_mine, second, size), swap(normed_theirs, second | 1, size)]
+        far = [swap(near_first[0], second, size), swap(near_second[1], first, size)]
+        normed_parts = [normed_mine, normed_sib, *near_first, *near_second, *far]
+    else:
+        normed_parts = gather_start(jnp.concatenate((normed_mine, normed_sib)), bits, size)[1]
+
+    normed_parts[1], out_cotangent = tie(normed_parts[1], out_cotangent)
+    cot_own = to_row(out_cotangent)
+
+    gate_up = lax.all_gather(jnp.stack(gate_up), "dp", axis=1, tiled=True)
+    down = lax.all_gather(ffn_down.T, "dp", axis=0, tiled=True)
 
     proj_own = jnp.concatenate((w_query, w_forget, w_input, w_gate_out), axis=1)
     proj_weights = jnp.concatenate((proj_own, swap(proj_own, 1, size)), axis=1)
-    out_weights = jnp.concatenate((w_out, swap(w_out, 1, size)))
     vectors = jnp.stack((forget_floor, group_gain))
     vectors = jnp.concatenate((vectors, swap(vectors, 1, size)), axis=1)
     floor_row, gain_row = vectors[:1], vectors[1:]
@@ -372,79 +544,142 @@
     info = jnp.concatenate((me[None], jnp.zeros((1,), jnp.int32), seg_last[:-1], seg_last))
     seg = seg[:, None, :]
 
-    proj = mm(normed, proj_weights, NN)
-    gated, mixed, states, scores = recurrence(info, proj, floor_row, gain_row, seg, half_heads, size)
-    cot_own = to_row(out_cotangent)
-    if len(bits) == 2:
-        cot_near = gather_near(after(cot_own, *normed_parts), bits, size)
-
-    resid = own_rows + scatter_chips(
-        lambda at: mm(chunk(gated, at), out_weights, NN).astype(bf16), bits, size
+    proj = jnp.zeros((seq_len, 4 * width), f32)
+    at = 0
+    early = len(normed_parts) * 3 // 4 if two else 0
+    for index, part in enumerate(normed_parts):
+        if two and index == early:
+            proj, *normed_parts[early:], cot_own, layer_input, w_out = tie(
+                proj, *normed_parts[early:], cot_own, layer_input, w_out
+            )
+            part = normed_parts[index]
+        proj = lax.dynamic_update_slice(proj, mm(part, proj_weights, NN), (at, 0))
+        at += part.shape[0]
+    gated, mixed, states, scores = recurrence(
+        info, proj, floor_row, gain_row, seg, half_heads, size
     )
+    out_weights = jnp.concatenate((w_out, swap(w_out, 1, size)))
+
+    own_rows = to_row(layer_input)
+    if two:
+        cot_near = gather_near(cot_own, bits, size)
+        gated, cot_near, own_rows = tie(gated, cot_near, own_rows)
+    own_rows = own_rows.astype(f32)
+
+    mixer_sum = Scatter(lambda at: mm(chunk(gated, at), out_weights, NN).astype(bf16), bits, size)
+    resid = own_rows + mixer_sum.total(own_rows)[0]
     row_scale = rms_scale(resid)
     ffn_own = (resid * row_scale * norm2_gain).astype(bf16)
-    ffn_parts = gather_chips(ffn_own, bits, size)
-    ffn_in = jnp.concatenate(ffn_parts)
-    if len(bits) == 2:
-        cot_held = [after(near, *ffn_parts) for near in cot_near]
-        cot_parts = [cot_own, *cot_near, *gather_far(cot_held, bits, size)]
+    ffn_own, gate_up = tie(ffn_own, gate_up)
+    if two:
+        ffn_near = gather_near(ffn_own, bits, size)
+        ffn_near, cot_near = tie(ffn_near, cot_near)
+        ffn_far = gather_far(ffn_near, bits, size)
+        cot_flat = [cot_own, *cot_near, *gather_far(cot_near, bits, size)]
+        ffn_parts = [ffn_own, *ffn_near, ffn_far]
     else:
-        cot_parts = gather_chips(after(cot_own, *ffn_parts), bits, size)
-    cot = jnp.concatenate(cot_parts)
-
-    gate_up = jnp.concatenate((gate_up, swap(gate_up, 1, size)), axis=1)
-    gate_rows, up_rows = gate_up[0], gate_up[1]
-    down_rows = jnp.concatenate((down, swap(down, 1, size)))
-    gate_ff = mm(ffn_in, gate_rows, NT)
-    up_ff = mm(ffn_in, up_rows, NT)
-    gate_sig = jax.nn.sigmoid(gate_ff)
-    inner = (gate_ff * gate_sig * up_ff).astype(bf16)
-
-    def pair_grad(left, right, cut):
-        other = swap(mm(left[:, cut:], right, TN).astype(bf16), 1, size)
-        return (mm(left[:, :cut], right, TN) + other.astype(f32)).astype(bf16)
-
-    down_grad = pair_grad(inner, cot, hidden_half)
-    ffn_down_grad = lax.psum_scatter(down_grad, "dp", scatter_dimension=0, tiled=True)
-
-    inner_grad = mm(cot, down_rows, NT)
-    gate_grad = (inner_grad * up_ff * gate_sig * (1.0 + gate_ff * (1.0 - gate_sig))).astype(bf16)
-    up_grad = (inner_grad * gate_ff * gate_sig).astype(bf16)
-    ffn_in_grad = scatter_chips(
-        lambda at: (
-            mm(chunk(gate_grad, at), gate_rows, NN) + mm(chunk(up_grad, at), up_rows, NN)
-        ).astype(bf16),
-        bits,
-        size,
+        ffn_parts = gather_start(ffn_own, bits, size)[1]
+        cot_flat = gather_start(cot_own, bits, size)[1]
+    ffn_flat = [*ffn_parts[:3], *ffn_parts[3]] if two else ffn_parts
+    count = len(ffn_parts)
+    gate_rows, up_rows = stack_rows(gate_up, swap(gate_up, 1, size))
+
+    gate_part, up_part, inner = [], [], []
+    for at in range(count):
+        if at:
+            ffn_parts[at], inner[-1] = tie(ffn_parts[at], inner[-1])
+        if two and at == 3:
+            ffn_parts[3] = jnp.concatenate(ffn_parts[3])
+        gate, up = mm(ffn_parts[at], gate_rows, NT), mm(ffn_parts[at], up_rows, NT)
+        sig = jax.nn.sigmoid(gate)
+        up_part.append(gate * sig)
+        gate_part.append(up * sig * (1.0 + gate * (1.0 - sig)))
+        inner.append((up_part[-1] * up).astype(bf16))
+    lower, upper = (0, hidden_half), (hidden_half, hidden_half)
+    down_other = cross([inner], cot_flat, left_cols=upper)
+    down_other, inner[0], down = tie(down_other, inner[0], down)
+    down_own = cross([inner], cot_flat, left_cols=lower)
+    down_pair = add_pair(down_own[0], swap(down_other[0], 1, size))
+    (down_rows,) = stack_rows(down[None], swap(down, 1, size)[None])
+    down_pair, cot_flat = tie(down_pair, cot_flat)
+    cot_parts = [*cot_flat[:3], jnp.concatenate(cot_flat[3:])] if two else cot_flat
+    ffn_down_grad = lax.psum_scatter(down_pair, "dp", scatter_dimension=0, tiled=True)
+
+    gate_grad, up_grad, totals = [None] * count, [None] * count, []
+
+    def ffn_part(at):
+        part = cot_parts[at]
+        if totals:
+            part, totals[-1] = tie(part, totals[-1])
+        inner_grad = mm(part, down_rows, NT)
+        gate_grad[at] = (inner_grad * gate_part[at]).astype(bf16)
+        up_grad[at] = (inner_grad * up_part[at]).astype(bf16)
+        totals.append(
+            add(mm(gate_grad[at], gate_rows, NN), mm(up_grad[at], up_rows, NN)).astype(bf16)
+        )
+        return totals[-1]
+
+    ffn_sum = Scatter(ffn_part, bits, size)
+    if two:
+        ffn_sum.own, gate_grad, up_grad = tie(ffn_sum.own, gate_grad, up_grad)
+    gate_up_other = cross([gate_grad, up_grad], ffn_flat, left_cols=upper)
+    if two:
+        ffn_sum.moved, gate_up_other = tie(ffn_sum.moved, gate_up_other)
+        ffn_sum.finish()
+        ffn_sum.sends, gate_grad, up_grad = tie(ffn_sum.sends, gate_grad, up_grad)
+    gate_up_other, gate_grad, up_grad, ffn_down_grad = tie(
+        gate_up_other, gate_grad, up_grad, ffn_down_grad
     )
-    gate_up_grad = jnp.stack(
-        (pair_grad(gate_grad, ffn_in, hidden_half), pair_grad(up_grad, ffn_in, hidden_half))
-    )
-    gate_up_grad = lax.psum_scatter(
-        after(gate_up_grad, down_grad), "dp", scatter_dimension=1, tiled=True
-    )
+    gate_up_own = cross([gate_grad, up_grad], ffn_flat, left_cols=lower)
+    gate_up_pair = add_pair(
+        gate_up_own.reshape(-1, model_width), swap(gate_up_other, 1, size).reshape(-1, model_width)
+    ).reshape(gate_up_own.shape)
+    ffn_in_grad, gate_up_pair = ffn_sum.total(gate_up_pair)
+    gate_up_grad = lax.psum_scatter(gate_up_pair, "dp", scatter_dimension=1, tiled=True)
 
     scaled = ffn_in_grad * norm2_gain
     resid_grad = cot_own.astype(f32) + row_scale * (
         scaled - resid * row_scale * row_scale * jnp.mean(scaled * resid, axis=-1, keepdims=True)
     )
     norm2_part = jnp.sum(ffn_in_grad * resid * row_scale, axis=0)
-    mixer_parts = gather_chips(resid_grad.astype(bf16), bits, size)
+    mixer_parts = gather_start(resid_grad.astype(bf16), bits, size)[1]
     mixer_grad = jnp.concatenate(mixer_parts)
 
-    inner_late = after(inner, *mixer_parts)
-    output = resid + scatter_chips(
-        lambda at: mm(chunk(inner_late, at), down_rows, NN).astype(bf16), bits, size
-    )
-    output = from_row(output.astype(bf16))
-
+    out_other = cross([[gated]], mixer_parts, left_cols=(half_width, half_width))
+    out_other, gated = tie(out_other, gated)
+    out_own = cross([[gated]], mixer_parts, left_cols=(0, half_width))
+    mixer_grad, out_own = tie(mixer_grad, out_own)
+    out_pair = add_pair(out_own[0], swap(out_other[0], 1, size))
     gated_grad = mm(mixer_grad, out_weights, NT)
     proj_grad, floor_grad, gain_grad = recurrence_back(
         info, proj, floor_row, gain_row, seg, mixed, gated_grad, states, scores, half_heads, size
     )
-    normed_grad = scatter_chips(
-        lambda at: mm(chunk(proj_grad, at), proj_weights, NT).astype(bf16), bits, size
-    )
+    line = [proj_grad]
+
+    def normed_part(at):
+        part = mm(chunk(line[0], at), proj_weights, NT).astype(bf16)
+        line[0], part = tie(line[0], part)
+        return part
+
+    normed_sum = Scatter(normed_part, bits, size)
+    proj_grad = line[0]
+
+    proj_other = cross([normed_parts], [proj_grad], right_cols=(2 * width, 2 * width))
+    if two:
+        normed_sum.at_first, normed_sum.at_second, proj_other = tie(
+            normed_sum.at_first, normed_sum.at_second, proj_other
+        )
+        normed_sum.finish()
+        normed_sum.sends, proj_grad = tie(normed_sum.sends, proj_grad)
+    proj_grad, proj_other = tie(proj_grad, proj_other)
+    proj_own = cross([normed_parts], [proj_grad], right_cols=(0, 2 * width))
+    normed_grad, proj_own = normed_sum.total(proj_own)
+    proj_pair = add_pair(proj_own[0], swap(proj_other[0], 1, size))
+    proj_pair, out_pair, gate_up_grad = tie(proj_pair, out_pair, gate_up_grad)
+    out_grad = lax.psum_scatter(out_pair, "dp", scatter_dimension=1, tiled=True)
+    proj_w_grad = lax.psum_scatter(proj_pair, "dp", scatter_dimension=0, tiled=True).astype(f32)
+
+    input_scale = rms_scale(own_rows)
     scaled_in = normed_grad * norm1_gain
     input_grad = resid_grad + input_scale * (
         scaled_in
@@ -456,13 +691,9 @@
     norm1_part = jnp.sum(normed_grad * own_rows * input_scale, axis=0)
     input_grad = from_row(input_grad)
 
-    out_grad = pair_grad(gated, mixer_grad, half_width)
-    proj_w_grad = mm(normed, proj_grad[:, 2 * width :], TN).astype(bf16)
-    proj_w_grad = mm(normed, proj_grad[:, : 2 * width], TN) + swap(proj_w_grad, 1, size).astype(f32)
-    proj_w_grad = lax.psum_scatter(
-        proj_w_grad.astype(bf16), "dp", scatter_dimension=0, tiled=True
-    ).astype(f32)
-    out_grad = lax.psum_scatter(out_grad, "dp", scatter_dimension=1, tiled=True)
+    inner, norm1_part = tie(inner, norm1_part)
+    output_sum = Scatter(lambda at: mm(inner[at], down_rows, NN).astype(bf16), bits, size)
+    output = from_row(add(resid, output_sum.total(resid)[0]).astype(bf16))
 
     vector_grads = jnp.concatenate((gain_grad, floor_grad))
     vector_grads = vector_grads[:, :half_width] + swap(vector_grads[:, half_width:], 1, size)

time: 657 us -> 580 us (0.88)
  waiting for transfers between devices: 289 us -> 169 us
  Pallas kernels: 33 us -> 104 us
  matrix products: 162 us -> 108 us
  local copies, waits for them, and re-layouts: 49.5 us -> 77.7 us
    ppermute x58 -> x60, waiting for transfers between devices: 210 us -> 138 us  [swap(): return lax.ppermute(tensor, 'head', [(at, at ^ bit) for at in range(size)])]
    pallas_call x0 -> x14, Pallas kernels: none -> 70.8 us  [the longest x8 55.6 us: cross(): pl.pallas_call(functools.partial(cross_kernel, [len(group) for group in g...]
    dot_general x35 -> x41, matrix products: 162 us -> 108 us  [mm(): lax.dot_general(left, right, (dims, ((), ())), preferred_element_type=out)]
    reduce_scatter x4, waiting for transfers between devices: 69 us -> 30.4 us  [the longest x1 30.4 us: per_device(): lax.psum_scatter(proj_pair, 'dp', scatter_dimension=0, tiled=True)]
    unnamed x151 -> x309, local copies, waits for them, and re-layouts: 23.3 us -> 61.6 us
    all_gather x2, waiting for transfers between devices: 6.68 us -> 0.01 us  [the longest x1 0.01 us: per_device(): gate_up = lax.all_gather(jnp.stack(gate_up), 'dp', axis=1, tiled=True)]
    ppermute x58 -> x60, starting transfers between devices: 51.3 us -> 52.7 us  [swap(): return lax.ppermute(tensor, 'head', [(at, at ^ bit) for at in range(size)])]
  transfers between devices with their start and end apart: 70 -> 72, of which waited for: 30 -> 27; matrix products, arithmetic and copies ran while one was open for 30% -> 27% of each run, Pallas kernels for 5% -> 18%
where the time goes in v2:
time: 580 us; the launch traced here: 575 us
  waiting for transfers between devices  169 us (29%)
  matrix products  108 us (19%)
  Pallas kernels  104 us (18%)
  local copies, waits for them, and re-layouts  77.7 us (13%)
  starting transfers between devices  62.1 us (11%)
  other arithmetic  37.6 us (6%)
  between operations  16.5 us (3%)
    ppermute x60, waiting for transfers between devices, swap(): return lax.ppermute(tensor, 'head', [(at, at ^ bit) for at in range(size)])  138 us
    dot_general x41, matrix products, mm(): lax.dot_general(left, right, (dims, ((), ())), preferred_element_type=out)  108 us
    unnamed x309, local copies, waits for them, and re-layouts  61.6 us
    pallas_call x8, Pallas kernels, cross(): pl.pallas_call(functools.partial(cross_kernel, [len(group) for group in g...  55.6 us
    ppermute x60, starting transfers between devices, swap(): return lax.ppermute(tensor, 'head', [(at, at ^ bit) for at in range(size)])  52.7 us
    reduce_scatter x1, waiting for transfers between devices, per_device(): lax.psum_scatter(proj_pair, 'dp', scatter_dimension=0, tiled=True)  30.4 us
    pallas_call x1, Pallas kernels, recurrence_back(): pl.pallas_call(functools.partial(backward_kernel, blocks, half_heads), ou...  17.2 us
    pallas_call x1, Pallas kernels, recurrence(): pl.pallas_call(functools.partial(forward_kernel, blocks, half_heads), out...  15.7 us
  transfers between devices with their start and end apart: 72, of which 27 were waited for; matrix products, arithmetic and copies ran while one was open for 27% of the time, Pallas kernels for 18%

profile of v2, /device:TPU:0, one launch (start us, length us, event | category | flops | bytes accessed | tf_op | source)
XLA Modules:
  0.0 575.3 jit_solution(18038032213394204748)
XLA Ops:
  7.3 3.9 pad_maximum_fusion
  13.2 2.6 collective-permute-start.5
  23.6 4.7 collective-permute-done.5.refs_5_
  33.3 2.8 constant_dynamic-update-slice_fusion
  45.7 7.1 %collective-permute-done.7.refs_7_ = bf16[128,2048]{1,0:T(8,128)(2,1)S(1)} collective-permute-done((bf16[128,2048]{1,0:T(8,128)(2,1)S(1)}, bf16[128,2048]{1,0:T(8,128)(2,1)S(1)}, u32[]{:S(2)}, u32[]{:S(2)}) %collective-permute-start.7) | collective-permute-done | bytes 524320 | tf_op jit(solution)/shard_map/ppermute | solution.py:17
  58.8 14.4 %convolution_dynamic-update-slice_fusion.proj_ref = f32[1024,2048]{1,0:T(8,128)S(1)} fusion(f32[1024,2048]{1,0:T(8,128)S(1)} %convolution_dynamic-update-slice_fusion.1, bf16[128,2048]{1,0:T(8,128)(2,1)S(1)} %collective-permute-done.7.refs_7_, bf16[2048,2048]{1,0:T(8,128)(2,1)S(1)} %constant_dynamic-update-slice_fusion), kind=kOutput, calls=%fused_computation.21 | convolution fusion | flops 1073741824 | bytes 9961472 | tf_op jit(solution)/shard_map/dot_general | solution.py:21
  73.2 15.7 %shard_map.254 = (bf16[1024,512]{1,0:T(8,128)(2,1)S(1)}, f32[1024,512]{1,0:T(8,128)S(1)}, f32[8,4,128,128]{3,2,1,0:T(8,128)S(1)}, bf16[8,4,128,128]{3,2,1,0:T(8,128)(2,1)S(1)}) custom-call(s32[17]{0:T(128)S(1)} %pad_add_fusion.info, f32[1024,2048]{1,0:T(8,128)S(1)} %convolution_dynamic-update-slice_fusion.proj_ref, ...), custom_call_target="tpu_custom_call" | custom-call | tf_op jit(solution)/shard_map/pallas_call | solution.py:255
  99.3 9.0 %collective-permute-done.17 = bf16[128,2048]{1,0:T(8,128)(2,1)S(1)} collective-permute-done((bf16[128,2048]{1,0:T(8,128)(2,1)S(1)}, bf16[128,2048]{1,0:T(8,128)(2,1)S(1)}, u32[]{:S(2)}, u32[]{:S(2)}) %collective-permute-start.17) | collective-permute-done | bytes 524320 | tf_op jit(solution)/shard_map/ppermute | solution.py:17
  109.7 9.0 %collective-permute-done.15 = bf16[128,2048]{1,0:T(8,128)(2,1)S(1)} collective-permute-done((bf16[128,2048]{1,0:T(8,128)(2,1)S(1)}, bf16[128,2048]{1,0:T(8,128)(2,1)S(1)}, u32[]{:S(2)}, u32[]{:S(2)}) %collective-permute-start.15) | collective-permute-done | bytes 524320 | tf_op jit(solution)/shard_map/ppermute | solution.py:17
  122.9 10.1 %collective-permute-done.18 = bf16[128,2048]{1,0:T(8,128)(2,1)S(1)} collective-permute-done((bf16[128,2048]{1,0:T(8,128)(2,1)S(1)}, bf16[128,2048]{1,0:T(8,128)(2,1)S(1)}, u32[]{:S(2)}, u32[]{:S(2)}) %collective-permute-start.18) | collective-permute-done | bytes 524320 | tf_op jit(solution)/shard_map/ppermute | solution.py:17
  140.5 22.7 %collective-permute-done.21.refs_10_ = bf16[256,2048]{1,0:T(8,128)(2,1)} collective-permute-done((bf16[256,2048]{1,0:T(8,128)(2,1)}, bf16[256,2048]{1,0:T(8,128)(2,1)}, u32[]{:S(2)}, u32[]{:S(2)}) %collective-permute-start.21) | collective-permute-done | bytes 1048608 | tf_op jit(solution)/shard_map/ppermute | solution.py:17
  170.9 2.7 copy-done.36
  173.6 3.0 shard_map.255
  178.4 3.3 multiply_convert_fusion.12
  181.7 3.4 fusion.51
  185.1 4.9 multiply_convert_fusion.11
  190.0 3.4 fusion.52
  193.4 4.9 multiply_convert_fusion.10
  200.4 3.5 multiply_convert_fusion.9
  204.0 6.3 %shard_map.256 = bf16[1,704,2048]{2,1,0:T(8,128)(2,1)S(1)} custom-call(bf16[256,1408]{1,0:T(8,128)(2,1)S(1)} %get-tuple-element.268.refs_0_, bf16[256,1408]{1,0:T(8,128)(2,1)S(1)} %get-tuple-element.270.refs_1_, bf16[256,1408]{1,0:T(8,128)(2,1)S(1)} %get-tuple-element.271.refs_2_, bf16[256,1408]{1,0:T(8,128)(2,1)S(1)} %get-tuple-element.269.refs_3_, ...), custom_call_target="tpu_custom_call" | custom-call | tf_op jit(solution)/shard_map/pallas_call | solution.py:444
  223.9 6.1 %shard_map.257 = bf16[1,704,2048]{2,1,0:T(8,128)(2,1)S(1)} custom-call(bf16[256,1408]{1,0:T(8,128)(2,1)S(1)} %copy-done.49, bf16[256,1408]{1,0:T(8,128)(2,1)S(1)} %copy-done.55, bf16[256,1408]{1,0:T(8,128)(2,1)S(1)} %copy-done.52, bf16[256,1408]{1,0:T(8,128)(2,1)S(1)} %copy-done.58, bf16[256,2048]{1,0:T(8,128)(2,1)S(1)} %pad_maximum_fusion.4.refs_4_, ...), custom_call_target="tpu_custom_call" | custom-call | tf_op jit(solution)/shard_map/pallas_call | solution.py:444
  236.7 6.4 %multiply_convert_fusion.8 = (bf16[256,1408]{1,0:T(8,128)(2,1)S(1)}, bf16[256,1408]{1,0:T(8,128)(2,1)S(1)}) fusion(f32[256,1408]{1,0:T(8,128)S(1)} %copy-done.136, f32[256,1408]{1,0:T(8,128)} %get-tuple-element.353, bf16[1408,2048]{1,0:T(8,128)(2,1)S(1)} %shard_map.259, bf16[128,2048]{1,0:T(8,128)(2,1)S(1)} %copy-done.82, bf16[128,2048]{1,0:T(8,128)(2,1)S(1)} %copy-done.85), kind=kOutput, calls=%fused_computation.69 | convolution fusion | flops 1483177984 | bytes 11141120 | tf_op jit(solution)/shard_map/dot_general | solution.py:21
  256.7 3.7 multiply_convert_fusion.4
  265.6 4.1 multiply_convert_fusion.2
  271.6 2.8 fusion.3
  274.6 12.3 %shard_map.260 = bf16[2,704,2048]{2,1,0:T(8,128)(2,1)S(1)} custom-call(bf16[256,1408]{1,0:T(8,128)(2,1)S(1)} %get-tuple-element.230.refs_0_, bf16[256,1408]{1,0:T(8,128)(2,1)S(1)} %get-tuple-element.231.refs_1_, bf16[256,1408]{1,0:T(8,128)(2,1)S(1)} %get-tuple-element.232.refs_2_, bf16[256,1408]{1,0:T(8,128)(2,1)S(1)} %get-tuple-element.233.refs_3_, ...), custom_call_target="tpu_custom_call" | custom-call | tf_op jit(solution)/shard_map/pallas_call | solution.py:444
  289.4 2.7 add_convert_fusion.4
  306.7 11.3 %shard_map.261 = bf16[2,704,2048]{2,1,0:T(8,128)(2,1)S(1)} custom-call(bf16[256,1408]{1,0:T(8,128)(2,1)S(1)} %copy-done.73, bf16[256,1408]{1,0:T(8,128)(2,1)S(1)} %copy-done.65, bf16[256,1408]{1,0:T(8,128)(2,1)S(1)} %copy-done.69, bf16[256,1408]{1,0:T(8,128)(2,1)S(1)} %copy-done.61, bf16[256,1408]{1,0:T(8,128)(2,1)S(1)} %copy-done.75, ...), custom_call_target="tpu_custom_call" | custom-call | tf_op jit(solution)/shard_map/pallas_call | solution.py:444
  329.1 23.1 %collective-permute-done.37.refs_3_ = bf16[256,2048]{1,0:T(8,128)(2,1)S(1)} collective-permute-done((bf16[256,2048]{1,0:T(8,128)(2,1)S(1)}, bf16[256,2048]{1,0:T(8,128)(2,1)S(1)}, u32[]{:S(2)}, u32[]{:S(2)}) %collective-permute-start.37) | collective-permute-done | bytes 1048608 | tf_op jit(solution)/shard_map/ppermute | solution.py:17
  354.5 10.8 %collective-permute-done.39.refs_5_ = bf16[128,2048]{1,0:T(8,128)(2,1)S(1)} collective-permute-done((bf16[128,2048]{1,0:T(8,128)(2,1)S(1)}, bf16[128,2048]{1,0:T(8,128)(2,1)S(1)}, u32[]{:S(2)}, u32[]{:S(2)}) %collective-permute-start.39) | collective-permute-done | bytes 524320 | tf_op jit(solution)/shard_map/ppermute | solution.py:17
  366.0 3.4 shard_map.263
  369.5 2.7 shard_map.264
  378.3 17.2 %shard_map.265 = (bf16[1024,2048]{1,0:T(8,128)(2,1)S(1)}, f32[1,512]{1,0:T(1,128)S(1)}, f32[1,512]{1,0:T(1,128)S(1)}) custom-call(s32[17]{0:T(128)S(1)} %pad_add_fusion.info, f32[1024,2048]{1,0:T(8,128)S(1)} %bitcast.140, f32[1,512]{1,0:T(1,128)S(1)} %get-tuple-element.343.floor_ref, f32[1,512]{1,0:T(1,128)S(1)} %get-tuple-element.342.gain_ref, ...), custom_call_target="tpu_custom_call" | custom-call | tf_op jit(solution)/shard_map/pallas_call | solution.py:294
  407.2 3.3 convolution_convert_fusion.8
  410.6 7.3 %shard_map.266 = bf16[1,2048,1024]{2,1,0:T(8,128)(2,1)} custom-call(bf16[128,2048]{1,0:T(8,128)(2,1)S(1)} %get-tuple-element.152.refs_0_, bf16[128,2048]{1,0:T(8,128)(2,1)S(1)} %copy-done.24, bf16[128,2048]{1,0:T(8,128)(2,1)S(1)} %collective-permute-done.2.refs_2_, bf16[128,2048]{1,0:T(8,128)(2,1)S(1)} %copy-done.26, bf16[128,2048]{1,0:T(8,128)(2,1)S(1)} %copy-done.28, ...), custom_call_target="tpu_custom_call" | custom-call | tf_op jit(solution)/shard_map/pallas_call | solution.py:444
  418.0 3.8 collective-permute-done.42
  426.7 4.3 collective-permute-done.56
  431.0 3.6 collective-permute-start.59
  438.9 6.2 %shard_map.267 = bf16[1,2048,1024]{2,1,0:T(8,128)(2,1)S(1)} custom-call(bf16[128,2048]{1,0:T(8,128)(2,1)S(1)} %get-tuple-element.152.refs_0_, bf16[128,2048]{1,0:T(8,128)(2,1)S(1)} %copy-done.24, bf16[128,2048]{1,0:T(8,128)(2,1)S(1)} %collective-permute-done.2.refs_2_, bf16[128,2048]{1,0:T(8,128)(2,1)S(1)} %copy-done.26, bf16[128,2048]{1,0:T(8,128)(2,1)S(1)} %copy-done.28, ...), custom_call_target="tpu_custom_call" | custom-call | tf_op jit(solution)/shard_map/pallas_call | solution.py:444
  452.9 5.2 shard_map.268
  472.3 4.7 convolution_convert_fusion.6
  485.0 10.4 %collective-permute-done.61 = f32[2,2048]{1,0:T(2,128)S(1)} collective-permute-done((f32[2,2048]{1,0:T(2,128)S(1)}, f32[2,2048]{1,0:T(2,128)S(1)}, u32[]{:S(2)}, u32[]{:S(2)}) %collective-permute-start.61) | collective-permute-done | bytes 16416 | tf_op jit(solution)/shard_map/ppermute | solution.py:17
  498.5 5.9 %collective-permute-done.62 = f32[2,2048]{1,0:T(2,128)S(1)} collective-permute-done((f32[2,2048]{1,0:T(2,128)S(1)}, f32[2,2048]{1,0:T(2,128)S(1)}, u32[]{:S(2)}, u32[]{:S(2)}) %collective-permute-start.62) | collective-permute-done | bytes 16416 | tf_op jit(solution)/shard_map/ppermute | solution.py:17
  504.4 3.1 collective-permute-start.65
  515.1 6.1 %collective-permute-done.50 = bf16[128,2048]{1,0:T(8,128)(2,1)} collective-permute-done((bf16[128,2048]{1,0:T(8,128)(2,1)}, bf16[128,2048]{1,0:T(8,128)(2,1)}, u32[]{:S(2)}, u32[]{:S(2)}) %collective-permute-start.50) | collective-permute-done | bytes 524320 | tf_op jit(solution)/shard_map/ppermute | solution.py:17
  526.5 3.3 maximum_select_fusion
  535.3 30.4 %reduce-scatter.9.cloned.1.call-done = bf16[512,1024]{1,0:T(8,128)(2,1)} async-done(((bf16[2048,1024]{1,0:T(8,128)(2,1)}), bf16[512,1024]{1,0:T(8,128)(2,1)}) %reduce-scatter.9.cloned.1.call-update) | async-done | bytes 1048592 | tf_op jit(solution)/shard_map/reduce_scatter | solution.py:680
  565.7 2.5 fusion.42
  (564 shorter events, 214.5 us)
Async XLA Ops:
  7.2 130.0 %all-gather.3.cloned.1.call-start = ((), (), s32[]{:S(2)}) async-start(), calls=%async_computation.4 | async-start | bytes 7208960 | tf_op jit(solution)/shard_map/all_gather | solution.py:533
  11.1 22.1 %collective-permute-start = (bf16[2048,1024]{1,0:T(8,128)(2,1)}, bf16[2048,1024]{1,0:T(8,128)(2,1)}, u32[]{:S(2)}, u32[]{:S(2)}) collective-permute-start(bf16[2048,1024]{1,0:T(8,128)(2,1)} %pad_maximum_fusion), channel_id=1, source_target_pairs={{0,4},{4,0},{8,12},{12,8},{16,20},{20,16},{24,28},{28,24},{1,5},{5... | collective-permute-start | bytes 12582920 | tf_op jit(solution)/shard_map/ppermute | solution.py:17
  19.2 195.2 %all-gather.5.cloned.1.call-start = ((), (), s32[]{:S(2)}) async-start(), calls=%async_computation.5 | async-start | bytes 3604480 | tf_op jit(solution)/shard_map/all_gather | solution.py:534
  23.0 18.6 %collective-permute-start.3 = (bf16[128,2048]{1,0:T(8,128)(2,1)}, bf16[128,2048]{1,0:T(8,128)(2,1)S(1)}, u32[]{:S(2)}, u32[]{:S(2)}) collective-permute-start(bf16[128,2048]{1,0:T(8,128)(2,1)} %get-tuple-element.153), channel_id=1, source_target_pairs={{0,12},{4,8},{8,4},{12,0},{16,28},{20,24},{24,20},{28,16},{1,13},{... | collective-permute-start | bytes 1572872 | tf_op jit(solution)/shard_map/ppermute | solution.py:17
  31.2 21.6 %collective-permute-start.7 = (bf16[128,2048]{1,0:T(8,128)(2,1)S(1)}, bf16[128,2048]{1,0:T(8,128)(2,1)S(1)}, u32[]{:S(2)}, u32[]{:S(2)}) collective-permute-start(bf16[128,2048]{1,0:T(8,128)(2,1)S(1)} %collective-permute-done.5.refs_5_), channel_id=1, source_target_pairs={{0,8},{4,12},{8,0},{12,4},{16,24},{20,28},{24,16},{28,20},{1,9},{5... | collective-permute-start | bytes 1572872 | tf_op jit(solution)/shard_map/ppermute | solution.py:17
  32.7 21.0 %collective-permute-start.6 = (bf16[128,2048]{1,0:T(8,128)(2,1)S(1)}, bf16[128,2048]{1,0:T(8,128)(2,1)S(1)}, u32[]{:S(2)}, u32[]{:S(2)}) collective-permute-start(bf16[128,2048]{1,0:T(8,128)(2,1)S(1)} %collective-permute-done.2.refs_2_), channel_id=1, source_target_pairs={{0,16},{4,20},{8,24},{12,28},{16,0},{20,4},{24,8},{28,12},{1,17},{... | collective-permute-start | bytes 1572872 | tf_op jit(solution)/shard_map/ppermute | solution.py:17
  53.7 38.4 %collective-permute-start.11 = (bf16[256,2048]{1,0:T(8,128)(2,1)S(1)}, bf16[256,2048]{1,0:T(8,128)(2,1)S(1)}, u32[]{:S(2)}, u32[]{:S(2)}) collective-permute-start(bf16[256,2048]{1,0:T(8,128)(2,1)S(1)} %pad_maximum_fusion.4.refs_4_), channel_id=1, source_target_pairs={{0,16},{4,20},{8,24},{12,28},{16,0},{20,4},{24,8},{28,12},{1,17},{... | collective-permute-start | bytes 3145736 | tf_op jit(solution)/shard_map/ppermute | solution.py:17
  55.3 36.8 %collective-permute-start.10 = (bf16[256,2048]{1,0:T(8,128)(2,1)S(1)}, bf16[256,2048]{1,0:T(8,128)(2,1)S(1)}, u32[]{:S(2)}, u32[]{:S(2)}) collective-permute-start(bf16[256,2048]{1,0:T(8,128)(2,1)S(1)} %pad_maximum_fusion.4.refs_4_), channel_id=1, source_target_pairs={{0,8},{4,12},{8,0},{12,4},{16,24},{20,28},{24,16},{28,20},{1,9},{5... | collective-permute-start | bytes 3145736 | tf_op jit(solution)/shard_map/ppermute | solution.py:17
  56.9 34.4 %collective-permute-start.12 = (bf16[128,2048]{1,0:T(8,128)(2,1)S(1)}, bf16[128,2048]{1,0:T(8,128)(2,1)S(1)}, u32[]{:S(2)}, u32[]{:S(2)}) collective-permute-start(bf16[128,2048]{1,0:T(8,128)(2,1)S(1)} %get-tuple-element.335), channel_id=1, source_target_pairs={{0,4},{4,0},{8,12},{12,8},{16,20},{20,16},{24,28},{28,24},{1,5},{5... | collective-permute-start | bytes 1572872 | tf_op jit(solution)/shard_map/ppermute | solution.py:17
  57.0 35.1 %collective-permute-start.13 = (bf16[256,2048]{1,0:T(8,128)(2,1)S(1)}, bf16[256,2048]{1,0:T(8,128)(2,1)S(1)}, u32[]{:S(2)}, u32[]{:S(2)}) collective-permute-start(bf16[256,2048]{1,0:T(8,128)(2,1)S(1)} %copy-done.114), channel_id=1, source_target_pairs={{0,4},{4,0},{8,12},{12,8},{16,20},{20,16},{24,28},{28,24},{1,5},{5... | collective-permute-start | bytes 3145736 | tf_op jit(solution)/shard_map/ppermute | solution.py:17
  96.1 22.6 %collective-permute-start.15 = (bf16[128,2048]{1,0:T(8,128)(2,1)S(1)}, bf16[128,2048]{1,0:T(8,128)(2,1)S(1)}, u32[]{:S(2)}, u32[]{:S(2)}) collective-permute-start(bf16[128,2048]{1,0:T(8,128)(2,1)S(1)} %get-tuple-element.332), channel_id=1, source_target_pairs={{0,16},{4,20},{8,24},{12,28},{16,0},{20,4},{24,8},{28,12},{1,17},{... | collective-permute-start | bytes 1572872 | tf_op jit(solution)/shard_map/ppermute | solution.py:17
  97.8 22.0 %collective-permute-start.14 = (bf16[128,2048]{1,0:T(8,128)(2,1)S(1)}, bf16[128,2048]{1,0:T(8,128)(2,1)S(1)}, u32[]{:S(2)}, u32[]{:S(2)}) collective-permute-start(bf16[128,2048]{1,0:T(8,128)(2,1)S(1)} %get-tuple-element.333), channel_id=1, source_target_pairs={{0,8},{4,12},{8,0},{12,4},{16,24},{20,28},{24,16},{28,20},{1,9},{5... | collective-permute-start | bytes 1572872 | tf_op jit(solution)/shard_map/ppermute | solution.py:17
  137.2 33.7 %collective-permute-start.22 = (bf16[2,704,2048]{2,1,0:T(8,128)(2,1)}, bf16[2,704,2048]{2,1,0:T(8,128)(2,1)}, u32[]{:S(2)}, u32[]{:S(2)}) collective-permute-start(bf16[2,704,2048]{2,1,0:T(8,128)(2,1)} %all-gather.3.cloned.1.call-done.own), channel_id=1, source_target_pairs={{0,4},{4,0},{8,12},{12,8},{16,20},{20,16},{24,28},{28,24},{1,5},{5... | collective-permute-start | bytes 17301512 | tf_op jit(solution)/shard_map/ppermute | solution.py:17
  137.2 25.9 %collective-permute-start.21 = (bf16[256,2048]{1,0:T(8,128)(2,1)}, bf16[256,2048]{1,0:T(8,128)(2,1)}, u32[]{:S(2)}, u32[]{:S(2)}) collective-permute-start(bf16[256,2048]{1,0:T(8,128)(2,1)} %multiply_convert_fusion.refs_8_), channel_id=1, source_target_pairs={{0,16},{4,20},{8,24},{12,28},{16,0},{20,4},{24,8},{28,12},{1,17},{... | collective-permute-start | bytes 3145736 | tf_op jit(solution)/shard_map/ppermute | solution.py:17
  138.9 25.6 %collective-permute-start.20 = (bf16[256,2048]{1,0:T(8,128)(2,1)}, bf16[256,2048]{1,0:T(8,128)(2,1)}, u32[]{:S(2)}, u32[]{:S(2)}) collective-permute-start(bf16[256,2048]{1,0:T(8,128)(2,1)} %multiply_convert_fusion.refs_8_), channel_id=1, source_target_pairs={{0,8},{4,12},{8,0},{12,4},{16,24},{20,28},{24,16},{28,20},{1,9},{5... | collective-permute-start | bytes 3145736 | tf_op jit(solution)/shard_map/ppermute | solution.py:17
  140.4 151.7 %reduce-scatter.5.cloned.1.call-start = ((), (), s32[]{:S(2)}) async-start(), calls=%async_computation.6 | async-start | bytes 3604480 | tf_op jit(solution)/shard_map/reduce_scatter | solution.py:606
  166.8 37.1 %collective-permute-start.26 = (bf16[128,2048]{1,0:T(8,128)(2,1)S(1)}, bf16[128,2048]{1,0:T(8,128)(2,1)S(1)}, u32[]{:S(2)}, u32[]{:S(2)}) collective-permute-start(bf16[128,2048]{1,0:T(8,128)(2,1)S(1)} %slice.231), channel_id=1, source_target_pairs={{0,8},{4,12},{8,0},{12,4},{16,24},{20,28},{24,16},{28,20},{1,9},{5... | collective-permute-start | bytes 1572872 | tf_op jit(solution)/shard_map/ppermute | solution.py:17
  168.4 35.6 %collective-permute-start.25 = (bf16[128,2048]{1,0:T(8,128)(2,1)S(1)}, bf16[128,2048]{1,0:T(8,128)(2,1)S(1)}, u32[]{:S(2)}, u32[]{:S(2)}) collective-permute-start(bf16[128,2048]{1,0:T(8,128)(2,1)S(1)} %slice.230), channel_id=1, source_target_pairs={{0,16},{4,20},{8,24},{12,28},{16,0},{20,4},{24,8},{28,12},{1,17},{... | collective-permute-start | bytes 1572872 | tf_op jit(solution)/shard_map/ppermute | solution.py:17
  168.9 29.5 %collective-permute-start.24 = (bf16[128,2048]{1,0:T(8,128)(2,1)S(1)}, bf16[128,2048]{1,0:T(8,128)(2,1)S(1)}, u32[]{:S(2)}, u32[]{:S(2)}) collective-permute-start(bf16[128,2048]{1,0:T(8,128)(2,1)S(1)} %slice.229), channel_id=1, source_target_pairs={{0,8},{4,12},{8,0},{12,4},{16,24},{20,28},{24,16},{28,20},{1,9},{5... | collective-permute-start | bytes 1572872 | tf_op jit(solution)/shard_map/ppermute | solution.py:17
  169.3 29.1 %collective-permute-start.23 = (bf16[128,2048]{1,0:T(8,128)(2,1)S(1)}, bf16[128,2048]{1,0:T(8,128)(2,1)S(1)}, u32[]{:S(2)}, u32[]{:S(2)}) collective-permute-start(bf16[128,2048]{1,0:T(8,128)(2,1)S(1)} %slice.228), channel_id=1, source_target_pairs={{0,16},{4,20},{8,24},{12,28},{16,0},{20,4},{24,8},{28,12},{1,17},{... | collective-permute-start | bytes 1572872 | tf_op jit(solution)/shard_map/ppermute | solution.py:17
  214.4 17.9 %collective-permute-start.28 = (bf16[704,2048]{1,0:T(8,128)(2,1)}, bf16[704,2048]{1,0:T(8,128)(2,1)}, u32[]{:S(2)}, u32[]{:S(2)}) collective-permute-start(bf16[704,2048]{1,0:T(8,128)(2,1)} %all-gather.5.cloned.1.call-done), channel_id=1, source_target_pairs={{0,4},{4,0},{8,12},{12,8},{16,20},{20,16},{24,28},{28,24},{1,5},{5... | collective-permute-start | bytes 8650760 | tf_op jit(solution)/shard_map/ppermute | solution.py:17
  232.3 227.8 %reduce-scatter.7.cloned.1.call-start = ((), (), s32[]{:S(2)}) async-start(), calls=%async_computation.7 | async-start | bytes 7208960 | tf_op jit(solution)/shard_map/reduce_scatter | solution.py:638
  247.9 41.5 %collective-permute-start.30 = (bf16[128,2048]{1,0:T(8,128)(2,1)}, bf16[128,2048]{1,0:T(8,128)(2,1)S(1)}, u32[]{:S(2)}, u32[]{:S(2)}) collective-permute-start(bf16[128,2048]{1,0:T(8,128)(2,1)} %get-tuple-element.328), channel_id=1, source_target_pairs={{0,16},{4,20},{8,24},{12,28},{16,0},{20,4},{24,8},{28,12},{1,17},{... | collective-permute-start | bytes 1572872 | tf_op jit(solution)/shard_map/ppermute | solution.py:17
  248.6 40.8 %collective-permute-start.29 = (bf16[128,2048]{1,0:T(8,128)(2,1)}, bf16[128,2048]{1,0:T(8,128)(2,1)}, u32[]{:S(2)}, u32[]{:S(2)}) collective-permute-start(bf16[128,2048]{1,0:T(8,128)(2,1)} %get-tuple-element.329), channel_id=1, source_target_pairs={{0,8},{4,12},{8,0},{12,4},{16,24},{20,28},{24,16},{28,20},{1,9},{5... | collective-permute-start | bytes 1572872 | tf_op jit(solution)/shard_map/ppermute | solution.py:17
  256.1 33.2 %collective-permute-start.31 = (bf16[128,2048]{1,0:T(8,128)(2,1)S(1)}, bf16[128,2048]{1,0:T(8,128)(2,1)S(1)}, u32[]{:S(2)}, u32[]{:S(2)}) collective-permute-start(bf16[128,2048]{1,0:T(8,128)(2,1)S(1)} %slice.291), channel_id=1, source_target_pairs={{0,8},{4,12},{8,0},{12,4},{16,24},{20,28},{24,16},{28,20},{1,9},{5... | collective-permute-start | bytes 1572872 | tf_op jit(solution)/shard_map/ppermute | solution.py:17
  264.2 25.2 %collective-permute-start.32 = (bf16[128,2048]{1,0:T(8,128)(2,1)S(1)}, bf16[128,2048]{1,0:T(8,128)(2,1)S(1)}, u32[]{:S(2)}, u32[]{:S(2)}) collective-permute-start(bf16[128,2048]{1,0:T(8,128)(2,1)S(1)} %slice.292), channel_id=1, source_target_pairs={{0,16},{4,20},{8,24},{12,28},{16,0},{20,4},{24,8},{28,12},{1,17},{... | collective-permute-start | bytes 1572872 | tf_op jit(solution)/shard_map/ppermute | solution.py:17
  292.1 25.9 %collective-permute-start.35 = (bf16[2,704,2048]{2,1,0:T(8,128)(2,1)}, bf16[2,704,2048]{2,1,0:T(8,128)(2,1)S(1)}, u32[]{:S(2)}, u32[]{:S(2)}) collective-permute-start(bf16[2,704,2048]{2,1,0:T(8,128)(2,1)} %copy-done.37), channel_id=1, source_target_pairs={{0,4},{4,0},{8,12},{12,8},{16,20},{20,16},{24,28},{28,24},{1,5},{5... | collective-permute-start | bytes 17301512 | tf_op jit(solution)/shard_map/ppermute | solution.py:17
  292.2 29.8 %collective-permute-start.33 = (bf16[128,2048]{1,0:T(8,128)(2,1)}, bf16[128,2048]{1,0:T(8,128)(2,1)}, u32[]{:S(2)}, u32[]{:S(2)}) collective-permute-start(bf16[128,2048]{1,0:T(8,128)(2,1)} %get-tuple-element.218), channel_id=1, source_target_pairs={{0,8},{4,12},{8,0},{12,4},{16,24},{20,28},{24,16},{28,20},{1,9},{5... | collective-permute-start | bytes 1572872 | tf_op jit(solution)/shard_map/ppermute | solution.py:17
  293.7 28.2 %collective-permute-start.34 = (bf16[128,2048]{1,0:T(8,128)(2,1)}, bf16[128,2048]{1,0:T(8,128)(2,1)}, u32[]{:S(2)}, u32[]{:S(2)}) collective-permute-start(bf16[128,2048]{1,0:T(8,128)(2,1)} %get-tuple-element.219), channel_id=1, source_target_pairs={{0,16},{4,20},{8,24},{12,28},{16,0},{20,4},{24,8},{28,12},{1,17},{... | collective-permute-start | bytes 1572872 | tf_op jit(solution)/shard_map/ppermute | solution.py:17
  322.0 211.5 %reduce-scatter.11.cloned.1.call-start = ((), (), s32[]{:S(2)}) async-start(), calls=%async_computation.9 | async-start | bytes 1310720 | tf_op jit(solution)/shard_map/reduce_scatter | solution.py:679
  327.3 25.0 %collective-permute-start.37 = (bf16[256,2048]{1,0:T(8,128)(2,1)S(1)}, bf16[256,2048]{1,0:T(8,128)(2,1)S(1)}, u32[]{:S(2)}, u32[]{:S(2)}) collective-permute-start(bf16[256,2048]{1,0:T(8,128)(2,1)S(1)} %get-tuple-element.295.refs_1_), channel_id=1, source_target_pairs={{0,16},{4,20},{8,24},{12,28},{16,0},{20,4},{24,8},{28,12},{1,17},{... | collective-permute-start | bytes 3145736 | tf_op jit(solution)/shard_map/ppermute | solution.py:17
  328.6 24.7 %collective-permute-start.36 = (bf16[256,2048]{1,0:T(8,128)(2,1)S(1)}, bf16[256,2048]{1,0:T(8,128)(2,1)S(1)}, u32[]{:S(2)}, u32[]{:S(2)}) collective-permute-start(bf16[256,2048]{1,0:T(8,128)(2,1)S(1)} %get-tuple-element.295.refs_1_), channel_id=1, source_target_pairs={{0,8},{4,12},{8,0},{12,4},{16,24},{20,28},{24,16},{28,20},{1,9},{5... | collective-permute-start | bytes 3145736 | tf_op jit(solution)/shard_map/ppermute | solution.py:17
  398.1 19.9 %collective-permute-start.41 = (bf16[128,2048]{1,0:T(8,128)(2,1)S(1)}, bf16[128,2048]{1,0:T(8,128)(2,1)S(1)}, u32[]{:S(2)}, u32[]{:S(2)}) collective-permute-start(bf16[128,2048]{1,0:T(8,128)(2,1)S(1)} %get-tuple-element.324), channel_id=1, source_target_pairs={{0,16},{4,20},{8,24},{12,28},{16,0},{20,4},{24,8},{28,12},{1,17},{... | collective-permute-start | bytes 1572872 | tf_op jit(solution)/shard_map/ppermute | solution.py:17
  399.1 18.9 %collective-permute-start.40 = (bf16[128,2048]{1,0:T(8,128)(2,1)S(1)}, bf16[128,2048]{1,0:T(8,128)(2,1)S(1)}, u32[]{:S(2)}, u32[]{:S(2)}) collective-permute-start(bf16[128,2048]{1,0:T(8,128)(2,1)S(1)} %get-tuple-element.325), channel_id=1, source_target_pairs={{0,8},{4,12},{8,0},{12,4},{16,24},{20,28},{24,16},{28,20},{1,9},{5... | collective-permute-start | bytes 1572872 | tf_op jit(solution)/shard_map/ppermute | solution.py:17
  403.0 18.7 %collective-permute-start.42 = (bf16[128,2048]{1,0:T(8,128)(2,1)S(1)}, bf16[128,2048]{1,0:T(8,128)(2,1)S(1)}, u32[]{:S(2)}, u32[]{:S(2)}) collective-permute-start(bf16[128,2048]{1,0:T(8,128)(2,1)S(1)} %slice.249), channel_id=1, source_target_pairs={{0,8},{4,12},{8,0},{12,4},{16,24},{20,28},{24,16},{28,20},{1,9},{5... | collective-permute-start | bytes 1572872 | tf_op jit(solution)/shard_map/ppermute | solution.py:17
  423.8 26.9 %collective-permute-start.54 = (bf16[2048,1024]{1,0:T(8,128)(2,1)}, bf16[2048,1024]{1,0:T(8,128)(2,1)}, u32[]{:S(2)}, u32[]{:S(2)}) collective-permute-start(bf16[2048,1024]{1,0:T(8,128)(2,1)} %bitcast.28), channel_id=1, source_target_pairs={{0,4},{4,0},{8,12},{12,8},{16,20},{20,16},{24,28},{28,24},{1,5},{5... | collective-permute-start | bytes 12582920 | tf_op jit(solution)/shard_map/ppermute | solution.py:17
  423.8 24.4 %collective-permute-start.55 = (bf16[256,2048]{1,0:T(8,128)(2,1)}, bf16[256,2048]{1,0:T(8,128)(2,1)}, u32[]{:S(2)}, u32[]{:S(2)}) collective-permute-start(bf16[256,2048]{1,0:T(8,128)(2,1)} %bitcast.30), channel_id=1, source_target_pairs={{0,4},{4,0},{8,12},{12,8},{16,20},{20,16},{24,28},{28,24},{1,5},{5... | collective-permute-start | bytes 3145736 | tf_op jit(solution)/shard_map/ppermute | solution.py:17
  424.3 22.7 %collective-permute-start.44 = (bf16[128,2048]{1,0:T(8,128)(2,1)}, bf16[128,2048]{1,0:T(8,128)(2,1)}, u32[]{:S(2)}, u32[]{:S(2)}) collective-permute-start(bf16[128,2048]{1,0:T(8,128)(2,1)} %add_convert_fusion.3), channel_id=1, source_target_pairs={{0,8},{4,12},{8,0},{12,4},{16,24},{20,28},{24,16},{28,20},{1,9},{5... | collective-permute-start | bytes 1572872 | tf_op jit(solution)/shard_map/ppermute | solution.py:17
  425.9 21.1 %collective-permute-start.45 = (bf16[128,2048]{1,0:T(8,128)(2,1)}, bf16[128,2048]{1,0:T(8,128)(2,1)}, u32[]{:S(2)}, u32[]{:S(2)}) collective-permute-start(bf16[128,2048]{1,0:T(8,128)(2,1)} %add_convert_fusion.2), channel_id=1, source_target_pairs={{0,16},{4,20},{8,24},{12,28},{16,0},{20,4},{24,8},{28,12},{1,17},{... | collective-permute-start | bytes 1572872 | tf_op jit(solution)/shard_map/ppermute | solution.py:17
  431.0 31.9 %collective-permute-start.59 = (f32[2,256]{1,0:T(2,128)S(1)}, f32[2,256]{1,0:T(2,128)S(1)}, u32[]{:S(2)}, u32[]{:S(2)}) collective-permute-start(f32[2,256]{1,0:T(2,128)S(1)} %fusion.34), channel_id=1, source_target_pairs={{0,3},{1,0},{2,1},{3,2},{4,7},{5,4},{6,5},{7,6},{8,11},{9,8},{10,9... | collective-permute-start | bytes 6152 | tf_op jit(solution)/shard_map/ppermute | solution.py:701
  447.0 15.8 %collective-permute-start.58 = (f32[2,256]{1,0:T(2,128)S(1)}, f32[2,256]{1,0:T(2,128)S(1)}, u32[]{:S(2)}, u32[]{:S(2)}) collective-permute-start(f32[2,256]{1,0:T(2,128)S(1)} %fusion.34), channel_id=1, source_target_pairs={{0,2},{1,3},{2,0},{3,1},{4,6},{5,7},{6,4},{7,5},{8,10},{9,11},{10,... | collective-permute-start | bytes 6152 | tf_op jit(solution)/shard_map/ppermute | solution.py:701
  447.1 15.8 %collective-permute-start.57 = (f32[2,256]{1,0:T(2,128)S(1)}, f32[2,256]{1,0:T(2,128)S(1)}, u32[]{:S(2)}, u32[]{:S(2)}) collective-permute-start(f32[2,256]{1,0:T(2,128)S(1)} %fusion.34), channel_id=1, source_target_pairs={{0,1},{1,2},{2,3},{3,0},{4,5},{5,6},{6,7},{7,4},{8,9},{9,10},{10,1... | collective-permute-start | bytes 6152 | tf_op jit(solution)/shard_map/ppermute | solution.py:701
  460.1 105.6 %reduce-scatter.9.cloned.1.call-start = ((), (), s32[]{:S(2)}) async-start(), calls=%async_computation.8 | async-start | bytes 5242880 | tf_op jit(solution)/shard_map/reduce_scatter | solution.py:680
  466.2 17.1 %collective-permute-start.60 = (f32[2,2048]{1,0:T(2,128)S(1)}, f32[2,2048]{1,0:T(2,128)S(1)}, u32[]{:S(2)}, u32[]{:S(2)}) collective-permute-start(f32[2,2048]{1,0:T(2,128)S(1)} %pad_maximum_fusion.7), channel_id=1, source_target_pairs={{0,4},{4,0},{8,12},{12,8},{16,20},{20,16},{24,28},{28,24},{1,5},{5... | collective-permute-start | bytes 49160 | tf_op jit(solution)/shard_map/ppermute | solution.py:17
  470.7 36.8 %collective-permute-start.48 = (bf16[128,2048]{1,0:T(8,128)(2,1)}, bf16[128,2048]{1,0:T(8,128)(2,1)S(1)}, u32[]{:S(2)}, u32[]{:S(2)}) collective-permute-start(bf16[128,2048]{1,0:T(8,128)(2,1)} %slice.300), channel_id=1, source_target_pairs={{0,8},{4,12},{8,0},{12,4},{16,24},{20,28},{24,16},{28,20},{1,9},{5... | collective-permute-start | bytes 1572872 | tf_op jit(solution)/shard_map/ppermute | solution.py:17
  480.1 28.4 %collective-permute-start.49 = (bf16[128,2048]{1,0:T(8,128)(2,1)S(1)}, bf16[128,2048]{1,0:T(8,128)(2,1)S(1)}, u32[]{:S(2)}, u32[]{:S(2)}) collective-permute-start(bf16[128,2048]{1,0:T(8,128)(2,1)S(1)} %slice.301), channel_id=1, source_target_pairs={{0,16},{4,20},{8,24},{12,28},{16,0},{20,4},{24,8},{28,12},{1,17},{... | collective-permute-start | bytes 1572872 | tf_op jit(solution)/shard_map/ppermute | solution.py:17
  480.7 27.9 %collective-permute-start.47 = (bf16[128,2048]{1,0:T(8,128)(2,1)S(1)}, bf16[128,2048]{1,0:T(8,128)(2,1)S(1)}, u32[]{:S(2)}, u32[]{:S(2)}) collective-permute-start(bf16[128,2048]{1,0:T(8,128)(2,1)S(1)} %get-tuple-element.319), channel_id=1, source_target_pairs={{0,16},{4,20},{8,24},{12,28},{16,0},{20,4},{24,8},{28,12},{1,17},{... | collective-permute-start | bytes 1572872 | tf_op jit(solution)/shard_map/ppermute | solution.py:17
  482.2 26.4 %collective-permute-start.46 = (bf16[128,2048]{1,0:T(8,128)(2,1)S(1)}, bf16[128,2048]{1,0:T(8,128)(2,1)S(1)}, u32[]{:S(2)}, u32[]{:S(2)}) collective-permute-start(bf16[128,2048]{1,0:T(8,128)(2,1)S(1)} %get-tuple-element.320), channel_id=1, source_target_pairs={{0,8},{4,12},{8,0},{12,4},{16,24},{20,28},{24,16},{28,20},{1,9},{5... | collective-permute-start | bytes 1572872 | tf_op jit(solution)/shard_map/ppermute | solution.py:17
  (174 other events, 1272.0 us)
Sparse Core Ops, SparseCore 0:
  19.3 106.0 all-gather.2
  140.5 58.5 all-gather.4
  232.4 56.4 reduce-scatter.4
  322.1 102.3 reduce-scatter.6
  460.2 26.6 reduce-scatter.10
  489.2 76.4 reduce-scatter.8

commit v3 on v2

--- a/solution.py
+++ b/solution.py
@@ -357,111 +357,82 @@
     )(own, other)
 
 
-def add_kernel(left, right, out):
-    out[...] = (left[...].astype(f32) + right[...].astype(f32)).astype(bf16)
-
-
-def add_pair(left, right):
-    rows, depth = left.shape
-    step = rows
-    while step > 256 and step % 32 == 0:
-        step //= 2
-    block = pl.BlockSpec((step, depth), lambda at: (at, 0))
+def free_call(kernel, out_shape, megabytes, *args):
+    vmem = pl.BlockSpec(memory_space=pltpu.VMEM)
     return pl.pallas_call(
-        add_kernel,
-        out_shape=jax.ShapeDtypeStruct((rows, depth), bf16),
-        grid=(rows // step,),
-        in_specs=[block] * 2,
-        out_specs=block,
-        compiler_params=pltpu.CompilerParams(vmem_limit_bytes=10 * 2**20),
-        cost_estimate=pl.CostEstimate(flops=0, bytes_accessed=0, transcendentals=0),
-    )(left, right)
-
-
-def cross_kernel(groups, count, left_cols, right_cols, *refs):
-    lefts, rights = refs[: sum(groups)], refs[sum(groups) : sum(groups) + count]
-    out, left_held, right_held, out_held, left_sem, right_sem, out_sem = refs[sum(groups) + count :]
-    rows, width = out.shape[1:]
-    spare = left_cols % 128
-    step = out_held.shape[3]
-    tiles = width // step
-    left_copies, right_copies = [], [[] for _ in range(tiles)]
-    at = 0
-    for group, many in enumerate(groups):
-        first = 0
-        for ref in lefts[at : at + many]:
-            here = pl.ds(first, ref.shape[0])
-            left_copies.append(
-                pltpu.make_async_copy(ref, left_held.at[group, here], left_sem.at[len(left_copies)])
-            )
-            first += ref.shape[0]
-        at += many
-    for tile in range(tiles):
-        first = 0
-        for index, ref in enumerate(rights):
-            source = ref.at[:, pl.ds(right_cols + tile * step, step)]
-            target = right_held.at[tile, pl.ds(first, ref.shape[0])]
-            right_copies[tile].append(
-                pltpu.make_async_copy(source, target, right_sem.at[tile, index])
-            )
-            first += ref.shape[0]
-    for copy in right_copies[0] + left_copies:
-        copy.start()
-    for copies in right_copies[1:]:
-        for copy in copies:
-            copy.start()
-    for copy in left_copies:
-        copy.wait()
-    out_copies = []
-    for tile in range(tiles):
-        for copy in right_copies[tile]:
-            copy.wait()
-        for group in range(len(groups)):
-            left = left_held[group, :, left_cols - spare : left_cols + rows]
-            product = mm(left, right_held[tile], TN)
-            out_held[tile, group] = product[spare:].astype(bf16)
-            out_copies.append(
-                pltpu.make_async_copy(
-                    out_held.at[tile, group],
-                    out.at[group, :, pl.ds(tile * step, step)],
-                    out_sem.at[tile, group],
-                )
-            )
-            out_copies[-1].start()
-    for copy in out_copies:
-        copy.wait()
-
-
-def cross(groups, rights, left_cols=None, right_cols=None):
-    tokens = sum(part.shape[0] for part in rights)
-    left_width, right_width = groups[0][0].shape[1], rights[0].shape[1]
-    left_cols, right_cols = left_cols or (0, left_width), right_cols or (0, right_width)
-    rows, width = left_cols[1], right_cols[1]
-    step = 512 if width % 512 == 0 else width
-    tiles, many = width // step, len(groups)
-    anywhere = pl.BlockSpec(memory_space=pl.ANY)
-    args = [part for group in groups for part in group] + list(rights)
-    return pl.pallas_call(
-        functools.partial(
-            cross_kernel, [len(group) for group in groups], len(rights), left_cols[0], right_cols[0]
-        ),
-        out_shape=jax.ShapeDtypeStruct((many, rows, width), bf16),
-        in_specs=[anywhere] * len(args),
-        out_specs=anywhere,
-        scratch_shapes=[
-            pltpu.VMEM((many, tokens, left_width), bf16),
-            pltpu.VMEM((tiles, tokens, step), bf16),
-            pltpu.VMEM((tiles, many, rows, step), bf16),
-            pltpu.SemaphoreType.DMA((len(args) - len(rights),)),
-            pltpu.SemaphoreType.DMA((tiles, len(rights))),
-            pltpu.SemaphoreType.DMA((tiles, many)),
-        ],
-        compiler_params=pltpu.CompilerParams(
-            vmem_limit_bytes=2 * (many * tokens * left_width + tokens * width + many * rows * width)
-            + 10 * 2**20
-        ),
+        kernel,
+        out_shape=out_shape,
+        in_specs=[vmem] * len(args),
+        out_specs=jax.tree.map(lambda _: vmem, out_shape),
+        compiler_params=pltpu.CompilerParams(vmem_limit_bytes=megabytes * 2**20),
         cost_estimate=pl.CostEstimate(flops=0, bytes_accessed=0, transcendentals=0),
     )(*args)
+
+
+def add_kernel(count, *refs):
+    out = refs[-1]
+    rows = refs[0].shape[0]
+    step = 64 if rows % 64 == 0 else rows
+    for at in range(count):
+        for row in range(0, rows, step):
+            here = slice(row, row + step)
+            left, right = refs[2 * at][here], refs[2 * at + 1][here]
+            out[at, here] = (left.astype(f32) + right.astype(f32)).astype(bf16)
+
+
+def add_pairs(*pairs):
+    out = jax.ShapeDtypeStruct((len(pairs),) + pairs[0][0].shape, bf16)
+    args = [one for pair in pairs for one in pair]
+    return free_call(functools.partial(add_kernel, len(pairs)), out, 8, *args)
+
+
+def pieces(lefts, rights):
+    found, left, right, start, begin = [], 0, 0, 0, 0
+    while left < len(lefts):
+        rows = min(lefts[left].shape[0] - start, rights[right].shape[0] - begin)
+        found.append(((lefts[left], start), (rights[right], begin), rows))
+        start, begin = start + rows, begin + rows
+        if start == lefts[left].shape[0]:
+            left, start = left + 1, 0
+        if begin == rights[right].shape[0]:
+            right, begin = right + 1, 0
+    return found
+
+
+def cross_kernel(count, by_rows, *refs):
+    own, other = refs[-2:]
+    rows = refs[0].shape[1]
+    width = refs[count].shape[1]
+    step = 512 if rows < 2048 else 256
+    step = step if (width if by_rows else width // 2) % step == 0 else width // 2
+    found = pieces(refs[:count], refs[count:-2])
+    for col in range(0, width, step):
+        lanes = slice(col, col + step)
+        total, lefts, rights, held = None, [], [], 0
+        for index, ((one, start), (two, begin), tokens) in enumerate(found):
+            lefts.append(one[start : start + tokens])
+            rights.append(two[begin : begin + tokens, lanes])
+            held += tokens
+            if held >= 256 or index == len(found) - 1:
+                left = lefts[0] if len(lefts) == 1 else jnp.concatenate(lefts)
+                right = rights[0] if len(rights) == 1 else jnp.concatenate(rights)
+                term = mm(left, right, TN)
+                total = term if total is None else total + term
+                lefts, rights, held = [], [], 0
+        if by_rows:
+            own[:, lanes] = total[: rows // 2].astype(bf16)
+            other[:, lanes] = total[rows // 2 :].astype(bf16)
+        elif col < width // 2:
+            own[:, lanes] = total.astype(bf16)
+        else:
+            other[:, col - width // 2 : col - width // 2 + step] = total.astype(bf16)
+
+
+def cross(lefts, rights, by_rows=True):
+    rows, width = lefts[0].shape[1], rights[0].shape[1]
+    half = (rows // 2, width) if by_rows else (rows, width // 2)
+    out = [jax.ShapeDtypeStruct(half, bf16)] * 2
+    return free_call(functools.partial(cross_kernel, len(lefts), by_rows), out, 10, *lefts, *rights)
 
 
 def per_device(
@@ -553,6 +524,10 @@
                 proj, *normed_parts[early:], cot_own, layer_input, w_out
             )
             part = normed_parts[index]
+        if two and index >= early:
+            if index == early:
+                continue
+            part = jnp.concatenate(normed_parts[early:])
         proj = lax.dynamic_update_slice(proj, mm(part, proj_weights, NN), (at, 0))
         at += part.shape[0]
     gated, mixed, states, scores = recurrence(
@@ -588,53 +563,57 @@
     for at in range(count):
         if at:
             ffn_parts[at], inner[-1] = tie(ffn_parts[at], inner[-1])
+        if at == count - 1:
+            ffn_parts[at], cot_flat = tie(ffn_parts[at], cot_flat)
         if two and at == 3:
             ffn_parts[3] = jnp.concatenate(ffn_parts[3])
         gate, up = mm(ffn_parts[at], gate_rows, NT), mm(ffn_parts[at], up_rows, NT)
         sig = jax.nn.sigmoid(gate)
-        up_part.append(gate * sig)
-        gate_part.append(up * sig * (1.0 + gate * (1.0 - sig)))
-        inner.append((up_part[-1] * up).astype(bf16))
-    lower, upper = (0, hidden_half), (hidden_half, hidden_half)
-    down_other = cross([inner], cot_flat, left_cols=upper)
-    down_other, inner[0], down = tie(down_other, inner[0], down)
-    down_own = cross([inner], cot_flat, left_cols=lower)
-    down_pair = add_pair(down_own[0], swap(down_other[0], 1, size))
-    (down_rows,) = stack_rows(down[None], swap(down, 1, size)[None])
-    down_pair, cot_flat = tie(down_pair, cot_flat)
+        silu = gate * sig
+        up_part.append(silu.astype(bf16))
+        gate_part.append((up * sig * (1.0 + gate * (1.0 - sig))).astype(bf16))
+        inner.append((silu * up).astype(bf16))
+    inner[-1], down = tie(inner[-1], down)
+    down_own, down_other = cross(inner, cot_flat)
+    down_received, down_own = tie(swap(down, 1, size), down_own)
+    down_other = swap(down_other, 1, size)
+    down_pair = None
+    (down_rows,) = stack_rows(down[None], down_received[None])
     cot_parts = [*cot_flat[:3], jnp.concatenate(cot_flat[3:])] if two else cot_flat
-    ffn_down_grad = lax.psum_scatter(down_pair, "dp", scatter_dimension=0, tiled=True)
-
     gate_grad, up_grad, totals = [None] * count, [None] * count, []
 
     def ffn_part(at):
+        nonlocal down_other, down_pair
         part = cot_parts[at]
+        if len(totals) == 1:
+            down_other, totals[0] = tie(down_other, totals[0])
+            down_pair = add_pairs((down_own, down_other))[0]
+            part, down_pair = tie(part, down_pair)
         if totals:
             part, totals[-1] = tie(part, totals[-1])
         inner_grad = mm(part, down_rows, NT)
-        gate_grad[at] = (inner_grad * gate_part[at]).astype(bf16)
-        up_grad[at] = (inner_grad * up_part[at]).astype(bf16)
+        gate_grad[at] = (inner_grad * gate_part[at].astype(f32)).astype(bf16)
+        up_grad[at] = (inner_grad * up_part[at].astype(f32)).astype(bf16)
         totals.append(
             add(mm(gate_grad[at], gate_rows, NN), mm(up_grad[at], up_rows, NN)).astype(bf16)
         )
         return totals[-1]
 
     ffn_sum = Scatter(ffn_part, bits, size)
+    ffn_down_grad = lax.psum_scatter(down_pair, "dp", scatter_dimension=0, tiled=True)
     if two:
-        ffn_sum.own, gate_grad, up_grad = tie(ffn_sum.own, gate_grad, up_grad)
-    gate_up_other = cross([gate_grad, up_grad], ffn_flat, left_cols=upper)
+        ffn_sum.own, gate_grad[0] = tie(ffn_sum.own, gate_grad[0])
+    gate_own, gate_other = cross(gate_grad, ffn_flat)
+    gate_other, up_grad[0] = tie(gate_other, up_grad[0])
+    up_own, up_other = cross(up_grad, ffn_flat)
+    up_other, ffn_down_grad = tie(up_other, ffn_down_grad)
     if two:
-        ffn_sum.moved, gate_up_other = tie(ffn_sum.moved, gate_up_other)
+        ffn_sum.moved, up_other = tie(ffn_sum.moved, up_other)
         ffn_sum.finish()
-        ffn_sum.sends, gate_grad, up_grad = tie(ffn_sum.sends, gate_grad, up_grad)
-    gate_up_other, gate_grad, up_grad, ffn_down_grad = tie(
-        gate_up_other, gate_grad, up_grad, ffn_down_grad
+    gate_up_pair = add_pairs(
+        (gate_own, swap(gate_other, 1, size)), (up_own, swap(up_other, 1, size))
     )
-    gate_up_own = cross([gate_grad, up_grad], ffn_flat, left_cols=lower)
-    gate_up_pair = add_pair(
-        gate_up_own.reshape(-1, model_width), swap(gate_up_other, 1, size).reshape(-1, model_width)
-    ).reshape(gate_up_own.shape)
-    ffn_in_grad, gate_up_pair = ffn_sum.total(gate_up_pair)
+    ffn_in_grad = ffn_sum.total(resid)[0]
     gate_up_grad = lax.psum_scatter(gate_up_pair, "dp", scatter_dimension=1, tiled=True)
 
     scaled = ffn_in_grad * norm2_gain
@@ -643,40 +622,33 @@
     )
     norm2_part = jnp.sum(ffn_in_grad * resid * row_scale, axis=0)
     mixer_parts = gather_start(resid_grad.astype(bf16), bits, size)[1]
+    output_parts = [mm(inner[at], down_rows, NN).astype(bf16) for at in range(count)]
+    output_parts, mixer_parts[-1] = tie(output_parts, mixer_parts[-1])
+    output_sum = Scatter(lambda at: output_parts[at], bits, size)
     mixer_grad = jnp.concatenate(mixer_parts)
 
-    out_other = cross([[gated]], mixer_parts, left_cols=(half_width, half_width))
-    out_other, gated = tie(out_other, gated)
-    out_own = cross([[gated]], mixer_parts, left_cols=(0, half_width))
-    mixer_grad, out_own = tie(mixer_grad, out_own)
-    out_pair = add_pair(out_own[0], swap(out_other[0], 1, size))
+    out_own, out_other = cross([gated], mixer_parts)
+    mixer_grad, out_other = tie(mixer_grad, out_other)
+    out_pair = add_pairs((out_own, swap(out_other, 1, size)))[0]
     gated_grad = mm(mixer_grad, out_weights, NT)
     proj_grad, floor_grad, gain_grad = recurrence_back(
         info, proj, floor_row, gain_row, seg, mixed, gated_grad, states, scores, half_heads, size
     )
-    line = [proj_grad]
-
-    def normed_part(at):
-        part = mm(chunk(line[0], at), proj_weights, NT).astype(bf16)
-        line[0], part = tie(line[0], part)
-        return part
-
-    normed_sum = Scatter(normed_part, bits, size)
-    proj_grad = line[0]
-
-    proj_other = cross([normed_parts], [proj_grad], right_cols=(2 * width, 2 * width))
     if two:
-        normed_sum.at_first, normed_sum.at_second, proj_other = tie(
-            normed_sum.at_first, normed_sum.at_second, proj_other
-        )
+        output_sum.moved, proj_grad = tie(output_sum.moved, proj_grad)
+
+    proj_own, proj_other = cross(normed_parts, [proj_grad], by_rows=False)
+    proj_other, proj_grad = tie(proj_other, proj_grad)
+    normed_all = mm(proj_grad, proj_weights, NT).astype(bf16)
+    proj_other, normed_all = tie(swap(proj_other, 1, size), normed_all)
+    proj_pair = add_pairs((proj_own, proj_other))[0]
+    normed_sum = Scatter(lambda at: chunk(normed_all, at), bits, size)
+    if two:
         normed_sum.finish()
-        normed_sum.sends, proj_grad = tie(normed_sum.sends, proj_grad)
-    proj_grad, proj_other = tie(proj_grad, proj_other)
-    proj_own = cross([normed_parts], [proj_grad], right_cols=(0, 2 * width))
-    normed_grad, proj_own = normed_sum.total(proj_own)
-    proj_pair = add_pair(proj_own[0], swap(proj_other[0], 1, size))
-    proj_pair, out_pair, gate_up_grad = tie(proj_pair, out_pair, gate_up_grad)
+    normed_grad = normed_sum.total(proj_own)[0]
+    out_pair, gate_up_grad = tie(out_pair, gate_up_grad)
     out_grad = lax.psum_scatter(out_pair, "dp", scatter_dimension=1, tiled=True)
+    proj_pair, out_grad = tie(proj_pair, out_grad)
     proj_w_grad = lax.psum_scatter(proj_pair, "dp", scatter_dimension=0, tiled=True).astype(f32)
 
     input_scale = rms_scale(own_rows)
@@ -691,8 +663,9 @@
     norm1_part = jnp.sum(normed_grad * own_rows * input_scale, axis=0)
     input_grad = from_row(input_grad)
 
-    inner, norm1_part = tie(inner, norm1_part)
-    output_sum = Scatter(lambda at: mm(inner[at], down_rows, NN).astype(bf16), bits, size)
+    if two:
+        output_sum.finish()
+        output_sum.sends, norm1_part = tie(output_sum.sends, norm1_part)
     output = from_row(add(resid, output_sum.total(resid)[0]).astype(bf16))
 
     vector_grads = jnp.concatenate((gain_grad, floor_grad))

time: 580 us -> 533 us (0.919)
  local copies, waits for them, and re-layouts: 77.7 us -> 56.1 us
  Pallas kernels: 104 us -> 85.2 us
  other arithmetic: 37.6 us -> 27.4 us
    unnamed x309 -> x295, local copies, waits for them, and re-layouts: 61.6 us -> 39 us
    reduce_scatter x1, waiting for transfers between devices: 30.4 us -> 11.3 us  [per_device(): lax.psum_scatter(proj_pair, 'dp', scatter_dimension=0, tiled=True)]
    pallas_call x12 -> x9, Pallas kernels: 65.4 us -> 48.8 us  [free_call(): pl.pallas_call(kernel, out_shape=out_shape, in_specs=[vmem] * len(args),...]
    ppermute x60 -> x61, waiting for transfers between devices: 138 us -> 153 us  [swap(): return lax.ppermute(tensor, 'head', [(at, at ^ bit) for at in range(size)])]
    dot_general x41 -> x37, matrix products: 108 us -> 103 us  [mm(): lax.dot_general(left, right, (dims, ((), ())), preferred_element_type=out)]
    ppermute x60 -> x61, starting transfers between devices: 52.7 us -> 52.9 us  [swap(): return lax.ppermute(tensor, 'head', [(at, at ^ bit) for at in range(size)])]
  transfers between devices with their start and end apart: 72 -> 73, of which waited for: 27 -> 29; matrix products, arithmetic and copies ran while one was open for 27% -> 27% of each run, Pallas kernels for 18% -> 15%
where the time goes in v3:
time: 533 us; the launch traced here: 523 us
  waiting for transfers between devices  171 us (32%)
  matrix products  103 us (19%)
  Pallas kernels  85.2 us (16%)
  starting transfers between devices  63.1 us (12%)
  local copies, waits for them, and re-layouts  56.1 us (11%)
  other arithmetic  27.4 us (5%)
  between operations  16.7 us (3%)
    ppermute x61, waiting for transfers between devices, swap(): return lax.ppermute(tensor, 'head', [(at, at ^ bit) for at in range(size)])  153 us
    dot_general x37, matrix products, mm(): lax.dot_general(left, right, (dims, ((), ())), preferred_element_type=out)  103 us
    ppermute x61, starting transfers between devices, swap(): return lax.ppermute(tensor, 'head', [(at, at ^ bit) for at in range(size)])  52.9 us
    pallas_call x9, Pallas kernels, free_call(): pl.pallas_call(kernel, out_shape=out_shape, in_specs=[vmem] * len(args),...  48.8 us
    unnamed x295, local copies, waits for them, and re-layouts  39 us
    pallas_call x1, Pallas kernels, recurrence_back(): pl.pallas_call(functools.partial(backward_kernel, blocks, half_heads), ou...  17 us
    pallas_call x1, Pallas kernels, recurrence(): pl.pallas_call(functools.partial(forward_kernel, blocks, half_heads), out...  15.9 us
    reduce_scatter x1, waiting for transfers between devices, per_device(): lax.psum_scatter(proj_pair, 'dp', scatter_dimension=0, tiled=True)  11.3 us
  transfers between devices with their start and end apart: 73, of which 29 were waited for; matrix products, arithmetic and copies ran while one was open for 27% of the time, Pallas kernels for 15%

profile of v3, /device:TPU:0, one launch (start us, length us, event | category | flops | bytes accessed | tf_op | source)
XLA Modules:
  0.0 523.0 jit_solution(3627549540291870373)
XLA Ops:
  7.3 3.9 pad_maximum_fusion
  13.2 2.6 collective-permute-start.5
  23.4 7.2 %collective-permute-done.2.refs_2_ = bf16[128,2048]{1,0:T(8,128)(2,1)S(1)} collective-permute-done((bf16[128,2048]{1,0:T(8,128)(2,1)S(1)}, bf16[128,2048]{1,0:T(8,128)(2,1)S(1)}, u32[]{:S(2)}, u32[]{:S(2)}) %collective-permute-start.2) | collective-permute-done | bytes 524320 | tf_op jit(solution)/shard_map/ppermute | solution.py:17
  34.1 2.7 constant_dynamic-update-slice_fusion
  48.0 7.0 %collective-permute-done.6.refs_6_ = bf16[128,2048]{1,0:T(8,128)(2,1)S(1)} collective-permute-done((bf16[128,2048]{1,0:T(8,128)(2,1)S(1)}, bf16[128,2048]{1,0:T(8,128)(2,1)S(1)}, u32[]{:S(2)}, u32[]{:S(2)}) %collective-permute-start.6) | collective-permute-done | bytes 524320 | tf_op jit(solution)/shard_map/ppermute | solution.py:17
  60.0 15.9 %shard_map.254 = (bf16[1024,512]{1,0:T(8,128)(2,1)S(1)}, f32[1024,512]{1,0:T(8,128)S(1)}, f32[8,4,128,128]{3,2,1,0:T(8,128)S(1)}, bf16[8,4,128,128]{3,2,1,0:T(8,128)(2,1)S(1)}) custom-call(s32[17]{0:T(128)S(1)} %pad_add_fusion.info, f32[1024,2048]{1,0:T(8,128)S(1)} %convolution_dynamic-update-slice_fusion.proj_ref, ...), custom_call_target="tpu_custom_call" | custom-call | tf_op jit(solution)/shard_map/pallas_call | solution.py:255
  86.6 9.1 %collective-permute-done.17 = bf16[128,2048]{1,0:T(8,128)(2,1)S(1)} collective-permute-done((bf16[128,2048]{1,0:T(8,128)(2,1)S(1)}, bf16[128,2048]{1,0:T(8,128)(2,1)S(1)}, u32[]{:S(2)}, u32[]{:S(2)}) %collective-permute-start.17) | collective-permute-done | bytes 524320 | tf_op jit(solution)/shard_map/ppermute | solution.py:17
  97.6 10.1 %collective-permute-done.14 = bf16[128,2048]{1,0:T(8,128)(2,1)S(1)} collective-permute-done((bf16[128,2048]{1,0:T(8,128)(2,1)S(1)}, bf16[128,2048]{1,0:T(8,128)(2,1)S(1)}, u32[]{:S(2)}, u32[]{:S(2)}) %collective-permute-start.14) | collective-permute-done | bytes 524320 | tf_op jit(solution)/shard_map/ppermute | solution.py:17
  109.6 11.1 %collective-permute-done.19 = bf16[128,2048]{1,0:T(8,128)(2,1)S(1)} collective-permute-done((bf16[128,2048]{1,0:T(8,128)(2,1)S(1)}, bf16[128,2048]{1,0:T(8,128)(2,1)S(1)}, u32[]{:S(2)}, u32[]{:S(2)}) %collective-permute-start.19) | collective-permute-done | bytes 524320 | tf_op jit(solution)/shard_map/ppermute | solution.py:17
  128.2 22.5 %collective-permute-done.20.refs_5_ = bf16[256,2048]{1,0:T(8,128)(2,1)S(1)} collective-permute-done((bf16[256,2048]{1,0:T(8,128)(2,1)S(1)}, bf16[256,2048]{1,0:T(8,128)(2,1)S(1)}, u32[]{:S(2)}, u32[]{:S(2)}) %collective-permute-start.20) | collective-permute-done | bytes 1048608 | tf_op jit(solution)/shard_map/ppermute | solution.py:17
  157.5 2.6 copy-done.7
  160.1 3.1 shard_map.255
  165.2 3.5 multiply_convert_fusion.16
  170.7 3.5 multiply_convert_fusion.15
  174.2 3.1 fusion.52
  177.3 5.2 multiply_convert_fusion.14
  185.7 3.5 multiply_convert_fusion.13
  198.3 7.8 %shard_map.256 = (bf16[704,2048]{1,0:T(8,128)(2,1)S(1)}, bf16[704,2048]{1,0:T(8,128)(2,1)}) custom-call(bf16[256,1408]{1,0:T(8,128)(2,1)S(1)} %copy-done.46, bf16[256,1408]{1,0:T(8,128)(2,1)S(1)} %copy-done.48, bf16[256,1408]{1,0:T(8,128)(2,1)S(1)} %copy-done.50, bf16[256,1408]{1,0:T(8,128)(2,1)S(1)} %copy-done.52, ...), custom_call_target="tpu_custom_call" | custom-call | tf_op jit(solution)/shard_map/pallas_call | solution.py:362
  207.7 6.3 %multiply_convert_fusion.11 = (bf16[256,1408]{1,0:T(8,128)(2,1)S(1)}, bf16[256,1408]{1,0:T(8,128)(2,1)S(1)}) fusion(f32[256,1408]{1,0:T(8,128)} %copy-done.126, f32[256,1408]{1,0:T(8,128)} %get-tuple-element.325, bf16[1408,2048]{1,0:T(8,128)(2,1)S(1)} %shard_map.257, bf16[128,2048]{1,0:T(8,128)(2,1)S(1)} %copy-done.67, bf16[128,2048]{1,0:T(8,128)(2,1)S(1)} %copy-done.64), kind=kOutput, calls=%fused_computation.68 | convolution fusion | flops 1484619776 | bytes 11141120 | tf_op jit(solution)/shard_map/dot_general | solution.py:21
  216.0 2.8 fusion
  221.4 5.9 %multiply_convert_fusion.8 = (bf16[256,1408]{1,0:T(8,128)(2,1)S(1)}, bf16[256,1408]{1,0:T(8,128)(2,1)S(1)}) fusion(f32[256,1408]{1,0:T(8,128)} %copy-done.125, f32[256,1408]{1,0:T(8,128)} %get-tuple-element.321, bf16[256,2048]{1,0:T(8,128)(2,1)} %copy-done.37, bf16[1408,2048]{1,0:T(8,128)(2,1)} %copy-done.8), kind=kOutput, calls=%fused_computation.65 | convolution fusion | flops 1482522624 | bytes 11141120 | tf_op jit(solution)/shard_map/dot_general | solution.py:21
  227.4 4.6 fusion.55
  232.0 4.7 fusion.1
  253.6 2.8 fusion.3
  256.3 9.1 %shard_map.259 = (bf16[704,2048]{1,0:T(8,128)(2,1)S(1)}, bf16[704,2048]{1,0:T(8,128)(2,1)}) custom-call(bf16[256,1408]{1,0:T(8,128)(2,1)S(1)} %get-tuple-element.192.refs_0_, bf16[256,1408]{1,0:T(8,128)(2,1)S(1)} %get-tuple-element.279.refs_1_, bf16[256,1408]{1,0:T(8,128)(2,1)S(1)} %get-tuple-element.277.refs_2_, bf16[256,1408]{1,0:T(8,128)(2,1)S(1)} %copy-done.57, ...), custom_call_target="tpu_custom_call" | custom-call | tf_op jit(solution)/shard_map/pallas_call | solution.py:362
  267.0 7.9 %shard_map.260 = (bf16[704,2048]{1,0:T(8,128)(2,1)S(1)}, bf16[704,2048]{1,0:T(8,128)(2,1)S(1)}) custom-call(bf16[256,1408]{1,0:T(8,128)(2,1)S(1)} %get-tuple-element.194.refs_0_, bf16[256,1408]{1,0:T(8,128)(2,1)S(1)} %get-tuple-element.280.refs_1_, bf16[256,1408]{1,0:T(8,128)(2,1)S(1)} %get-tuple-element.278.refs_2_, bf16[256,1408]{1,0:T(8,128)(2,1)S(1)} %copy-done.55, ...), custom_call_target="tpu_custom_call" | custom-call | tf_op jit(solution)/shard_map/pallas_call | solution.py:362
  278.8 5.1 collective-permute-done.56.refs_3_
  287.5 3.4 shard_map.266
  290.9 2.5 copy-done.3
  298.5 5.5 %convolution_convert_fusion.5 = bf16[256,2048]{1,0:T(8,128)(2,1)S(1)} fusion(bf16[256,1408]{1,0:T(8,128)(2,1)S(1)} %copy-done.53, bf16[1408,2048]{1,0:T(8,128)(2,1)} %copy-done.8), kind=kOutput, calls=%fused_computation.28 | convolution fusion | flops 1476919296 | bytes 7536640 | tf_op jit(solution)/shard_map/dot_general | solution.py:21
  304.0 5.3 %collective-permute-done.34 = bf16[128,2048]{1,0:T(8,128)(2,1)S(1)} collective-permute-done((bf16[128,2048]{1,0:T(8,128)(2,1)S(1)}, bf16[128,2048]{1,0:T(8,128)(2,1)S(1)}, u32[]{:S(2)}, u32[]{:S(2)}) %collective-permute-start.34) | collective-permute-done | bytes 524320 | tf_op jit(solution)/shard_map/ppermute | solution.py:17
  321.1 19.5 %collective-permute-done.35.refs_3_ = bf16[256,2048]{1,0:T(8,128)(2,1)S(1)} collective-permute-done((bf16[256,2048]{1,0:T(8,128)(2,1)S(1)}, bf16[256,2048]{1,0:T(8,128)(2,1)S(1)}, u32[]{:S(2)}, u32[]{:S(2)}) %collective-permute-start.35) | collective-permute-done | bytes 1048608 | tf_op jit(solution)/shard_map/ppermute | solution.py:17
  342.4 2.8 convolution_convert_fusion.8
  345.4 7.6 %collective-permute-done.36.refs_5_ = bf16[128,2048]{1,0:T(8,128)(2,1)S(1)} collective-permute-done((bf16[128,2048]{1,0:T(8,128)(2,1)S(1)}, bf16[128,2048]{1,0:T(8,128)(2,1)S(1)}, u32[]{:S(2)}, u32[]{:S(2)}) %collective-permute-start.36) | collective-permute-done | bytes 524320 | tf_op jit(solution)/shard_map/ppermute | solution.py:17
  360.5 2.6 fusion.58.grad_ref
  364.3 17.0 %shard_map.262 = (bf16[1024,2048]{1,0:T(8,128)(2,1)S(1)}, f32[1,512]{1,0:T(1,128)S(1)}, f32[1,512]{1,0:T(1,128)S(1)}) custom-call(s32[17]{0:T(128)S(1)} %copy-done.71, f32[1024,2048]{1,0:T(8,128)S(1)} %bitcast.128, f32[1,512]{1,0:T(1,128)S(1)} %get-tuple-element.315.floor_ref, f32[1,512]{1,0:T(1,128)S(1)} %copy-done.69, ...), custom_call_target="tpu_custom_call" | custom-call | tf_op jit(solution)/shard_map/pallas_call | solution.py:294
  381.5 11.2 %shard_map.263 = (bf16[2048,1024]{1,0:T(8,128)(2,1)S(1)}, bf16[2048,1024]{1,0:T(8,128)(2,1)}) custom-call(bf16[128,2048]{1,0:T(8,128)(2,1)S(1)} %copy-done.6, bf16[128,2048]{1,0:T(8,128)(2,1)S(1)} %copy-done.19, bf16[128,2048]{1,0:T(8,128)(2,1)S(1)} %copy-done.23, bf16[128,2048]{1,0:T(8,128)(2,1)S(1)} %copy-done.25, bf16[128,2048]{1,0:T(8,128)(2,1)S(1)} %copy-done.27, ...), custom_call_target="tpu_custom_call" | custom-call | tf_op jit(solution)/shard_map/pallas_call | solution.py:362
  395.3 7.7 %collective-permute-done.57 = f32[2,256]{1,0:T(2,128)S(1)} collective-permute-done((f32[2,256]{1,0:T(2,128)S(1)}, f32[2,256]{1,0:T(2,128)S(1)}, u32[]{:S(2)}, u32[]{:S(2)}) %collective-permute-start.57) | collective-permute-done | bytes 2080 | tf_op jit(solution)/shard_map/ppermute | solution.py:17
  403.0 2.7 collective-permute-start.59
  408.5 12.6 %convolution_convert_fusion = bf16[1024,2048]{1,0:T(8,128)(2,1)S(1)} fusion(bf16[1024,2048]{1,0:T(8,128)(2,1)} %copy-done.15, bf16[2048,2048]{1,0:T(8,128)(2,1)} %copy-done.75), kind=kOutput, calls=%fused_computation.2 | convolution fusion | flops 8592031744 | bytes 16777216 | tf_op jit(solution)/shard_map/dot_general | solution.py:21
  425.8 3.6 shard_map.264
  431.4 3.1 reduce-scatter.9.cloned.1.call-done
  439.4 9.1 %collective-permute-done.46 = bf16[128,2048]{1,0:T(8,128)(2,1)S(1)} collective-permute-done((bf16[128,2048]{1,0:T(8,128)(2,1)S(1)}, bf16[128,2048]{1,0:T(8,128)(2,1)S(1)}, u32[]{:S(2)}, u32[]{:S(2)}) %collective-permute-start.46) | collective-permute-done | bytes 524320 | tf_op jit(solution)/shard_map/ppermute | solution.py:17
  453.8 9.5 %collective-permute-done.48 = bf16[128,2048]{1,0:T(8,128)(2,1)S(1)} collective-permute-done((bf16[128,2048]{1,0:T(8,128)(2,1)S(1)}, bf16[128,2048]{1,0:T(8,128)(2,1)S(1)}, u32[]{:S(2)}, u32[]{:S(2)}) %collective-permute-start.48) | collective-permute-done | bytes 524320 | tf_op jit(solution)/shard_map/ppermute | solution.py:17
  471.1 10.1 %collective-permute-done.62 = f32[2,2048]{1,0:T(2,128)S(1)} collective-permute-done((f32[2,2048]{1,0:T(2,128)S(1)}, f32[2,2048]{1,0:T(2,128)S(1)}, u32[]{:S(2)}, u32[]{:S(2)}) %collective-permute-start.62) | collective-permute-done | bytes 16416 | tf_op jit(solution)/shard_map/ppermute | solution.py:17
  487.5 2.8 collective-permute-start.66
  501.9 11.3 %reduce-scatter.11.cloned.1.call-done = bf16[512,1024]{1,0:T(8,128)(2,1)} async-done(((bf16[2048,1024]{1,0:T(8,128)(2,1)}), bf16[512,1024]{1,0:T(8,128)(2,1)}) %reduce-scatter.11.cloned.1.call-update) | async-done | bytes 1048592 | tf_op jit(solution)/shard_map/reduce_scatter | solution.py:652
  513.2 2.5 fusion.43
  (543 shorter events, 180.5 us)
Async XLA Ops:
  7.2 117.9 %all-gather.3.cloned.1.call-start = ((), (), s32[]{:S(2)}) async-start(), calls=%async_computation.4 | async-start | bytes 7208960 | tf_op jit(solution)/shard_map/all_gather | solution.py:504
  11.1 23.0 %collective-permute-start = (bf16[2048,1024]{1,0:T(8,128)(2,1)}, bf16[2048,1024]{1,0:T(8,128)(2,1)}, u32[]{:S(2)}, u32[]{:S(2)}) collective-permute-start(bf16[2048,1024]{1,0:T(8,128)(2,1)} %pad_maximum_fusion), channel_id=1, source_target_pairs={{0,4},{4,0},{8,12},{12,8},{16,20},{20,16},{24,28},{28,24},{1,5},{5... | collective-permute-start | bytes 12582920 | tf_op jit(solution)/shard_map/ppermute | solution.py:17
  13.2 17.7 %collective-permute-start.5 = (bf16[128,2048]{1,0:T(8,128)(2,1)}, bf16[128,2048]{1,0:T(8,128)(2,1)S(1)}, u32[]{:S(2)}, u32[]{:S(2)}) collective-permute-start(bf16[128,2048]{1,0:T(8,128)(2,1)} %get-tuple-element.137), channel_id=1, source_target_pairs={{0,20},{4,16},{8,28},{12,24},{16,4},{20,0},{24,12},{28,8},{1,21},{... | collective-permute-start | bytes 1572872 | tf_op jit(solution)/shard_map/ppermute | solution.py:17
  15.8 14.7 %collective-permute-start.2 = (bf16[128,2048]{1,0:T(8,128)(2,1)S(1)}, bf16[128,2048]{1,0:T(8,128)(2,1)S(1)}, u32[]{:S(2)}, u32[]{:S(2)}) collective-permute-start(bf16[128,2048]{1,0:T(8,128)(2,1)S(1)} %get-tuple-element.136.refs_0_), channel_id=1, source_target_pairs={{0,8},{4,12},{8,0},{12,4},{16,24},{20,28},{24,16},{28,20},{1,9},{5... | collective-permute-start | bytes 1572872 | tf_op jit(solution)/shard_map/ppermute | solution.py:17
  18.9 170.3 %all-gather.5.cloned.1.call-start = ((), (), s32[]{:S(2)}) async-start(), calls=%async_computation.5 | async-start | bytes 3604480 | tf_op jit(solution)/shard_map/all_gather | solution.py:505
  22.9 18.7 %collective-permute-start.3 = (bf16[128,2048]{1,0:T(8,128)(2,1)}, bf16[128,2048]{1,0:T(8,128)(2,1)S(1)}, u32[]{:S(2)}, u32[]{:S(2)}) collective-permute-start(bf16[128,2048]{1,0:T(8,128)(2,1)} %get-tuple-element.137), channel_id=1, source_target_pairs={{0,12},{4,8},{8,4},{12,0},{16,28},{20,24},{24,20},{28,16},{1,13},{... | collective-permute-start | bytes 1572872 | tf_op jit(solution)/shard_map/ppermute | solution.py:17
  30.5 14.9 %collective-permute-start.4 = (bf16[128,2048]{1,0:T(8,128)(2,1)S(1)}, bf16[128,2048]{1,0:T(8,128)(2,1)S(1)}, u32[]{:S(2)}, u32[]{:S(2)}) collective-permute-start(bf16[128,2048]{1,0:T(8,128)(2,1)S(1)} %get-tuple-element.136.refs_0_), channel_id=1, source_target_pairs={{0,16},{4,20},{8,24},{12,28},{16,0},{20,4},{24,8},{28,12},{1,17},{... | collective-permute-start | bytes 1572872 | tf_op jit(solution)/shard_map/ppermute | solution.py:17
  30.9 24.0 %collective-permute-start.6 = (bf16[128,2048]{1,0:T(8,128)(2,1)S(1)}, bf16[128,2048]{1,0:T(8,128)(2,1)S(1)}, u32[]{:S(2)}, u32[]{:S(2)}) collective-permute-start(bf16[128,2048]{1,0:T(8,128)(2,1)S(1)} %collective-permute-done.2.refs_2_), channel_id=1, source_target_pairs={{0,16},{4,20},{8,24},{12,28},{16,0},{20,4},{24,8},{28,12},{1,17},{... | collective-permute-start | bytes 1572872 | tf_op jit(solution)/shard_map/ppermute | solution.py:17
  32.6 22.4 %collective-permute-start.7 = (bf16[128,2048]{1,0:T(8,128)(2,1)S(1)}, bf16[128,2048]{1,0:T(8,128)(2,1)S(1)}, u32[]{:S(2)}, u32[]{:S(2)}) collective-permute-start(bf16[128,2048]{1,0:T(8,128)(2,1)S(1)} %collective-permute-done.5.refs_5_), channel_id=1, source_target_pairs={{0,8},{4,12},{8,0},{12,4},{16,24},{20,28},{24,16},{28,20},{1,9},{5... | collective-permute-start | bytes 1572872 | tf_op jit(solution)/shard_map/ppermute | solution.py:17
  54.9 24.0 %collective-permute-start.10 = (bf16[256,2048]{1,0:T(8,128)(2,1)S(1)}, bf16[256,2048]{1,0:T(8,128)(2,1)S(1)}, u32[]{:S(2)}, u32[]{:S(2)}) collective-permute-start(bf16[256,2048]{1,0:T(8,128)(2,1)S(1)} %pad_maximum_fusion.4.refs_4_), channel_id=1, source_target_pairs={{0,8},{4,12},{8,0},{12,4},{16,24},{20,28},{24,16},{28,20},{1,9},{5... | collective-permute-start | bytes 3145736 | tf_op jit(solution)/shard_map/ppermute | solution.py:17
  56.5 23.3 %collective-permute-start.11 = (bf16[256,2048]{1,0:T(8,128)(2,1)S(1)}, bf16[256,2048]{1,0:T(8,128)(2,1)S(1)}, u32[]{:S(2)}, u32[]{:S(2)}) collective-permute-start(bf16[256,2048]{1,0:T(8,128)(2,1)S(1)} %pad_maximum_fusion.4.refs_4_), channel_id=1, source_target_pairs={{0,16},{4,20},{8,24},{12,28},{16,0},{20,4},{24,8},{28,12},{1,17},{... | collective-permute-start | bytes 3145736 | tf_op jit(solution)/shard_map/ppermute | solution.py:17
  57.1 20.3 %collective-permute-start.12 = (bf16[128,2048]{1,0:T(8,128)(2,1)S(1)}, bf16[128,2048]{1,0:T(8,128)(2,1)S(1)}, u32[]{:S(2)}, u32[]{:S(2)}) collective-permute-start(bf16[128,2048]{1,0:T(8,128)(2,1)S(1)} %get-tuple-element.307), channel_id=1, source_target_pairs={{0,4},{4,0},{8,12},{12,8},{16,20},{20,16},{24,28},{28,24},{1,5},{5... | collective-permute-start | bytes 1572872 | tf_op jit(solution)/shard_map/ppermute | solution.py:17
  57.2 22.6 %collective-permute-start.13 = (bf16[256,2048]{1,0:T(8,128)(2,1)S(1)}, bf16[256,2048]{1,0:T(8,128)(2,1)S(1)}, u32[]{:S(2)}, u32[]{:S(2)}) collective-permute-start(bf16[256,2048]{1,0:T(8,128)(2,1)S(1)} %copy-done.97), channel_id=1, source_target_pairs={{0,4},{4,0},{8,12},{12,8},{16,20},{20,16},{24,28},{28,24},{1,5},{5... | collective-permute-start | bytes 3145736 | tf_op jit(solution)/shard_map/ppermute | solution.py:17
  80.8 14.9 %collective-permute-start.17 = (bf16[128,2048]{1,0:T(8,128)(2,1)S(1)}, bf16[128,2048]{1,0:T(8,128)(2,1)S(1)}, u32[]{:S(2)}, u32[]{:S(2)}) collective-permute-start(bf16[128,2048]{1,0:T(8,128)(2,1)S(1)} %slice.281), channel_id=1, source_target_pairs={{0,16},{4,20},{8,24},{12,28},{16,0},{20,4},{24,8},{28,12},{1,17},{... | collective-permute-start | bytes 1572872 | tf_op jit(solution)/shard_map/ppermute | solution.py:17
  82.7 14.9 %collective-permute-start.16 = (bf16[128,2048]{1,0:T(8,128)(2,1)S(1)}, bf16[128,2048]{1,0:T(8,128)(2,1)S(1)}, u32[]{:S(2)}, u32[]{:S(2)}) collective-permute-start(bf16[128,2048]{1,0:T(8,128)(2,1)S(1)} %slice.280), channel_id=1, source_target_pairs={{0,8},{4,12},{8,0},{12,4},{16,24},{20,28},{24,16},{28,20},{1,9},{5... | collective-permute-start | bytes 1572872 | tf_op jit(solution)/shard_map/ppermute | solution.py:17
  84.1 23.5 %collective-permute-start.14 = (bf16[128,2048]{1,0:T(8,128)(2,1)S(1)}, bf16[128,2048]{1,0:T(8,128)(2,1)S(1)}, u32[]{:S(2)}, u32[]{:S(2)}) collective-permute-start(bf16[128,2048]{1,0:T(8,128)(2,1)S(1)} %get-tuple-element.305), channel_id=1, source_target_pairs={{0,8},{4,12},{8,0},{12,4},{16,24},{20,28},{24,16},{28,20},{1,9},{5... | collective-permute-start | bytes 1572872 | tf_op jit(solution)/shard_map/ppermute | solution.py:17
  85.6 22.0 %collective-permute-start.15 = (bf16[128,2048]{1,0:T(8,128)(2,1)S(1)}, bf16[128,2048]{1,0:T(8,128)(2,1)S(1)}, u32[]{:S(2)}, u32[]{:S(2)}) collective-permute-start(bf16[128,2048]{1,0:T(8,128)(2,1)S(1)} %get-tuple-element.304), channel_id=1, source_target_pairs={{0,16},{4,20},{8,24},{12,28},{16,0},{20,4},{24,8},{28,12},{1,17},{... | collective-permute-start | bytes 1572872 | tf_op jit(solution)/shard_map/ppermute | solution.py:17
  125.1 32.4 %collective-permute-start.22 = (bf16[2,704,2048]{2,1,0:T(8,128)(2,1)}, bf16[2,704,2048]{2,1,0:T(8,128)(2,1)}, u32[]{:S(2)}, u32[]{:S(2)}) collective-permute-start(bf16[2,704,2048]{2,1,0:T(8,128)(2,1)} %all-gather.3.cloned.1.call-done.own), channel_id=1, source_target_pairs={{0,4},{4,0},{8,12},{12,8},{16,20},{20,16},{24,28},{28,24},{1,5},{5... | collective-permute-start | bytes 17301512 | tf_op jit(solution)/shard_map/ppermute | solution.py:17
  125.1 25.5 %collective-permute-start.20 = (bf16[256,2048]{1,0:T(8,128)(2,1)S(1)}, bf16[256,2048]{1,0:T(8,128)(2,1)S(1)}, u32[]{:S(2)}, u32[]{:S(2)}) collective-permute-start(bf16[256,2048]{1,0:T(8,128)(2,1)S(1)} %multiply_convert_fusion.refs_4_), channel_id=1, source_target_pairs={{0,8},{4,12},{8,0},{12,4},{16,24},{20,28},{24,16},{28,20},{1,9},{5... | collective-permute-start | bytes 3145736 | tf_op jit(solution)/shard_map/ppermute | solution.py:17
  126.6 25.3 %collective-permute-start.21 = (bf16[256,2048]{1,0:T(8,128)(2,1)S(1)}, bf16[256,2048]{1,0:T(8,128)(2,1)}, u32[]{:S(2)}, u32[]{:S(2)}) collective-permute-start(bf16[256,2048]{1,0:T(8,128)(2,1)S(1)} %multiply_convert_fusion.refs_4_), channel_id=1, source_target_pairs={{0,16},{4,20},{8,24},{12,28},{16,0},{20,4},{24,8},{28,12},{1,17},{... | collective-permute-start | bytes 3145736 | tf_op jit(solution)/shard_map/ppermute | solution.py:17
  128.1 150.0 %reduce-scatter.5.cloned.1.call-start = ((), (), s32[]{:S(2)}) async-start(), calls=%async_computation.6 | async-start | bytes 3604480 | tf_op jit(solution)/shard_map/reduce_scatter | solution.py:603
  152.0 30.5 %collective-permute-start.23 = (bf16[128,2048]{1,0:T(8,128)(2,1)S(1)}, bf16[128,2048]{1,0:T(8,128)(2,1)S(1)}, u32[]{:S(2)}, u32[]{:S(2)}) collective-permute-start(bf16[128,2048]{1,0:T(8,128)(2,1)S(1)} %slice.228), channel_id=1, source_target_pairs={{0,16},{4,20},{8,24},{12,28},{16,0},{20,4},{24,8},{28,12},{1,17},{... | collective-permute-start | bytes 1572872 | tf_op jit(solution)/shard_map/ppermute | solution.py:17
  154.6 27.9 %collective-permute-start.24 = (bf16[128,2048]{1,0:T(8,128)(2,1)S(1)}, bf16[128,2048]{1,0:T(8,128)(2,1)S(1)}, u32[]{:S(2)}, u32[]{:S(2)}) collective-permute-start(bf16[128,2048]{1,0:T(8,128)(2,1)S(1)} %slice.229), channel_id=1, source_target_pairs={{0,8},{4,12},{8,0},{12,4},{16,24},{20,28},{24,16},{28,20},{1,9},{5... | collective-permute-start | bytes 1572872 | tf_op jit(solution)/shard_map/ppermute | solution.py:17
  155.3 27.2 %collective-permute-start.25 = (bf16[128,2048]{1,0:T(8,128)(2,1)S(1)}, bf16[128,2048]{1,0:T(8,128)(2,1)S(1)}, u32[]{:S(2)}, u32[]{:S(2)}) collective-permute-start(bf16[128,2048]{1,0:T(8,128)(2,1)S(1)} %slice.230), channel_id=1, source_target_pairs={{0,16},{4,20},{8,24},{12,28},{16,0},{20,4},{24,8},{28,12},{1,17},{... | collective-permute-start | bytes 1572872 | tf_op jit(solution)/shard_map/ppermute | solution.py:17
  156.0 26.6 %collective-permute-start.26 = (bf16[128,2048]{1,0:T(8,128)(2,1)S(1)}, bf16[128,2048]{1,0:T(8,128)(2,1)S(1)}, u32[]{:S(2)}, u32[]{:S(2)}) collective-permute-start(bf16[128,2048]{1,0:T(8,128)(2,1)S(1)} %slice.231), channel_id=1, source_target_pairs={{0,8},{4,12},{8,0},{12,4},{16,24},{20,28},{24,16},{28,20},{1,9},{5... | collective-permute-start | bytes 1572872 | tf_op jit(solution)/shard_map/ppermute | solution.py:17
  189.2 17.3 %collective-permute-start.27 = (bf16[704,2048]{1,0:T(8,128)(2,1)}, bf16[704,2048]{1,0:T(8,128)(2,1)S(1)}, u32[]{:S(2)}, u32[]{:S(2)}) collective-permute-start(bf16[704,2048]{1,0:T(8,128)(2,1)} %all-gather.5.cloned.1.call-done), channel_id=1, source_target_pairs={{0,4},{4,0},{8,12},{12,8},{16,20},{20,16},{24,28},{28,24},{1,5},{5... | collective-permute-start | bytes 8650760 | tf_op jit(solution)/shard_map/ppermute | solution.py:17
  221.0 187.3 %reduce-scatter.7.cloned.1.call-start = ((), (), s32[]{:S(2)}) async-start(), calls=%async_computation.7 | async-start | bytes 7208960 | tf_op jit(solution)/shard_map/reduce_scatter | solution.py:617
  244.3 33.9 %collective-permute-start.32 = (bf16[128,2048]{1,0:T(8,128)(2,1)}, bf16[128,2048]{1,0:T(8,128)(2,1)}, u32[]{:S(2)}, u32[]{:S(2)}) collective-permute-start(bf16[128,2048]{1,0:T(8,128)(2,1)} %slice.288), channel_id=1, source_target_pairs={{0,16},{4,20},{8,24},{12,28},{16,0},{20,4},{24,8},{28,12},{1,17},{... | collective-permute-start | bytes 1572872 | tf_op jit(solution)/shard_map/ppermute | solution.py:17
  245.8 32.4 %collective-permute-start.31 = (bf16[128,2048]{1,0:T(8,128)(2,1)}, bf16[128,2048]{1,0:T(8,128)(2,1)}, u32[]{:S(2)}, u32[]{:S(2)}) collective-permute-start(bf16[128,2048]{1,0:T(8,128)(2,1)} %slice.287), channel_id=1, source_target_pairs={{0,8},{4,12},{8,0},{12,4},{16,24},{20,28},{24,16},{28,20},{1,9},{5... | collective-permute-start | bytes 1572872 | tf_op jit(solution)/shard_map/ppermute | solution.py:17
  247.4 30.7 %collective-permute-start.29 = (bf16[128,2048]{1,0:T(8,128)(2,1)}, bf16[128,2048]{1,0:T(8,128)(2,1)}, u32[]{:S(2)}, u32[]{:S(2)}) collective-permute-start(bf16[128,2048]{1,0:T(8,128)(2,1)} %get-tuple-element.301), channel_id=1, source_target_pairs={{0,8},{4,12},{8,0},{12,4},{16,24},{20,28},{24,16},{28,20},{1,9},{5... | collective-permute-start | bytes 1572872 | tf_op jit(solution)/shard_map/ppermute | solution.py:17
  248.8 29.3 %collective-permute-start.30 = (bf16[128,2048]{1,0:T(8,128)(2,1)}, bf16[128,2048]{1,0:T(8,128)(2,1)}, u32[]{:S(2)}, u32[]{:S(2)}) collective-permute-start(bf16[128,2048]{1,0:T(8,128)(2,1)} %get-tuple-element.300), channel_id=1, source_target_pairs={{0,16},{4,20},{8,24},{12,28},{16,0},{20,4},{24,8},{28,12},{1,17},{... | collective-permute-start | bytes 1572872 | tf_op jit(solution)/shard_map/ppermute | solution.py:17
  293.5 141.0 %reduce-scatter.9.cloned.1.call-start = ((), (), s32[]{:S(2)}) async-start(), calls=%async_computation.8 | async-start | bytes 1310720 | tf_op jit(solution)/shard_map/reduce_scatter | solution.py:650
  295.0 14.3 %collective-permute-start.34 = (bf16[128,2048]{1,0:T(8,128)(2,1)S(1)}, bf16[128,2048]{1,0:T(8,128)(2,1)S(1)}, u32[]{:S(2)}, u32[]{:S(2)}) collective-permute-start(bf16[128,2048]{1,0:T(8,128)(2,1)S(1)} %add_convert_fusion.4), channel_id=1, source_target_pairs={{0,16},{4,20},{8,24},{12,28},{16,0},{20,4},{24,8},{28,12},{1,17},{... | collective-permute-start | bytes 1572872 | tf_op jit(solution)/shard_map/ppermute | solution.py:17
  316.1 24.4 %collective-permute-start.35 = (bf16[256,2048]{1,0:T(8,128)(2,1)S(1)}, bf16[256,2048]{1,0:T(8,128)(2,1)S(1)}, u32[]{:S(2)}, u32[]{:S(2)}) collective-permute-start(bf16[256,2048]{1,0:T(8,128)(2,1)S(1)} %get-tuple-element.263.refs_1_), channel_id=1, source_target_pairs={{0,16},{4,20},{8,24},{12,28},{16,0},{20,4},{24,8},{28,12},{1,17},{... | collective-permute-start | bytes 3145736 | tf_op jit(solution)/shard_map/ppermute | solution.py:17
  316.7 24.6 %collective-permute-start.41 = (bf16[256,2048]{1,0:T(8,128)(2,1)S(1)}, bf16[256,2048]{1,0:T(8,128)(2,1)S(1)}, u32[]{:S(2)}, u32[]{:S(2)}) collective-permute-start(bf16[256,2048]{1,0:T(8,128)(2,1)S(1)} %get-tuple-element.263.refs_1_), channel_id=1, source_target_pairs={{0,8},{4,12},{8,0},{12,4},{16,24},{20,28},{24,16},{28,20},{1,9},{5... | collective-permute-start | bytes 3145736 | tf_op jit(solution)/shard_map/ppermute | solution.py:17
  356.0 25.3 %collective-permute-start.37 = (bf16[128,2048]{1,0:T(8,128)(2,1)S(1)}, bf16[128,2048]{1,0:T(8,128)(2,1)S(1)}, u32[]{:S(2)}, u32[]{:S(2)}) collective-permute-start(bf16[128,2048]{1,0:T(8,128)(2,1)S(1)} %get-tuple-element.297), channel_id=1, source_target_pairs={{0,8},{4,12},{8,0},{12,4},{16,24},{20,28},{24,16},{28,20},{1,9},{5... | collective-permute-start | bytes 1572872 | tf_op jit(solution)/shard_map/ppermute | solution.py:17
  357.5 23.9 %collective-permute-start.38 = (bf16[128,2048]{1,0:T(8,128)(2,1)S(1)}, bf16[128,2048]{1,0:T(8,128)(2,1)S(1)}, u32[]{:S(2)}, u32[]{:S(2)}) collective-permute-start(bf16[128,2048]{1,0:T(8,128)(2,1)S(1)} %get-tuple-element.296), channel_id=1, source_target_pairs={{0,16},{4,20},{8,24},{12,28},{16,0},{20,4},{24,8},{28,12},{1,17},{... | collective-permute-start | bytes 1572872 | tf_op jit(solution)/shard_map/ppermute | solution.py:17
  358.1 23.2 %collective-permute-start.39 = (bf16[128,2048]{1,0:T(8,128)(2,1)S(1)}, bf16[128,2048]{1,0:T(8,128)(2,1)S(1)}, u32[]{:S(2)}, u32[]{:S(2)}) collective-permute-start(bf16[128,2048]{1,0:T(8,128)(2,1)S(1)} %slice.244), channel_id=1, source_target_pairs={{0,8},{4,12},{8,0},{12,4},{16,24},{20,28},{24,16},{28,20},{1,9},{5... | collective-permute-start | bytes 1572872 | tf_op jit(solution)/shard_map/ppermute | solution.py:17
  359.3 22.1 %collective-permute-start.40 = (bf16[128,2048]{1,0:T(8,128)(2,1)S(1)}, bf16[128,2048]{1,0:T(8,128)(2,1)S(1)}, u32[]{:S(2)}, u32[]{:S(2)}) collective-permute-start(bf16[128,2048]{1,0:T(8,128)(2,1)S(1)} %slice.245), channel_id=1, source_target_pairs={{0,16},{4,20},{8,24},{12,28},{16,0},{20,4},{24,8},{28,12},{1,17},{... | collective-permute-start | bytes 1572872 | tf_op jit(solution)/shard_map/ppermute | solution.py:17
  394.7 26.4 %collective-permute-start.43 = (bf16[2048,1024]{1,0:T(8,128)(2,1)}, bf16[2048,1024]{1,0:T(8,128)(2,1)}, u32[]{:S(2)}, u32[]{:S(2)}) collective-permute-start(bf16[2048,1024]{1,0:T(8,128)(2,1)} %get-tuple-element.228), channel_id=1, source_target_pairs={{0,4},{4,0},{8,12},{12,8},{16,20},{20,16},{24,28},{28,24},{1,5},{5... | collective-permute-start | bytes 12582920 | tf_op jit(solution)/shard_map/ppermute | solution.py:17
  403.0 31.5 %collective-permute-start.58 = (f32[2,256]{1,0:T(2,128)S(1)}, f32[2,256]{1,0:T(2,128)S(1)}, u32[]{:S(2)}, u32[]{:S(2)}) collective-permute-start(f32[2,256]{1,0:T(2,128)S(1)} %fusion.33), channel_id=1, source_target_pairs={{0,1},{1,2},{2,3},{3,0},{4,5},{5,6},{6,7},{7,4},{8,9},{9,10},{10,1... | collective-permute-start | bytes 6152 | tf_op jit(solution)/shard_map/ppermute | solution.py:674
  403.0 33.0 %collective-permute-start.59 = (f32[2,256]{1,0:T(2,128)S(1)}, f32[2,256]{1,0:T(2,128)S(1)}, u32[]{:S(2)}, u32[]{:S(2)}) collective-permute-start(f32[2,256]{1,0:T(2,128)S(1)} %fusion.33), channel_id=1, source_target_pairs={{0,2},{1,3},{2,0},{3,1},{4,6},{5,7},{6,4},{7,5},{8,10},{9,11},{10,... | collective-permute-start | bytes 6152 | tf_op jit(solution)/shard_map/ppermute | solution.py:674
  405.7 33.0 %collective-permute-start.60 = (f32[2,256]{1,0:T(2,128)S(1)}, f32[2,256]{1,0:T(2,128)S(1)}, u32[]{:S(2)}, u32[]{:S(2)}) collective-permute-start(f32[2,256]{1,0:T(2,128)S(1)} %fusion.33), channel_id=1, source_target_pairs={{0,3},{1,0},{2,1},{3,2},{4,7},{5,4},{6,5},{7,6},{8,11},{9,8},{10,9... | collective-permute-start | bytes 6152 | tf_op jit(solution)/shard_map/ppermute | solution.py:674
  408.3 104.9 %reduce-scatter.11.cloned.1.call-start = ((), (), s32[]{:S(2)}) async-start(), calls=%async_computation.9 | async-start | bytes 5242880 | tf_op jit(solution)/shard_map/reduce_scatter | solution.py:652
  423.5 15.9 %collective-permute-start.44 = (bf16[128,2048]{1,0:T(8,128)(2,1)}, bf16[128,2048]{1,0:T(8,128)(2,1)S(1)}, u32[]{:S(2)}, u32[]{:S(2)}) collective-permute-start(bf16[128,2048]{1,0:T(8,128)(2,1)} %get-tuple-element.274), channel_id=1, source_target_pairs={{0,8},{4,12},{8,0},{12,4},{16,24},{20,28},{24,16},{28,20},{1,9},{5... | collective-permute-start | bytes 1572872 | tf_op jit(solution)/shard_map/ppermute | solution.py:17
  424.8 14.6 %collective-permute-start.45 = (bf16[128,2048]{1,0:T(8,128)(2,1)S(1)}, bf16[128,2048]{1,0:T(8,128)(2,1)S(1)}, u32[]{:S(2)}, u32[]{:S(2)}) collective-permute-start(bf16[128,2048]{1,0:T(8,128)(2,1)S(1)} %get-tuple-element.273), channel_id=1, source_target_pairs={{0,16},{4,20},{8,24},{12,28},{16,0},{20,4},{24,8},{28,12},{1,17},{... | collective-permute-start | bytes 1572872 | tf_op jit(solution)/shard_map/ppermute | solution.py:17
  466.5 21.0 %collective-permute-start.50 = (bf16[128,2048]{1,0:T(8,128)(2,1)S(1)}, bf16[128,2048]{1,0:T(8,128)(2,1)S(1)}, u32[]{:S(2)}, u32[]{:S(2)}) collective-permute-start(bf16[128,2048]{1,0:T(8,128)(2,1)S(1)} %get-tuple-element.238), channel_id=1, source_target_pairs={{0,8},{4,12},{8,0},{12,4},{16,24},{20,28},{24,16},{28,20},{1,9},{5... | collective-permute-start | bytes 1572872 | tf_op jit(solution)/shard_map/ppermute | solution.py:17
  467.6 22.8 %collective-permute-start.51 = (bf16[128,2048]{1,0:T(8,128)(2,1)S(1)}, bf16[128,2048]{1,0:T(8,128)(2,1)S(1)}, u32[]{:S(2)}, u32[]{:S(2)}) collective-permute-start(bf16[128,2048]{1,0:T(8,128)(2,1)S(1)} %get-tuple-element.239), channel_id=1, source_target_pairs={{0,16},{4,20},{8,24},{12,28},{16,0},{20,4},{24,8},{28,12},{1,17},{... | collective-permute-start | bytes 1572872 | tf_op jit(solution)/shard_map/ppermute | solution.py:17
  (168 other events, 1464.8 us)
Sparse Core Ops, SparseCore 0:
  19.0 106.0 all-gather.2
  128.2 57.4 all-gather.4
  221.1 55.3 reduce-scatter.4
  293.6 101.9 reduce-scatter.6
  408.4 26.0 reduce-scatter.8
  436.7 76.4 reduce-scatter.10
